TPU v7x, 32 devices: a whole 2x2x4 slice. The times are simulated.
32 devices in a mesh: groups: 2 (over x), cols: 16 (over z, y, core).
Axes of the slice: x: 2, y: 2, z: 4, core: 2. Of those that a mesh axis runs over, the one named last changes fastest.
Arguments:
- hidden: bfloat16 [512, 14848], P(('groups', 'cols')), parts along dimension 0, may hold values from -6 to 6
- down_weight: bfloat16 [14848, 4096], P('cols'), may hold values from -0.046875 to 0.046875
- delta_values: bfloat16 [64, 186, 128, 128], P('cols'), may hold values from -0.119628906 to 0.119628906
- block_ids: int32 [64, 186], P('cols'), may hold values from 0 to 3711, as said below
- variant_slot: int32 [64], replicated, may hold values from 0 to 63, each once
- row_variant: int32 [512, 1], P(('groups', 'cols')), parts along dimension 0, may hold values from 0 to 63; in each aligned block of 256 rows (0 to 255, 256 to 511, ...) at most 8 rows name the same one
Outputs:
- mixed_out: bfloat16 [512, 4096], P(('groups', 'cols')), parts along dimension 0
There are 2 independent parts, one for each index of `groups`. A program takes and returns all parts, laid end to end along the dimension named above; an argument that names none is the same for every part. Nothing has to cross between parts.
Inputs may be any that keep to these rules, and one draw needn't show every extreme that they name: `block_ids`: the 186 entries of one slot are distinct. `row_variant`: at most 8 rows name the same variant, every variant is named by some row, and in every draw some variant is named by exactly 8 rows. `variant_slot`: each slot holds exactly one variant.
All inputs are finite; a program needn't handle non-finite values.
Results may differ from a plain program's by a relative error of at most 0.0055.
Values may be sent and summed in bfloat16 or wider, within the bound.
No kernel may reach another device: no remote copies, remote signals or barrier semaphores. Data moves between devices by JAX's collectives and lax.ppermute only.
A program may use at most 128 MiB of HBM per device.

v0:
```python
import jax
import jax.numpy as jnp
from jax import lax
from jax.sharding import PartitionSpec as P


def slot_places(chosen, variant_slot, capacity):
    table = jnp.arange(variant_slot.shape[0], dtype=jnp.int32)
    onehot = (chosen[:, None] == table[None, :]).astype(jnp.int32)
    before = jnp.cumsum(onehot, axis=0) - onehot
    rank = jnp.sum(before * onehot, axis=1)
    slot_of = jnp.sum(onehot * variant_slot[None, :], axis=1)
    return slot_of * capacity + rank


def body(hidden, down_weight, delta_values, block_ids, variant_slot, row_variant):
    peers = lax.axis_size("cols")
    row_dev, width_f = hidden.shape
    width_d = down_weight.shape[1]
    local_var = delta_values.shape[0]
    block_size = delta_values.shape[2]
    variants = variant_slot.shape[0]
    all_rows = row_dev * peers
    capacity = 2 * all_rows // variants
    d_blocks = width_d // block_size
    f_blocks = width_f // block_size
    local_slots = local_var * capacity
    split_rows = lax.all_to_all(hidden, "cols", split_axis=1, concat_axis=0, tiled=True)
    every_route = lax.all_gather(row_variant, "cols", axis=0, tiled=True)
    places = slot_places(every_route[:, 0], variant_slot, capacity)
    row_of_slot = jnp.full((variants * capacity,), all_rows, jnp.int32)
    row_of_slot = row_of_slot.at[places].set(jnp.arange(all_rows, dtype=jnp.int32))
    outgoing = jnp.take(split_rows, row_of_slot, axis=0, mode="fill", fill_value=0)
    arrived = lax.all_to_all(outgoing, "cols", split_axis=0, concat_axis=1, tiled=True)
    grouped = arrived.reshape(local_var, capacity, f_blocks, block_size)

    def apply_delta(row_block, values, block_list):
        picked = jnp.take(row_block, block_list // d_blocks, axis=1)
        products = jnp.einsum("rnk,nkj->rnj", picked, values, preferred_element_type=jnp.float32)
        upper = products.astype(jnp.bfloat16)
        lower = (products - upper.astype(jnp.float32)).astype(jnp.bfloat16)
        onehot = ((block_list % d_blocks)[:, None] == jnp.arange(d_blocks)[None, :]).astype(
            jnp.bfloat16
        )
        placed = jnp.einsum("rnj,nc->rcj", upper, onehot, preferred_element_type=jnp.float32)
        placed = placed + jnp.einsum(
            "rnj,nc->rcj", lower, onehot, preferred_element_type=jnp.float32
        )
        return placed.reshape(row_block.shape[0], width_d).astype(jnp.bfloat16)

    deltas = jax.vmap(apply_delta)(grouped, delta_values, block_ids)
    owner_delta = deltas.reshape(local_slots, width_d)
    row_block = split_rows
    summed = lax.psum_scatter(
        jnp.dot(row_block, down_weight, preferred_element_type=jnp.float32),
        "cols",
        scatter_dimension=0,
        tiled=True,
    )
    column_part = lax.all_to_all(owner_delta, "cols", split_axis=1, concat_axis=0, tiled=True)
    by_row = jnp.take(column_part, places, axis=0)
    own_delta = lax.all_to_all(by_row, "cols", split_axis=0, concat_axis=1, tiled=True)
    return (summed + own_delta.astype(jnp.float32)).astype(jnp.bfloat16)


def solution(mesh):
    return jax.shard_map(
        body,
        mesh=mesh,
        in_specs=(
            P(("groups", "cols"), None),
            P("cols", None),
            P("cols", None, None, None),
            P("cols", None),
            P(),
            P(("groups", "cols"), None),
        ),
        out_specs=P(("groups", "cols"), None),
        check_vma=False,
    )
```

profile of v0, /device:TPU:0, one launch (start us, length us, event | category | flops | bytes accessed | tf_op | source)
XLA Modules:
  0.0 139.7 jit_solution(9016784918016889757)
XLA Ops:
  6.5 1.9 %all_to_all.44 = bf16[16,16,928]{2,1,0:T(8,128)(2,1)S(1)} reshape(bf16[16,14848]{1,0:T(8,128)(2,1)} %param.6) | data formatting | bytes 950272 | tf_op jit(solution)/shard_map/all_to_all | solution.py:28
  8.4 1.1 copy.31
  9.5 7.4 %all-to-all-start = ((bf16[16,16,928]{2,0,1:T(8,128)(2,1)}), bf16[16,16,928]{2,0,1:T(8,128)(2,1)S(1)}, u32[]{:S(2)}, u32[]{:S(2)}) async-start(bf16[16,16,928]{2,0,1:T(8,128)(2,1)} %copy.31), calls=%async_computation | async-start | bytes 1048576 | tf_op jit(solution)/shard_map/all_to_all | solution.py:28
  17.0 0.6 dynamic-slice
  18.2 0.1 bitcast_dynamic-update-slice_fusion
  18.3 14.3 %all-reduce = s32[256]{0:T(256)S(1)} all-reduce(s32[256]{0:T(256)S(1)} %bitcast_dynamic-update-slice_fusion), channel_id=1, replica_groups=mesh['groups'=2,'cols'=16] {'cols'}, use_global_device_ids=true, to_apply=%add | all-reduce | flops 256 | bytes 2048
  32.7 0.6 reduce-window.6
  33.3 0.2 slice_reduce_fusion
  33.5 0.1 select_reduce_fusion
  33.7 7.4 %fusion.32 = f32[256,4096]{1,0:T(8,128)} fusion(bf16[256,928]{1,0:T(8,128)(2,1)S(1)} %bitcast.67, bf16[928,4096]{1,0:T(8,128)(2,1)} %param.7), kind=kOutput, calls=%fused_computation.60 | convolution fusion | flops 1946157056 | bytes 12271616 | tf_op jit(solution)/shard_map/dot_general | solution.py:55
  41.1 1.4 scatter_custom_fusion
  42.6 0.1 broadcast_in_dim.47
  42.7 2.1 %gather_fusion = bf16[512,928]{1,0:T(8,128)(2,1)S(1)} fusion(bf16[256,928]{1,0:T(8,128)(2,1)S(1)} %bitcast.68, s32[1024]{0:T(1024)S(1)} %pad_clamp_fusion.1), kind=kCustom, calls=%fused_computation | custom fusion | bytes 1902592 | tf_op jit(solution)/shard_map/jit(_take)/gather | solution.py:33
  44.7 1.1 broadcast_select_fusion
  45.8 4.0 %all-to-all-start.1 = ((bf16[16,32,928]{2,1,0:T(8,128)(2,1)}), bf16[16,32,928]{2,1,0:T(8,128)(2,1)S(1)}, u32[]{:S(2)}, u32[]{:S(2)}) async-start(bf16[16,32,928]{2,1,0:T(8,128)(2,1)} %broadcast_select_fusion), calls=%async_computation.2 | async-start | bytes 2097152 | tf_op jit(solution)/shard_map/all_to_all | solution.py:34
  49.9 0.1 reshape.118
  50.0 22.6 %all-to-all-done.1 = bf16[16,32,928]{2,1,0:T(8,128)(2,1)S(1)} async-done(((bf16[16,32,928]{2,1,0:T(8,128)(2,1)}), bf16[16,32,928]{2,1,0:T(8,128)(2,1)S(1)}, u32[]{:S(2)}, u32[]{:S(2)}) %all-to-all-start.1) | async-done | bytes 950304 | tf_op jit(solution)/shard_map/all_to_all | solution.py:34
  72.6 0.6 copy.33
  73.2 1.8 %reshape.100 = bf16[4,8,116,128]{3,2,1,0:T(8,128)(2,1)S(1)} reshape(bf16[32,16,928]{2,1,0:T(8,128)(2,1)S(1)} %copy.33) | data formatting | bytes 1900544 | tf_op jit(solution)/shard_map/reshape | solution.py:35
  75.0 0.1 copy.34
  75.1 4.7 %gather_fusion.2 = bf16[744,8,128]{2,1,0:T(8,128)(2,1)S(1)} fusion(bf16[4,8,116,128]{3,1,2,0:T(8,128)(2,1)S(1)} %copy.34, s32[744]{0:T(1024)S(1)} %reshape.118), kind=kCustom, calls=%fused_computation.2 | custom fusion | bytes 3053376 | tf_op jit(solution)/shard_map/vmap(jit(_take))/gather | solution.py:38
  79.9 11.4 %fusion = (bf16[4,8,186,128]{3,1,2,0:T(8,128)(2,1)S(1)}, bf16[4,8,186,128]{3,1,2,0:T(8,128)(2,1)S(1)}) fusion(bf16[4,186,128,128]{3,2,1,0:T(8,128)(2,1)} %param.8, bf16[4,186,8,128]{3,2,1,0:T(8,128)(2,1)S(1)} %bitcast.70, pred[4,186]{1,0:T(4,128)(4,1)S(1)} %get-tuple-element.9), kind=kOutput, calls=%fused_computation.6 | convolution fusion | flops 198844416 | bytes 28951272 | tf_op jit(solution)/shard_map/vmap(rnk,nkj->rnj)/dot_general | solution.py:39
  91.3 0.4 fusion.1
  91.6 0.4 fusion.15
  92.0 0.1 convert_element_type.47
  92.1 0.8 copy.37
  92.8 15.0 %all-to-all-start.2 = ((bf16[32,16,256]{2,0,1:T(8,128)(2,1)}), bf16[32,16,256]{2,0,1:T(8,128)(2,1)S(1)}, u32[]{:S(2)}, u32[]{:S(2)}) async-start(bf16[32,16,256]{2,0,1:T(8,128)(2,1)} %copy.37), calls=%async_computation.3 | async-start | bytes 524288 | tf_op jit(solution)/shard_map/all_to_all | solution.py:60
  107.9 10.5 %all-to-all-done.2 = bf16[32,16,256]{2,0,1:T(8,128)(2,1)S(1)} async-done(((bf16[32,16,256]{2,0,1:T(8,128)(2,1)}), bf16[32,16,256]{2,0,1:T(8,128)(2,1)S(1)}, u32[]{:S(2)}, u32[]{:S(2)}) %all-to-all-start.2) | async-done | bytes 262176 | tf_op jit(solution)/shard_map/all_to_all | solution.py:60
  118.5 1.2 gather_fusion.1
  119.6 0.1 broadcast_select_fusion.1
  119.7 11.4 %all_to_all.58 = bf16[16,16,256]{2,1,0:T(8,128)(2,1)S(1)} all-to-all(bf16[16,16,256]{2,1,0:T(8,128)(2,1)S(1)} %broadcast_select_fusion.1), channel_id=1, replica_groups=mesh['groups'=2,'cols'=16] {'cols'}, dimensions={0} | all-to-all | bytes 262144 | tf_op jit(solution)/shard_map/all_to_all | solution.py:62
  131.2 1.6 %add_convert_fusion = bf16[16,4096]{1,0:T(8,128)(2,1)} fusion(f32[16,4096]{1,0:T(8,128)} %reduce-scatter.2.cloned.1.call-done, f32[16,4096]{1,0:T(8,128)S(1)} %bitcast.73), kind=kLoop, calls=%fused_computation.21 | loop fusion | flops 131072 | bytes 655360 | tf_op jit(solution)/shard_map/convert_element_type | solution.py:63
  (30 shorter events, 0.3 us)
Async XLA Ops:
  6.5 10.4 %copy-start.3 = (u32[32]{0:T(128)S(1)}, u32[32]{0:T(128)}, u32[]{:S(2)}) copy-start(u32[32]{0:T(128)} %constant.102) | copy-start | bytes 388
  6.5 11.7 %copy-start.2 = (s32[16,1]{0,1:T(1,128)S(1)}, s32[16,1]{0,1:T(1,128)}, u32[]{:S(2)}) copy-start(s32[16,1]{0,1:T(1,128)} %param.11) | copy-start | bytes 196
  6.5 27.0 %copy-start.1 = (s32[64]{0:T(128)S(1)}, s32[64]{0:T(128)}, u32[]{:S(2)}) copy-start(s32[64]{0:T(128)} %param.10) | copy-start | bytes 772
  9.5 24.1 %all-to-all-start = ((bf16[16,16,928]{2,0,1:T(8,128)(2,1)}), bf16[16,16,928]{2,0,1:T(8,128)(2,1)S(1)}, u32[]{:S(2)}, u32[]{:S(2)}) async-start(bf16[16,16,928]{2,0,1:T(8,128)(2,1)} %copy.31), calls=%async_computation | async-start | bytes 1048576 | tf_op jit(solution)/shard_map/all_to_all | solution.py:28
  16.9 114.3 %reduce-scatter.2.cloned.1.call-start = ((), (), s32[]{:S(2)}) async-start(), calls=%async_computation.5 | async-start | bytes 4456448 | tf_op jit(solution)/shard_map/reduce_scatter | solution.py:54
  45.8 4.0 %copy-start = (s32[4,186]{1,0:T(4,128)S(1)}, s32[4,186]{1,0:T(4,128)}, u32[]{:S(2)}) copy-start(s32[4,186]{1,0:T(4,128)} %param.9) | copy-start | bytes 8932
  45.8 26.8 %all-to-all-start.1 = ((bf16[16,32,928]{2,1,0:T(8,128)(2,1)}), bf16[16,32,928]{2,1,0:T(8,128)(2,1)S(1)}, u32[]{:S(2)}, u32[]{:S(2)}) async-start(bf16[16,32,928]{2,1,0:T(8,128)(2,1)} %broadcast_select_fusion), calls=%async_computation.2 | async-start | bytes 2097152 | tf_op jit(solution)/shard_map/all_to_all | solution.py:34
  92.8 25.6 %all-to-all-start.2 = ((bf16[32,16,256]{2,0,1:T(8,128)(2,1)}), bf16[32,16,256]{2,0,1:T(8,128)(2,1)S(1)}, u32[]{:S(2)}, u32[]{:S(2)}) async-start(bf16[32,16,256]{2,0,1:T(8,128)(2,1)} %copy.37), calls=%async_computation.3 | async-start | bytes 524288 | tf_op jit(solution)/shard_map/all_to_all | solution.py:60
Sparse Core Ops, SparseCore 0:
  41.2 74.6 reduce-scatter.1
where the time goes:
time: 140 us
  waiting for transfers between devices  33.2 us (24%)
  starting transfers between devices  26.4 us (19%)
  blocking collectives  25.7 us (18%)
  matrix products  19.5 us (14%)
  local copies, waits for them, and re-layouts  16.8 us (12%)
  between operations  14.3 us (10%)
  other arithmetic  3.72 us (3%)
    all_to_all x1, waiting for transfers between devices, body(): lax.all_to_all(outgoing, 'cols', split_axis=0, concat_axis=1, tiled=True)  22.6 us
    all_to_all x1, starting transfers between devices, body(): lax.all_to_all(owner_delta, 'cols', split_axis=1, concat_axis=0, tiled=True)  15 us
    unnamed x1, blocking collectives  14.3 us
    dot_general x1, matrix products, apply_delta(): jnp.einsum('rnk,nkj->rnj', picked, values, preferred_element_type=jnp.flo...  11.4 us
    all_to_all x1, blocking collectives, body(): lax.all_to_all(by_row, 'cols', split_axis=0, concat_axis=1, tiled=True)  11.4 us
    all_to_all x1, waiting for transfers between devices, body(): lax.all_to_all(owner_delta, 'cols', split_axis=1, concat_axis=0, tiled=True)  10.5 us
    dot_general x1, matrix products, body(): jnp.dot(row_block, down_weight, preferred_element_type=jnp.float32)  7.42 us
    all_to_all x1, starting transfers between devices, body(): lax.all_to_all(hidden, 'cols', split_axis=1, concat_axis=0, tiled=True)  7.39 us
  transfers between devices with their start and end apart: 4, of which 2 were waited for; matrix products, arithmetic and copies ran while one was open for 20% of the time, Pallas kernels for 0%

commit v1 on v0

v1 whole, which is shorter than its diff:
```python
import functools

import jax
import jax.numpy as jnp
from jax import lax
from jax.experimental import pallas as pl
from jax.experimental.pallas import tpu as pltpu
from jax.sharding import PartitionSpec as P

LANES = 128
BF16 = jnp.bfloat16
F32 = jnp.float32


def windows(width_f, peers):
    share = width_f // peers
    most = max((s * share) % LANES for s in range(peers))
    window = -(-(share + most) // LANES) * LANES
    if window == share:
        window += LANES
    last = (width_f - window) // LANES
    starts = [min(s * share // LANES, last) for s in range(peers)]
    return share, window, last, starts


def params(**kw):
    return pltpu.CompilerParams(vmem_limit_bytes=48 * 1024 * 1024, **kw)


def lane_iota(rows, lanes):
    return lax.broadcasted_iota(jnp.int32, (rows, lanes), 1)


def split_kernel(plan, h_ref, id_ref, o_ref):
    share, window, _, starts = plan
    rows = h_ref.shape[0]
    lane = lane_iota(rows, window)
    ids = id_ref[...].astype(F32)
    for s, b in enumerate(starts):
        shift = s * share - b * LANES
        piece = h_ref[:, b * LANES : b * LANES + window].astype(F32)
        keep = (lane >= shift) & (lane < shift + share)
        spare = (shift + share) % window
        piece = jnp.where(keep, piece, jnp.where(lane == spare, ids, 0.0))
        o_ref[s] = piece.astype(BF16)


def own_shift(plan):
    share, _, last, _ = plan
    start = lax.axis_index("cols") * share
    return start - jnp.minimum(start // LANES, last) * LANES


def route_kernel(plan, capacity, shift_ref, x_ref, slot_ref, o_ref, place_ref):
    share, window, _, _ = plan
    peers, row_dev, _ = x_ref.shape
    rows = peers * row_dev
    variants = slot_ref.shape[1]
    slots = variants * capacity
    shift = shift_ref[0]
    x = x_ref[...].reshape(rows, window).astype(F32)
    lane = lane_iota(rows, window)
    spare = lax.rem(shift + share, window)
    ids = jnp.sum(jnp.where(lane == spare, x, 0.0), axis=1, keepdims=True)
    data = jnp.where((lane >= shift) & (lane < shift + share), x, 0.0).astype(BF16)
    onehot = ids.astype(jnp.int32) == lane_iota(rows, variants)
    onehot_f = jnp.where(onehot, 1.0, 0.0)
    row_i = lax.broadcasted_iota(jnp.int32, (rows, rows), 0)
    row_j = lane_iota(rows, rows)
    earlier = jnp.where(row_j < row_i, 1.0, 0.0).astype(BF16)
    before = jnp.dot(earlier, onehot_f.astype(BF16), preferred_element_type=F32)
    rank = jnp.sum(before * onehot_f, axis=1, keepdims=True)
    slot_of = jnp.sum(onehot_f * slot_ref[...].astype(F32), axis=1, keepdims=True)
    place = slot_of * capacity + rank
    place_ref[...] = place.astype(jnp.int32)
    across = jnp.sum(jnp.where(row_i == row_j, place, 0.0), axis=0, keepdims=True)
    pick = across.astype(jnp.int32) == lax.broadcasted_iota(jnp.int32, (slots, rows), 0)
    pick = jnp.where(pick, 1.0, 0.0).astype(BF16)
    filled = jnp.dot(pick, data, preferred_element_type=F32).astype(BF16)
    o_ref[...] = filled.reshape(o_ref.shape)


def base_kernel(plan, scal_ref, x_ref, w_ref, keep_ref, send_ref, mine_ref):
    share, window, _, _ = plan
    peers, row_dev, _ = x_ref.shape
    half = peers // 2 * row_dev

    @pl.when(pl.program_id(0) == 0)
    def _():
        bit = scal_ref[1]
        for side in (0, 1):
            which = bit if side == 0 else 1 - bit
            for q in range(peers // 2):
                piece = x_ref[2 * q + which].astype(F32)
                piece = pltpu.roll(piece, window - scal_ref[0], 1)
                mine_ref[side, q * row_dev : (q + 1) * row_dev] = piece[:, :share].astype(BF16)

    w = w_ref[...]
    keep = jnp.dot(mine_ref[0], w, preferred_element_type=F32)
    keep_ref[...] = keep.reshape(keep_ref.shape)
    send = jnp.dot(mine_ref[1], w, preferred_element_type=F32)
    send_ref[...] = send.astype(BF16).reshape(send_ref.shape)


def delta_kernel(plan, d_blocks, ids_ref, x_ref, v_ref, o_ref, rows_ref, acc_ref):
    _, window, _, starts = plan
    local_var, f_blocks, capacity, _ = rows_ref.shape
    group = v_ref.shape[1]
    var, step = pl.program_id(0), pl.program_id(1)

    @pl.when((var == 0) & (step == 0))
    def _():
        acc_ref[...] = jnp.zeros_like(acc_ref)
        done = set()
        for s, b in enumerate(starts):
            for k in range(window // LANES):
                tile = x_ref[s, :, k * LANES : (k + 1) * LANES].astype(F32)
                for v in range(local_var):
                    part = tile[v * capacity : (v + 1) * capacity]
                    if b + k in done:
                        part = part + rows_ref[v, b + k]
                    rows_ref[v, b + k] = part
                done.add(b + k)

    places, products = [], []
    for n in range(group):
        block = ids_ref[var, step * group + n]
        lhs = rows_ref[var, lax.div(block, d_blocks)].astype(BF16)
        products.append(jnp.dot(lhs, v_ref[0, n], preferred_element_type=F32))
        places.append(lax.rem(block, d_blocks))
    for j, product in zip(places, products):
        acc_ref[var, j] += product

    @pl.when((var == pl.num_programs(0) - 1) & (step == pl.num_programs(1) - 1))
    def _():
        for j in range(d_blocks):
            whole = jnp.concatenate([acc_ref[v, j] for v in range(local_var)], axis=0)
            if len(o_ref.shape) == 3:
                per = o_ref.shape[2] // LANES
                k = j % per
                o_ref[j // per, :, k * LANES : (k + 1) * LANES] = whole.astype(BF16)
            else:
                o_ref[:, j * LANES : (j + 1) * LANES] = whole.astype(BF16)


def pick_kernel(place_ref, c_ref, o_ref):
    peers, per_owner, cols = c_ref.shape
    slots = peers * per_owner
    rows = place_ref.shape[0]
    pick = place_ref[...] == lane_iota(rows, slots)
    pick = jnp.where(pick, 1.0, 0.0).astype(BF16)
    found = jnp.dot(pick, c_ref[...].reshape(slots, cols), preferred_element_type=F32)
    o_ref[...] = found.astype(BF16).reshape(o_ref.shape)


def split_factor(count, most):
    return max(g for g in range(1, most + 1) if count % g == 0)


def body(hidden, down_weight, delta_values, block_ids, variant_slot, row_variant):
    peers = lax.axis_size("cols")
    me = lax.axis_index("cols")
    row_dev, width_f = hidden.shape
    width_d = down_weight.shape[1]
    local_var, count, block_size, _ = delta_values.shape
    variants = variant_slot.shape[0]
    all_rows = row_dev * peers
    capacity = 2 * all_rows // variants
    d_blocks = width_d // block_size
    f_blocks = width_f // block_size
    local_slots = local_var * capacity
    plan = windows(width_f, peers)
    share, window, _, _ = plan
    half = peers // 2
    slice_d = width_d // peers

    scal = jnp.stack([own_shift(plan), me % 2]).astype(jnp.int32)
    smem = pl.BlockSpec(memory_space=pltpu.SMEM)

    outgoing = pl.pallas_call(
        functools.partial(split_kernel, plan),
        out_shape=jax.ShapeDtypeStruct((peers, row_dev, window), BF16),
        compiler_params=params(),
        name="split_rows",
    )(hidden, row_variant)
    x = lax.all_to_all(outgoing, "cols", 0, 0)

    slots, place = pl.pallas_call(
        functools.partial(route_kernel, plan, capacity),
        out_shape=(
            jax.ShapeDtypeStruct((peers, local_slots, window), BF16),
            jax.ShapeDtypeStruct((all_rows, 1), jnp.int32),
        ),
        in_specs=[smem, pl.BlockSpec(memory_space=pltpu.VMEM), pl.BlockSpec(memory_space=pltpu.VMEM)],
        compiler_params=params(),
        name="route",
    )(scal, x, variant_slot.reshape(1, variants))
    arrived = lax.all_to_all(slots, "cols", 0, 0)

    tile = min(512, width_d)
    keep, send = pl.pallas_call(
        functools.partial(base_kernel, plan),
        grid=(width_d // tile,),
        out_shape=(
            jax.ShapeDtypeStruct((half, row_dev, width_d), F32),
            jax.ShapeDtypeStruct((half, row_dev, width_d), BF16),
        ),
        in_specs=[
            smem,
            pl.BlockSpec((peers, row_dev, window), lambda t: (0, 0, 0)),
            pl.BlockSpec((share, tile), lambda t: (0, t)),
        ],
        out_specs=(
            pl.BlockSpec((half, row_dev, tile), lambda t: (0, 0, t)),
            pl.BlockSpec((half, row_dev, tile), lambda t: (0, 0, t)),
        ),
        scratch_shapes=[pltpu.VMEM((2, all_rows // 2, share), BF16)],
        compiler_params=params(),
        cost_estimate=pl.CostEstimate(
            flops=2 * all_rows * share * width_d,
            bytes_accessed=2 * share * width_d + 6 * all_rows // 2 * width_d,
            transcendentals=0,
        ),
        name="base",
    )(scal, x, down_weight)
    step = 1
    while True:
        got = lax.ppermute(send, "cols", [(i, i ^ step) for i in range(peers)])
        total = keep + got.astype(F32)
        step *= 2
        if step == peers:
            break
        bit = (me // step) % 2
        total = total.reshape(total.shape[0] // 2, 2, row_dev, width_d)
        keep = lax.dynamic_index_in_dim(total, bit, 1, keepdims=False)
        send = lax.dynamic_index_in_dim(total, 1 - bit, 1, keepdims=False).astype(BF16)
    summed = total.reshape(row_dev, width_d)

    group = split_factor(count, 64)
    aligned = slice_d % LANES == 0
    shape = (peers, local_slots, slice_d) if aligned else (local_slots, width_d)
    deltas = pl.pallas_call(
        functools.partial(delta_kernel, plan, d_blocks),
        grid_spec=pltpu.PrefetchScalarGridSpec(
            num_scalar_prefetch=1,
            grid=(local_var, count // group),
            in_specs=[
                pl.BlockSpec((peers, local_slots, window), lambda v, s, ids: (0, 0, 0)),
                pl.BlockSpec((1, group, block_size, block_size), lambda v, s, ids: (v, s, 0, 0)),
            ],
            out_specs=pl.BlockSpec(shape, lambda v, s, ids: (0,) * len(shape)),
            scratch_shapes=[
                pltpu.VMEM((local_var, f_blocks, capacity, block_size), F32),
                pltpu.VMEM((local_var, d_blocks, capacity, block_size), F32),
            ],
        ),
        out_shape=jax.ShapeDtypeStruct(shape, BF16),
        compiler_params=params(),
        cost_estimate=pl.CostEstimate(
            flops=2 * local_slots * count * block_size * block_size,
            bytes_accessed=2 * local_var * count * block_size * block_size,
            transcendentals=0,
        ),
        name="delta",
    )(block_ids, arrived, delta_values)
    if not aligned:
        deltas = deltas.reshape(local_slots, peers, slice_d).transpose(1, 0, 2)
    columns = lax.all_to_all(deltas, "cols", 0, 0)
    by_row = pl.pallas_call(
        pick_kernel,
        out_shape=jax.ShapeDtypeStruct((peers, row_dev, slice_d), BF16),
        compiler_params=params(),
        name="pick",
    )(place, columns)
    own = lax.all_to_all(by_row, "cols", 0, 0)
    own = own.transpose(1, 0, 2).reshape(row_dev, width_d)
    return (summed + own.astype(F32)).astype(BF16)


def solution(mesh):
    return jax.shard_map(
        body,
        mesh=mesh,
        in_specs=(
            P(("groups", "cols"), None),
            P("cols", None),
            P("cols", None, None, None),
            P("cols", None),
            P(),
            P(("groups", "cols"), None),
        ),
        out_specs=P(("groups", "cols"), None),
        check_vma=False,
    )
```

time: 140 us -> 121 us (0.86)
  Pallas kernels: 0 us -> 29.1 us
  blocking collectives: 25.7 us -> 0 us
  waiting for transfers between devices: 33.2 us -> 57.8 us
  matrix products: 19.5 us -> 0 us
  between operations: 14.3 us -> 0.26 us
  local copies, waits for them, and re-layouts: 16.8 us -> 3.75 us
    pallas_call x0 -> x5, Pallas kernels: none -> 29.1 us  [the longest x1 16.3 us: body(): pl.pallas_call(functools.partial(delta_kernel, plan, d_blocks), grid_spec...]
    dot_general x4 -> x0, matrix products: 19.5 us -> none  [the longest x1 11.4 us: apply_delta(): jnp.einsum('rnk,nkj->rnj', picked, values, preferred_element_type=jnp.flo...]
    ppermute x0 -> x4, waiting for transfers between devices: none -> 18.1 us  [body(): got = lax.ppermute(send, 'cols', [(i, i ^ step) for i in range(peers)])]
    unnamed x1 -> x0, blocking collectives: 14.3 us -> none
    all_to_all x1 -> x0, blocking collectives: 11.4 us -> none  [body(): lax.all_to_all(by_row, 'cols', split_axis=0, concat_axis=1, tiled=True)]
    gather x4 -> x0, local copies, waits for them, and re-layouts: 8.03 us -> none  [the longest x2 4.82 us: apply_delta(): picked = jnp.take(row_block, block_list // d_blocks, axis=1)]
    all_to_all x3 -> x4, waiting for transfers between devices: 33.2 us -> 39.7 us  [the longest x1 14.4 us: body(): x = lax.all_to_all(outgoing, 'cols', 0, 0)]
    all_to_all x3 -> x4, starting transfers between devices: 26.3 us -> 21.8 us  [the longest x1 7.39 us: body(): x = lax.all_to_all(outgoing, 'cols', 0, 0)]
  transfers between devices with their start and end apart: 4 -> 8, of which waited for: 2 -> 7; matrix products, arithmetic and copies ran while one was open for 20% -> 1% of each run, Pallas kernels for 0% -> 16%
where the time goes in v1:
time: 121 us; the launch traced here: 120 us
  waiting for transfers between devices  57.8 us (48%)
  Pallas kernels  29.1 us (24%)
  starting transfers between devices  25.5 us (21%)
  local copies, waits for them, and re-layouts  3.75 us (3%)
  other arithmetic  3.44 us (3%)
    ppermute x4, waiting for transfers between devices, body(): got = lax.ppermute(send, 'cols', [(i, i ^ step) for i in range(peers)])  18.1 us
    pallas_call x1, Pallas kernels, body(): pl.pallas_call(functools.partial(delta_kernel, plan, d_blocks), grid_spec...  16.3 us
    all_to_all x1, waiting for transfers between devices, body(): x = lax.all_to_all(outgoing, 'cols', 0, 0)  14.4 us
    all_to_all x1, waiting for transfers between devices, body(): columns = lax.all_to_all(deltas, 'cols', 0, 0)  9.97 us
    all_to_all x1, waiting for transfers between devices, body(): arrived = lax.all_to_all(slots, 'cols', 0, 0)  9.84 us
    pallas_call x1, Pallas kernels, body(): pl.pallas_call(functools.partial(base_kernel, plan), grid=(width_d // til...  8.58 us
    all_to_all x1, starting transfers between devices, body(): x = lax.all_to_all(outgoing, 'cols', 0, 0)  7.39 us
    all_to_all x1, starting transfers between devices, body(): columns = lax.all_to_all(deltas, 'cols', 0, 0)  6.5 us
  transfers between devices with their start and end apart: 8, of which 7 were waited for; matrix products, arithmetic and copies ran while one was open for 1% of the time, Pallas kernels for 16%

profile of v1, /device:TPU:0, one launch (start us, length us, event | category | flops | bytes accessed | tf_op | source)
XLA Modules:
  0.0 119.9 jit_solution(9949338400048215606)
XLA Ops:
  0.0 0.7 copy.8.id_ref
  0.7 1.0 copy-done
  1.8 0.9 split_rows.1
  2.6 7.4 %all-to-all-start = ((bf16[16,16,1024]{2,1,0:T(8,128)(2,1)}), bf16[16,16,1024]{2,1,0:T(8,128)(2,1)S(1)}, u32[]{:S(2)}, u32[]{:S(2)}) async-start(bf16[16,16,1024]{2,1,0:T(8,128)(2,1)} %split_rows.1), calls=%async_computation | async-start | bytes 1048576 | tf_op jit(solution)/shard_map/all_to_all | solution.py:186
  10.1 0.1 pad_add_fusion.scal_ref.shift_ref
  10.1 14.4 %all-to-all-done.x_ref = bf16[16,16,1024]{2,1,0:T(8,128)(2,1)S(1)} async-done(((bf16[16,16,1024]{2,1,0:T(8,128)(2,1)}), bf16[16,16,1024]{2,1,0:T(8,128)(2,1)S(1)}, u32[]{:S(2)}, u32[]{:S(2)}) %all-to-all-start) | async-done | bytes 524320 | tf_op jit(solution)/shard_map/all_to_all | solution.py:186
  24.5 8.6 %base.1 = (f32[8,16,4096]{2,1,0:T(8,128)S(1)}, bf16[8,16,4096]{2,1,0:T(8,128)(2,1)}) custom-call(s32[2]{0:T(128)S(1)} %pad_add_fusion.scal_ref.shift_ref, bf16[16,16,1024]{2,1,0:T(8,128)(2,1)S(1)} %all-to-all-done.x_ref, bf16[928,4096]{1,0:T(8,128)(2,1)} %w_ref.1), custom_call_target="tpu_custom_call" | custom-call | flops 1946157056 | bytes 10747904 | tf_op jit(solution)/shard_map/base/pallas_call | solution.py:201
  33.1 0.0 collective-permute-start
  33.1 3.0 %collective-permute-done = bf16[8,16,4096]{2,1,0:T(8,128)(2,1)} collective-permute-done((bf16[8,16,4096]{2,1,0:T(8,128)(2,1)}, bf16[8,16,4096]{2,1,0:T(8,128)(2,1)}, u32[]{:S(2)}, u32[]{:S(2)}) %collective-permute-start) | collective-permute-done | bytes 1048608 | tf_op jit(solution)/shard_map/ppermute | solution.py:228
  36.1 1.4 %convert_add_fusion = f32[8,16,4096]{2,1,0:T(8,128)S(1)} fusion(f32[8,16,4096]{2,1,0:T(8,128)S(1)} %get-tuple-element.9, bf16[8,16,4096]{2,1,0:T(8,128)(2,1)} %collective-permute-done), kind=kLoop, calls=%fused_computation | loop fusion | flops 1048576 | bytes 5242880 | tf_op jit(solution)/shard_map/add | solution.py:229
  37.5 0.9 fusion
  38.5 0.8 collective-permute-start.1
  39.3 0.0 copy-done.2
  39.3 2.4 %route.1 = (bf16[16,32,1024]{2,1,0:T(8,128)(2,1)}, s32[256,1]{1,0:T(8,128)S(1)}) custom-call(s32[2]{0:T(128)S(1)} %pad_add_fusion.scal_ref.shift_ref, bf16[16,16,1024]{2,1,0:T(8,128)(2,1)S(1)} %all-to-all-done.x_ref, s32[1,64]{1,0:T(1,128)S(1)} %bitcast.25), custom_call_target="tpu_custom_call" | custom-call | tf_op jit(solution)/shard_map/route/pallas_call | solution.py:188
  41.6 4.4 %all-to-all-start.1 = ((bf16[16,32,1024]{2,1,0:T(8,128)(2,1)}), bf16[16,32,1024]{2,1,0:T(8,128)(2,1)S(1)}, u32[]{:S(2)}, u32[]{:S(2)}) async-start(bf16[16,32,1024]{2,1,0:T(8,128)(2,1)} %get-tuple-element.12), calls=%async_computation.1 | async-start | bytes 2097152 | tf_op jit(solution)/shard_map/all_to_all | solution.py:198
  46.1 0.0 copy-start.1
  46.1 11.2 %collective-permute-done.1 = bf16[4,16,4096]{2,1,0:T(8,128)(2,1)} collective-permute-done((bf16[4,16,4096]{2,1,0:T(8,128)(2,1)}, bf16[4,16,4096]{2,1,0:T(8,128)(2,1)}, u32[]{:S(2)}, u32[]{:S(2)}) %collective-permute-start.1) | collective-permute-done | bytes 524320 | tf_op jit(solution)/shard_map/ppermute | solution.py:228
  57.3 1.2 bitcast_add_fusion
  58.5 1.0 copy-done.5
  59.5 0.1 collective-permute-start.2
  59.6 9.8 %all-to-all-done.1.x_ref = bf16[16,32,1024]{2,1,0:T(8,128)(2,1)S(1)} async-done(((bf16[16,32,1024]{2,1,0:T(8,128)(2,1)}), bf16[16,32,1024]{2,1,0:T(8,128)(2,1)S(1)}, u32[]{:S(2)}, u32[]{:S(2)}) %all-to-all-start.1) | async-done | bytes 1048608 | tf_op jit(solution)/shard_map/all_to_all | solution.py:198
  69.5 16.3 %delta.1 = bf16[16,32,256]{2,1,0:T(8,128)(2,1)} custom-call(s32[4,186]{1,0:T(4,128)S(1)} %copy-done.1, bf16[16,32,1024]{2,1,0:T(8,128)(2,1)S(1)} %all-to-all-done.1.x_ref, bf16[4,186,128,128]{3,2,1,0:T(8,128)(2,1)} %v_ref.1), custom_call_target="tpu_custom_call" | custom-call | flops 195035136 | bytes 24379392 | tf_op jit(solution)/shard_map/delta/pallas_call | solution.py:242
  85.8 6.5 %all-to-all-start.2 = ((bf16[16,32,256]{2,1,0:T(8,128)(2,1)}), bf16[16,32,256]{2,1,0:T(8,128)(2,1)S(1)}, u32[]{:S(2)}, u32[]{:S(2)}) async-start(bf16[16,32,256]{2,1,0:T(8,128)(2,1)} %delta.1), calls=%async_computation.2 | async-start | bytes 524288 | tf_op jit(solution)/shard_map/all_to_all | solution.py:268
  92.3 0.0 collective-permute-done.2
  92.3 0.1 bitcast_add_fusion.1
  92.3 10.0 %all-to-all-done.2.c_ref = bf16[16,32,256]{2,1,0:T(8,128)(2,1)S(1)} async-done(((bf16[16,32,256]{2,1,0:T(8,128)(2,1)}), bf16[16,32,256]{2,1,0:T(8,128)(2,1)S(1)}, u32[]{:S(2)}, u32[]{:S(2)}) %all-to-all-start.2) | async-done | bytes 262176 | tf_op jit(solution)/shard_map/all_to_all | solution.py:268
  102.3 0.9 pick.1
  103.2 3.5 %all-to-all-start.3 = ((bf16[16,16,256]{2,1,0:T(8,128)(2,1)}), bf16[16,16,256]{2,1,0:T(8,128)(2,1)S(1)}, u32[]{:S(2)}, u32[]{:S(2)}) async-start(bf16[16,16,256]{2,1,0:T(8,128)(2,1)} %pick.1), calls=%async_computation.3 | async-start | bytes 262144 | tf_op jit(solution)/shard_map/all_to_all | solution.py:275
  106.8 2.8 %collective-permute-start.3 = (bf16[1,16,4096]{2,1,0:T(8,128)(2,1)S(1)}, bf16[1,16,4096]{2,1,0:T(8,128)(2,1)S(1)}, u32[]{:S(2)}, u32[]{:S(2)}) collective-permute-start(bf16[1,16,4096]{2,1,0:T(8,128)(2,1)S(1)} %dynamic-slice_convert_fusion.1), channel_id=1, source_target_pairs={{0,8},{1,9},{2,10},{3,11},{4,12},{5,13},{6,14},{7,15},{8,0},{9,1},... | collective-permute-start | bytes 393224 | tf_op jit(solution)/shard_map/ppermute | solution.py:228
  109.6 5.5 %all-to-all-done.3 = bf16[16,16,256]{2,1,0:T(8,128)(2,1)S(1)} async-done(((bf16[16,16,256]{2,1,0:T(8,128)(2,1)}), bf16[16,16,256]{2,1,0:T(8,128)(2,1)S(1)}, u32[]{:S(2)}, u32[]{:S(2)}) %all-to-all-start.3) | async-done | bytes 131104 | tf_op jit(solution)/shard_map/all_to_all | solution.py:275
  115.2 4.0 %collective-permute-done.3 = bf16[1,16,4096]{2,1,0:T(8,128)(2,1)S(1)} collective-permute-done((bf16[1,16,4096]{2,1,0:T(8,128)(2,1)S(1)}, bf16[1,16,4096]{2,1,0:T(8,128)(2,1)S(1)}, u32[]{:S(2)}, u32[]{:S(2)}) %collective-permute-start.3) | collective-permute-done | bytes 131104 | tf_op jit(solution)/shard_map/ppermute | solution.py:228
  119.1 0.7 fusion.2
  (14 shorter events, 0.1 us)
Async XLA Ops:
  0.7 1.0 copy-start
  2.6 21.9 %all-to-all-start = ((bf16[16,16,1024]{2,1,0:T(8,128)(2,1)}), bf16[16,16,1024]{2,1,0:T(8,128)(2,1)S(1)}, u32[]{:S(2)}, u32[]{:S(2)}) async-start(bf16[16,16,1024]{2,1,0:T(8,128)(2,1)} %split_rows.1), calls=%async_computation | async-start | bytes 1048576 | tf_op jit(solution)/shard_map/all_to_all | solution.py:186
  33.1 3.0 %collective-permute-start = (bf16[8,16,4096]{2,1,0:T(8,128)(2,1)}, bf16[8,16,4096]{2,1,0:T(8,128)(2,1)}, u32[]{:S(2)}, u32[]{:S(2)}) collective-permute-start(bf16[8,16,4096]{2,1,0:T(8,128)(2,1)} %get-tuple-element.10), channel_id=1, source_target_pairs={{0,1},{1,0},{2,3},{3,2},{4,5},{5,4},{6,7},{7,6},{8,9},{9,8},{10,11... | collective-permute-start | bytes 3145736 | tf_op jit(solution)/shard_map/ppermute | solution.py:228
  36.1 3.2 %copy-start.2 = (s32[64]{0:T(128)S(1)}, s32[64]{0:T(128)}, u32[]{:S(2)}) copy-start(s32[64]{0:T(128)} %param.10) | copy-start | bytes 772
  37.5 1.7 %copy-start.3 = (f32[8,16,4096]{2,1,0:T(8,128)}, f32[8,16,4096]{2,1,0:T(8,128)S(1)}, u32[]{:S(2)}) copy-start(f32[8,16,4096]{2,1,0:T(8,128)S(1)} %convert_add_fusion) | copy-start | bytes 6291460
  38.5 18.8 %collective-permute-start.1 = (bf16[4,16,4096]{2,1,0:T(8,128)(2,1)}, bf16[4,16,4096]{2,1,0:T(8,128)(2,1)}, u32[]{:S(2)}, u32[]{:S(2)}) collective-permute-start(bf16[4,16,4096]{2,1,0:T(8,128)(2,1)} %fusion), channel_id=1, source_target_pairs={{0,2},{1,3},{2,0},{3,1},{4,6},{5,7},{6,4},{7,5},{8,10},{9,11},{10,... | collective-permute-start | bytes 1572872 | tf_op jit(solution)/shard_map/ppermute | solution.py:228
  41.6 15.6 %copy-start.4 = (f32[8,16,4096]{2,1,0:T(8,128)S(1)}, f32[8,16,4096]{2,1,0:T(8,128)}, u32[]{:S(2)}) copy-start(f32[8,16,4096]{2,1,0:T(8,128)} %copy-done.3) | copy-start | bytes 6291460
  41.6 27.8 %all-to-all-start.1 = ((bf16[16,32,1024]{2,1,0:T(8,128)(2,1)}), bf16[16,32,1024]{2,1,0:T(8,128)(2,1)S(1)}, u32[]{:S(2)}, u32[]{:S(2)}) async-start(bf16[16,32,1024]{2,1,0:T(8,128)(2,1)} %get-tuple-element.12), calls=%async_computation.1 | async-start | bytes 2097152 | tf_op jit(solution)/shard_map/all_to_all | solution.py:198
  46.1 23.4 %copy-start.1 = (s32[4,186]{1,0:T(4,128)S(1)}, s32[4,186]{1,0:T(4,128)}, u32[]{:S(2)}) copy-start(s32[4,186]{1,0:T(4,128)} %ids_ref.1) | copy-start | bytes 8932
  58.5 1.0 copy-start.5
  59.5 32.8 %collective-permute-start.2 = (bf16[2,16,4096]{2,1,0:T(8,128)(2,1)S(1)}, bf16[2,16,4096]{2,1,0:T(8,128)(2,1)S(1)}, u32[]{:S(2)}, u32[]{:S(2)}) collective-permute-start(bf16[2,16,4096]{2,1,0:T(8,128)(2,1)S(1)} %fusion.1), channel_id=1, source_target_pairs={{0,4},{1,5},{2,6},{3,7},{4,0},{5,1},{6,2},{7,3},{8,12},{9,13},{10,... | collective-permute-start | bytes 786440 | tf_op jit(solution)/shard_map/ppermute | solution.py:228
  59.6 32.7 %copy-start.6 = (f32[4,16,4096]{2,1,0:T(8,128)S(1)}, f32[4,16,4096]{2,1,0:T(8,128)}, u32[]{:S(2)}) copy-start(f32[4,16,4096]{2,1,0:T(8,128)} %copy-done.5) | copy-start | bytes 3145732
  85.8 16.6 %all-to-all-start.2 = ((bf16[16,32,256]{2,1,0:T(8,128)(2,1)}), bf16[16,32,256]{2,1,0:T(8,128)(2,1)S(1)}, u32[]{:S(2)}, u32[]{:S(2)}) async-start(bf16[16,32,256]{2,1,0:T(8,128)(2,1)} %delta.1), calls=%async_computation.2 | async-start | bytes 524288 | tf_op jit(solution)/shard_map/all_to_all | solution.py:268
  103.2 11.9 %all-to-all-start.3 = ((bf16[16,16,256]{2,1,0:T(8,128)(2,1)}), bf16[16,16,256]{2,1,0:T(8,128)(2,1)S(1)}, u32[]{:S(2)}, u32[]{:S(2)}) async-start(bf16[16,16,256]{2,1,0:T(8,128)(2,1)} %pick.1), calls=%async_computation.3 | async-start | bytes 262144 | tf_op jit(solution)/shard_map/all_to_all | solution.py:275
  106.8 12.3 %collective-permute-start.3 = (bf16[1,16,4096]{2,1,0:T(8,128)(2,1)S(1)}, bf16[1,16,4096]{2,1,0:T(8,128)(2,1)S(1)}, u32[]{:S(2)}, u32[]{:S(2)}) collective-permute-start(bf16[1,16,4096]{2,1,0:T(8,128)(2,1)S(1)} %dynamic-slice_convert_fusion.1), channel_id=1, source_target_pairs={{0,8},{1,9},{2,10},{3,11},{4,12},{5,13},{6,14},{7,15},{8,0},{9,1},... | collective-permute-start | bytes 393224 | tf_op jit(solution)/shard_map/ppermute | solution.py:228

commit v2 on v1

--- a/solution.py
+++ b/solution.py
@@ -23,8 +23,8 @@
     return share, window, last, starts
 
 
-def params(**kw):
-    return pltpu.CompilerParams(vmem_limit_bytes=48 * 1024 * 1024, **kw)
+def params(mib=16):
+    return pltpu.CompilerParams(vmem_limit_bytes=mib * 1024 * 1024)
 
 
 def lane_iota(rows, lanes):
@@ -93,54 +93,76 @@
             for q in range(peers // 2):
                 piece = x_ref[2 * q + which].astype(F32)
                 piece = pltpu.roll(piece, window - scal_ref[0], 1)
-                mine_ref[side, q * row_dev : (q + 1) * row_dev] = piece[:, :share].astype(BF16)
-
-    w = w_ref[...]
-    keep = jnp.dot(mine_ref[0], w, preferred_element_type=F32)
-    keep_ref[...] = keep.reshape(keep_ref.shape)
-    send = jnp.dot(mine_ref[1], w, preferred_element_type=F32)
-    send_ref[...] = send.astype(BF16).reshape(send_ref.shape)
-
-
-def delta_kernel(plan, d_blocks, ids_ref, x_ref, v_ref, o_ref, rows_ref, acc_ref):
+                at = side * half + q * row_dev
+                mine_ref[at : at + row_dev] = piece[:, :share].astype(BF16)
+
+    both = jnp.dot(mine_ref[...], w_ref[...], preferred_element_type=F32)
+    keep_ref[...] = both[:half].reshape(keep_ref.shape)
+    send_ref[...] = both[half:].astype(BF16).reshape(send_ref.shape)
+
+
+def delta_kernel(plan, d_blocks, group, ids_ref, x_ref, v_hbm, o_ref, rows_ref, acc_ref, held_ref, sems):
     _, window, _, starts = plan
     local_var, f_blocks, capacity, _ = rows_ref.shape
-    group = v_ref.shape[1]
-    var, step = pl.program_id(0), pl.program_id(1)
-
-    @pl.when((var == 0) & (step == 0))
-    def _():
-        acc_ref[...] = jnp.zeros_like(acc_ref)
-        done = set()
-        for s, b in enumerate(starts):
-            for k in range(window // LANES):
-                tile = x_ref[s, :, k * LANES : (k + 1) * LANES].astype(F32)
-                for v in range(local_var):
-                    part = tile[v * capacity : (v + 1) * capacity]
-                    if b + k in done:
-                        part = part + rows_ref[v, b + k]
-                    rows_ref[v, b + k] = part
-                done.add(b + k)
-
-    places, products = [], []
-    for n in range(group):
-        block = ids_ref[var, step * group + n]
-        lhs = rows_ref[var, lax.div(block, d_blocks)].astype(BF16)
-        products.append(jnp.dot(lhs, v_ref[0, n], preferred_element_type=F32))
-        places.append(lax.rem(block, d_blocks))
-    for j, product in zip(places, products):
-        acc_ref[var, j] += product
-
-    @pl.when((var == pl.num_programs(0) - 1) & (step == pl.num_programs(1) - 1))
-    def _():
-        for j in range(d_blocks):
-            whole = jnp.concatenate([acc_ref[v, j] for v in range(local_var)], axis=0)
-            if len(o_ref.shape) == 3:
-                per = o_ref.shape[2] // LANES
-                k = j % per
-                o_ref[j // per, :, k * LANES : (k + 1) * LANES] = whole.astype(BF16)
+    chunks, _, size, _ = held_ref.shape
+    per = chunks // local_var
+
+    def fetch(c):
+        source = v_hbm.at[c // per, pl.ds((c % per) * group, group)]
+        return pltpu.make_async_copy(source, held_ref.at[c], sems.at[c])
+
+    for c in range(chunks):
+        fetch(c).start()
+
+    acc_ref[...] = jnp.zeros_like(acc_ref)
+    done = set()
+    for s, b in enumerate(starts):
+        for k in range(window // LANES):
+            tile = x_ref[s, :, k * LANES : (k + 1) * LANES].astype(F32)
+            for v in range(local_var):
+                part = tile[v * capacity : (v + 1) * capacity]
+                if b + k in done:
+                    part = part + rows_ref[v, b + k]
+                rows_ref[v, b + k] = part
+            done.add(b + k)
+
+    zeros = jnp.zeros((capacity, size), F32)
+
+    def one_chunk(c, carry):
+        var = lax.div(c, per)
+        first = lax.rem(c, per) * group
+        pltpu.make_async_copy(
+            v_hbm.at[var, pl.ds(first, group)], held_ref.at[c], sems.at[c]
+        ).wait()
+        sums = []
+        for n in range(0, group, 2):
+            blocks = [ids_ref[var, first + m] for m in range(n, min(n + 2, group))]
+            lhs = [rows_ref[var, lax.div(block, d_blocks)] for block in blocks]
+            if len(blocks) == 2:
+                upper = jnp.concatenate([lhs[0], zeros], axis=1)
+                lower = jnp.concatenate([zeros, lhs[1]], axis=1)
+                left = jnp.concatenate([upper, lower], axis=0).astype(BF16)
+                right = held_ref[c, n : n + 2].reshape(2 * size, size)
             else:
-                o_ref[:, j * LANES : (j + 1) * LANES] = whole.astype(BF16)
+                left = lhs[0].astype(BF16)
+                right = held_ref[c, n]
+            product = jnp.dot(left, right, preferred_element_type=F32)
+            for q, block in enumerate(blocks):
+                part = product[q * capacity : (q + 1) * capacity]
+                sums.append((lax.rem(block, d_blocks), part))
+        for column, part in sums:
+            acc_ref[var, column] += part
+        return carry
+
+    lax.fori_loop(0, chunks, one_chunk, 0)
+    for j in range(d_blocks):
+        whole = jnp.concatenate([acc_ref[v, j] for v in range(local_var)], axis=0)
+        if len(o_ref.shape) == 3:
+            per_peer = o_ref.shape[2] // LANES
+            k = j % per_peer
+            o_ref[j // per_peer, :, k * LANES : (k + 1) * LANES] = whole.astype(BF16)
+        else:
+            o_ref[:, j * LANES : (j + 1) * LANES] = whole.astype(BF16)
 
 
 def pick_kernel(place_ref, c_ref, o_ref):
@@ -151,6 +173,26 @@
     pick = jnp.where(pick, 1.0, 0.0).astype(BF16)
     found = jnp.dot(pick, c_ref[...].reshape(slots, cols), preferred_element_type=F32)
     o_ref[...] = found.astype(BF16).reshape(o_ref.shape)
+
+
+def halve_kernel(bit_ref, keep_ref, got_ref, next_ref, send_ref):
+    bit = bit_ref[0]
+    for q in range(next_ref.shape[0]):
+        mine, other = 2 * q + bit, 2 * q + 1 - bit
+        next_ref[q] = keep_ref[mine] + got_ref[mine].astype(F32)
+        send_ref[q] = (keep_ref[other] + got_ref[other].astype(F32)).astype(BF16)
+
+
+def finish_kernel(keep_ref, got_ref, own_ref, o_ref):
+    peers, _, cols = own_ref.shape
+    base = keep_ref[0] + got_ref[0].astype(F32)
+    if cols % LANES == 0:
+        for s in range(peers):
+            at = slice(s * cols, (s + 1) * cols)
+            o_ref[:, at] = (base[:, at] + own_ref[s].astype(F32)).astype(BF16)
+    else:
+        own = jnp.concatenate([own_ref[s].astype(F32) for s in range(peers)], axis=1)
+        o_ref[...] = (base + own).astype(BF16)
 
 
 def split_factor(count, most):
@@ -176,6 +218,7 @@
 
     scal = jnp.stack([own_shift(plan), me % 2]).astype(jnp.int32)
     smem = pl.BlockSpec(memory_space=pltpu.SMEM)
+    vmem = pl.BlockSpec(memory_space=pltpu.VMEM)
 
     outgoing = pl.pallas_call(
         functools.partial(split_kernel, plan),
@@ -191,11 +234,12 @@
             jax.ShapeDtypeStruct((peers, local_slots, window), BF16),
             jax.ShapeDtypeStruct((all_rows, 1), jnp.int32),
         ),
-        in_specs=[smem, pl.BlockSpec(memory_space=pltpu.VMEM), pl.BlockSpec(memory_space=pltpu.VMEM)],
+        in_specs=[smem, vmem, vmem],
         compiler_params=params(),
         name="route",
     )(scal, x, variant_slot.reshape(1, variants))
     arrived = lax.all_to_all(slots, "cols", 0, 0)
+    x, place = lax.optimization_barrier((x, place))
 
     tile = min(512, width_d)
     keep, send = pl.pallas_call(
@@ -214,7 +258,7 @@
             pl.BlockSpec((half, row_dev, tile), lambda t: (0, 0, t)),
             pl.BlockSpec((half, row_dev, tile), lambda t: (0, 0, t)),
         ),
-        scratch_shapes=[pltpu.VMEM((2, all_rows // 2, share), BF16)],
+        scratch_shapes=[pltpu.VMEM((all_rows, share), BF16)],
         compiler_params=params(),
         cost_estimate=pl.CostEstimate(
             flops=2 * all_rows * share * width_d,
@@ -223,39 +267,39 @@
         ),
         name="base",
     )(scal, x, down_weight)
+    send, arrived = lax.optimization_barrier((send, arrived))
     step = 1
     while True:
         got = lax.ppermute(send, "cols", [(i, i ^ step) for i in range(peers)])
-        total = keep + got.astype(F32)
         step *= 2
         if step == peers:
             break
-        bit = (me // step) % 2
-        total = total.reshape(total.shape[0] // 2, 2, row_dev, width_d)
-        keep = lax.dynamic_index_in_dim(total, bit, 1, keepdims=False)
-        send = lax.dynamic_index_in_dim(total, 1 - bit, 1, keepdims=False).astype(BF16)
-    summed = total.reshape(row_dev, width_d)
+        bit = ((me // step) % 2).astype(jnp.int32).reshape(1)
+        left = (keep.shape[0] // 2, row_dev, width_d)
+        keep, send = pl.pallas_call(
+            halve_kernel,
+            in_specs=[smem, vmem, vmem],
+            out_shape=(jax.ShapeDtypeStruct(left, F32), jax.ShapeDtypeStruct(left, BF16)),
+            compiler_params=params(),
+            name="halve",
+        )(bit, keep, got)
 
     group = split_factor(count, 64)
     aligned = slice_d % LANES == 0
     shape = (peers, local_slots, slice_d) if aligned else (local_slots, width_d)
+    chunks = local_var * (count // group)
     deltas = pl.pallas_call(
-        functools.partial(delta_kernel, plan, d_blocks),
-        grid_spec=pltpu.PrefetchScalarGridSpec(
-            num_scalar_prefetch=1,
-            grid=(local_var, count // group),
-            in_specs=[
-                pl.BlockSpec((peers, local_slots, window), lambda v, s, ids: (0, 0, 0)),
-                pl.BlockSpec((1, group, block_size, block_size), lambda v, s, ids: (v, s, 0, 0)),
-            ],
-            out_specs=pl.BlockSpec(shape, lambda v, s, ids: (0,) * len(shape)),
-            scratch_shapes=[
-                pltpu.VMEM((local_var, f_blocks, capacity, block_size), F32),
-                pltpu.VMEM((local_var, d_blocks, capacity, block_size), F32),
-            ],
-        ),
+        functools.partial(delta_kernel, plan, d_blocks, group),
+        in_specs=[smem, vmem, pl.BlockSpec(memory_space=pl.ANY)],
+        out_specs=vmem,
+        scratch_shapes=[
+            pltpu.VMEM((local_var, f_blocks, capacity, block_size), F32),
+            pltpu.VMEM((local_var, d_blocks, capacity, block_size), F32),
+            pltpu.VMEM((chunks, group, block_size, block_size), BF16),
+            pltpu.SemaphoreType.DMA((chunks,)),
+        ],
         out_shape=jax.ShapeDtypeStruct(shape, BF16),
-        compiler_params=params(),
+        compiler_params=params(36),
         cost_estimate=pl.CostEstimate(
             flops=2 * local_slots * count * block_size * block_size,
             bytes_accessed=2 * local_var * count * block_size * block_size,
@@ -273,8 +317,12 @@
         name="pick",
     )(place, columns)
     own = lax.all_to_all(by_row, "cols", 0, 0)
-    own = own.transpose(1, 0, 2).reshape(row_dev, width_d)
-    return (summed + own.astype(F32)).astype(BF16)
+    return pl.pallas_call(
+        finish_kernel,
+        out_shape=jax.ShapeDtypeStruct((row_dev, width_d), BF16),
+        compiler_params=params(),
+        name="finish",
+    )(keep, got, own)
 
 
 def solution(mesh):

time: 121 us -> 109 us (0.901)
  waiting for transfers between devices: 57.8 us -> 47.2 us
  Pallas kernels: 29.1 us -> 21.1 us
  local copies, waits for them, and re-layouts: 3.75 us -> 11.7 us
  other arithmetic: 3.44 us -> 0.08 us
  starting transfers between devices: 25.5 us -> 28.2 us
    ppermute x4, waiting for transfers between devices: 18.1 us -> 6.51 us  [body(): got = lax.ppermute(send, 'cols', [(i, i ^ step) for i in range(peers)])]
    unnamed x15 -> x19, local copies, waits for them, and re-layouts: 2.76 us -> 11.7 us
    pallas_call x1 -> x5, Pallas kernels: 16.3 us -> 11.8 us  [the longest x1 9.96 us: body(): pl.pallas_call(functools.partial(delta_kernel, plan, d_blocks, group), in...]
    ppermute x4, starting transfers between devices: 3.68 us -> 7.33 us  [body(): got = lax.ppermute(send, 'cols', [(i, i ^ step) for i in range(peers)])]
    pallas_call x1, Pallas kernels: 8.58 us -> 5.11 us  [body(): pl.pallas_call(functools.partial(base_kernel, plan), grid=(width_d // til...]
    add x3 -> x0, other arithmetic: 2.64 us -> none  [body(): total = keep + got.astype(F32)]
    all_to_all x1, waiting for transfers between devices: 9.84 us -> 12.4 us  [body(): arrived = lax.all_to_all(slots, 'cols', 0, 0)]
    all_to_all x1, waiting for transfers between devices: 9.97 us -> 8.43 us  [body(): columns = lax.all_to_all(deltas, 'cols', 0, 0)]
  transfers between devices with their start and end apart: 8 -> 8, of which waited for: 7 -> 6; matrix products, arithmetic and copies ran while one was open for 1% -> 0% of each run, Pallas kernels for 16% -> 15%
where the time goes in v2:
time: 109 us; the launch traced here: 108 us
  waiting for transfers between devices  47.2 us (43%)
  starting transfers between devices  28.2 us (26%)
  Pallas kernels  21.1 us (19%)
  local copies, waits for them, and re-layouts  11.7 us (11%)
    all_to_all x1, waiting for transfers between devices, body(): x = lax.all_to_all(outgoing, 'cols', 0, 0)  14.4 us
    all_to_all x1, waiting for transfers between devices, body(): arrived = lax.all_to_all(slots, 'cols', 0, 0)  12.4 us
    unnamed x19, local copies, waits for them, and re-layouts  11.7 us
    pallas_call x1, Pallas kernels, body(): pl.pallas_call(functools.partial(delta_kernel, plan, d_blocks, group), in...  9.96 us
    all_to_all x1, waiting for transfers between devices, body(): columns = lax.all_to_all(deltas, 'cols', 0, 0)  8.43 us
    all_to_all x1, starting transfers between devices, body(): x = lax.all_to_all(outgoing, 'cols', 0, 0)  7.52 us
    ppermute x4, starting transfers between devices, body(): got = lax.ppermute(send, 'cols', [(i, i ^ step) for i in range(peers)])  7.33 us
    ppermute x4, waiting for transfers between devices, body(): got = lax.ppermute(send, 'cols', [(i, i ^ step) for i in range(peers)])  6.51 us
  transfers between devices with their start and end apart: 8, of which 6 were waited for; matrix products, arithmetic and copies ran while one was open for 0% of the time, Pallas kernels for 15%

profile of v2, /device:TPU:0, one launch (start us, length us, event | category | flops | bytes accessed | tf_op | source)
XLA Modules:
  0.0 108.3 jit_solution(1724776022443822906)
XLA Ops:
  0.0 0.7 copy.7.id_ref
  0.7 1.0 copy-done.5
  1.8 0.9 split_rows.1
  2.7 7.5 %all-to-all-start = ((bf16[16,16,1024]{2,1,0:T(8,128)(2,1)}), bf16[16,16,1024]{2,1,0:T(8,128)(2,1)S(1)}, u32[]{:S(2)}, u32[]{:S(2)}) async-start(bf16[16,16,1024]{2,1,0:T(8,128)(2,1)} %split_rows.1), calls=%async_computation | async-start | bytes 1048576 | tf_op jit(solution)/shard_map/all_to_all | solution.py:229
  10.2 0.1 pad_add_fusion.shift_ref.scal_ref
  10.3 14.4 %all-to-all-done.x_ref = bf16[16,16,1024]{2,1,0:T(8,128)(2,1)S(1)} async-done(((bf16[16,16,1024]{2,1,0:T(8,128)(2,1)}), bf16[16,16,1024]{2,1,0:T(8,128)(2,1)S(1)}, u32[]{:S(2)}, u32[]{:S(2)}) %all-to-all-start) | async-done | bytes 524320 | tf_op jit(solution)/shard_map/all_to_all | solution.py:229
  24.6 0.7 copy-done.7
  25.3 2.4 %route.1 = (bf16[16,32,1024]{2,1,0:T(8,128)(2,1)}, s32[256,1]{1,0:T(8,128)S(1)}) custom-call(s32[2]{0:T(128)S(1)} %pad_add_fusion.shift_ref.scal_ref, bf16[16,16,1024]{2,1,0:T(8,128)(2,1)S(1)} %all-to-all-done.x_ref, s32[1,64]{1,0:T(1,128)S(1)} %bitcast.6), custom_call_target="tpu_custom_call" | custom-call | tf_op jit(solution)/shard_map/route/pallas_call | solution.py:231
  27.7 4.1 %all-to-all-start.1 = ((bf16[16,32,1024]{2,1,0:T(8,128)(2,1)}), bf16[16,32,1024]{2,1,0:T(8,128)(2,1)S(1)}, u32[]{:S(2)}, u32[]{:S(2)}) async-start(bf16[16,32,1024]{2,1,0:T(8,128)(2,1)} %get-tuple-element.23), calls=%async_computation.1 | async-start | bytes 2097152 | tf_op jit(solution)/shard_map/all_to_all | solution.py:241
  31.8 3.1 %copy-done = bf16[928,4096]{1,0:T(8,128)(2,1)S(1)} copy-done((bf16[928,4096]{1,0:T(8,128)(2,1)S(1)}, bf16[928,4096]{1,0:T(8,128)(2,1)}, u32[]{:S(2)}) %copy-start) | copy-done | bytes 7602200
  35.0 5.1 %base.1 = (f32[8,16,4096]{2,1,0:T(8,128)S(1)}, bf16[8,16,4096]{2,1,0:T(8,128)(2,1)S(1)}) custom-call(s32[2]{0:T(128)S(1)} %pad_add_fusion.shift_ref.scal_ref, bf16[16,16,1024]{2,1,0:T(8,128)(2,1)S(1)} %all-to-all-done.x_ref, bf16[928,4096]{1,0:T(8,128)(2,1)S(1)} %copy-done), custom_call_target="tpu_custom_call" | custom-call | flops 1946157056 | bytes 10747904 | tf_op jit(solution)/shard_map/base/pallas_call | solution.py:245
  40.1 1.3 %copy-done.1 = f32[8,16,4096]{2,1,0:T(8,128)} copy-done((f32[8,16,4096]{2,1,0:T(8,128)}, f32[8,16,4096]{2,1,0:T(8,128)S(1)}, u32[]{:S(2)}) %copy-start.1) | copy-done | bytes 2097176
  41.4 1.0 copy-done.8
  42.4 12.4 %all-to-all-done.1.x_ref = bf16[16,32,1024]{2,1,0:T(8,128)(2,1)S(1)} async-done(((bf16[16,32,1024]{2,1,0:T(8,128)(2,1)}), bf16[16,32,1024]{2,1,0:T(8,128)(2,1)S(1)}, u32[]{:S(2)}, u32[]{:S(2)}) %all-to-all-start.1) | async-done | bytes 1048608 | tf_op jit(solution)/shard_map/all_to_all | solution.py:241
  54.7 0.6 collective-permute-start
  55.3 2.5 %collective-permute-done.got_ref = bf16[8,16,4096]{2,1,0:T(8,128)(2,1)S(1)} collective-permute-done((bf16[8,16,4096]{2,1,0:T(8,128)(2,1)}, bf16[8,16,4096]{2,1,0:T(8,128)(2,1)S(1)}, u32[]{:S(2)}, u32[]{:S(2)}) %collective-permute-start) | collective-permute-done | bytes 1048608 | tf_op jit(solution)/shard_map/ppermute | solution.py:273
  57.8 1.0 copy-done.3
  58.8 1.6 %copy-done.2 = f32[8,16,4096]{2,1,0:T(8,128)S(1)} copy-done((f32[8,16,4096]{2,1,0:T(8,128)S(1)}, f32[8,16,4096]{2,1,0:T(8,128)}, u32[]{:S(2)}) %copy-start.2) | copy-done | bytes 2097176
  60.4 1.2 %copy-done.4 = bf16[8,16,4096]{2,1,0:T(8,128)(2,1)S(1)} copy-done((bf16[8,16,4096]{2,1,0:T(8,128)(2,1)S(1)}, bf16[8,16,4096]{2,1,0:T(8,128)(2,1)}, u32[]{:S(2)}) %copy-start.4) | copy-done | bytes 1048600
  61.7 0.9 halve.3
  62.6 2.0 %collective-permute-start.1 = (bf16[4,16,4096]{2,1,0:T(8,128)(2,1)}, bf16[4,16,4096]{2,1,0:T(8,128)(2,1)S(1)}, u32[]{:S(2)}, u32[]{:S(2)}) collective-permute-start(bf16[4,16,4096]{2,1,0:T(8,128)(2,1)} %get-tuple-element.26), channel_id=1, source_target_pairs={{0,2},{1,3},{2,0},{3,1},{4,6},{5,7},{6,4},{7,5},{8,10},{9,11},{10,... | collective-permute-start | bytes 1572872 | tf_op jit(solution)/shard_map/ppermute | solution.py:273
  64.6 10.0 %delta.1 = bf16[16,32,256]{2,1,0:T(8,128)(2,1)} custom-call(s32[4,186]{1,0:T(4,128)S(1)} %copy-done.6, bf16[16,32,1024]{2,1,0:T(8,128)(2,1)S(1)} %all-to-all-done.1.x_ref, bf16[4,186,128,128]{3,2,1,0:T(8,128)(2,1)} %v_hbm.1), custom_call_target="tpu_custom_call" | custom-call | flops 195035136 | bytes 24379392 | tf_op jit(solution)/shard_map/delta/pallas_call | solution.py:291
  74.6 5.7 %all-to-all-start.2 = ((bf16[16,32,256]{2,1,0:T(8,128)(2,1)}), bf16[16,32,256]{2,1,0:T(8,128)(2,1)S(1)}, u32[]{:S(2)}, u32[]{:S(2)}) async-start(bf16[16,32,256]{2,1,0:T(8,128)(2,1)} %delta.1), calls=%async_computation.2 | async-start | bytes 524288 | tf_op jit(solution)/shard_map/all_to_all | solution.py:312
  80.3 0.1 halve.4
  80.4 2.0 %collective-permute-start.2 = (bf16[2,16,4096]{2,1,0:T(8,128)(2,1)S(1)}, bf16[2,16,4096]{2,1,0:T(8,128)(2,1)S(1)}, u32[]{:S(2)}, u32[]{:S(2)}) collective-permute-start(bf16[2,16,4096]{2,1,0:T(8,128)(2,1)S(1)} %get-tuple-element.28), channel_id=1, source_target_pairs={{0,4},{1,5},{2,6},{3,7},{4,0},{5,1},{6,2},{7,3},{8,12},{9,13},{10,... | collective-permute-start | bytes 786440 | tf_op jit(solution)/shard_map/ppermute | solution.py:273
  82.4 8.4 %all-to-all-done.2.c_ref = bf16[16,32,256]{2,1,0:T(8,128)(2,1)S(1)} async-done(((bf16[16,32,256]{2,1,0:T(8,128)(2,1)}), bf16[16,32,256]{2,1,0:T(8,128)(2,1)S(1)}, u32[]{:S(2)}, u32[]{:S(2)}) %all-to-all-start.2) | async-done | bytes 262176 | tf_op jit(solution)/shard_map/all_to_all | solution.py:312
  90.8 0.9 pick.1
  91.7 3.5 %all-to-all-start.3 = ((bf16[16,16,256]{2,1,0:T(8,128)(2,1)}), bf16[16,16,256]{2,1,0:T(8,128)(2,1)S(1)}, u32[]{:S(2)}, u32[]{:S(2)}) async-start(bf16[16,16,256]{2,1,0:T(8,128)(2,1)} %pick.1), calls=%async_computation.3 | async-start | bytes 262144 | tf_op jit(solution)/shard_map/all_to_all | solution.py:319
  95.3 2.8 %collective-permute-start.3 = (bf16[1,16,4096]{2,1,0:T(8,128)(2,1)S(1)}, bf16[1,16,4096]{2,1,0:T(8,128)(2,1)S(1)}, u32[]{:S(2)}, u32[]{:S(2)}) collective-permute-start(bf16[1,16,4096]{2,1,0:T(8,128)(2,1)S(1)} %get-tuple-element.30), channel_id=1, source_target_pairs={{0,8},{1,9},{2,10},{3,11},{4,12},{5,13},{6,14},{7,15},{8,0},{9,1},... | collective-permute-start | bytes 393224 | tf_op jit(solution)/shard_map/ppermute | solution.py:273
  98.1 5.5 %all-to-all-done.3.own_ref = bf16[16,16,256]{2,1,0:T(8,128)(2,1)S(1)} async-done(((bf16[16,16,256]{2,1,0:T(8,128)(2,1)}), bf16[16,16,256]{2,1,0:T(8,128)(2,1)S(1)}, u32[]{:S(2)}, u32[]{:S(2)}) %all-to-all-start.3) | async-done | bytes 131104 | tf_op jit(solution)/shard_map/all_to_all | solution.py:319
  103.6 4.0 %collective-permute-done.3.got_ref = bf16[1,16,4096]{2,1,0:T(8,128)(2,1)S(1)} collective-permute-done((bf16[1,16,4096]{2,1,0:T(8,128)(2,1)S(1)}, bf16[1,16,4096]{2,1,0:T(8,128)(2,1)S(1)}, u32[]{:S(2)}, u32[]{:S(2)}) %collective-permute-start.3) | collective-permute-done | bytes 131104 | tf_op jit(solution)/shard_map/ppermute | solution.py:273
  107.6 0.7 finish.1
  (13 shorter events, 0.1 us)
Async XLA Ops:
  0.7 1.0 copy-start.5
  2.7 61.9 %copy-start.6 = (s32[4,186]{1,0:T(4,128)S(1)}, s32[4,186]{1,0:T(4,128)}, u32[]{:S(2)}) copy-start(s32[4,186]{1,0:T(4,128)} %ids_ref.1) | copy-start | bytes 8932
  2.7 22.0 %all-to-all-start = ((bf16[16,16,1024]{2,1,0:T(8,128)(2,1)}), bf16[16,16,1024]{2,1,0:T(8,128)(2,1)S(1)}, u32[]{:S(2)}, u32[]{:S(2)}) async-start(bf16[16,16,1024]{2,1,0:T(8,128)(2,1)} %split_rows.1), calls=%async_computation | async-start | bytes 1048576 | tf_op jit(solution)/shard_map/all_to_all | solution.py:229
  24.6 0.7 copy-start.7
  27.7 27.0 %all-to-all-start.1 = ((bf16[16,32,1024]{2,1,0:T(8,128)(2,1)}), bf16[16,32,1024]{2,1,0:T(8,128)(2,1)S(1)}, u32[]{:S(2)}, u32[]{:S(2)}) async-start(bf16[16,32,1024]{2,1,0:T(8,128)(2,1)} %get-tuple-element.23), calls=%async_computation.1 | async-start | bytes 2097152 | tf_op jit(solution)/shard_map/all_to_all | solution.py:241
  31.8 3.2 %copy-start = (bf16[928,4096]{1,0:T(8,128)(2,1)S(1)}, bf16[928,4096]{1,0:T(8,128)(2,1)}, u32[]{:S(2)}) copy-start(bf16[928,4096]{1,0:T(8,128)(2,1)} %w_ref.1) | copy-start | bytes 22806532
  40.1 1.3 %copy-start.1 = (f32[8,16,4096]{2,1,0:T(8,128)}, f32[8,16,4096]{2,1,0:T(8,128)S(1)}, u32[]{:S(2)}) copy-start(f32[8,16,4096]{2,1,0:T(8,128)S(1)} %get-tuple-element.21.keep_ref) | copy-start | bytes 6291460
  41.4 1.0 copy-start.8
  54.7 3.1 %collective-permute-start = (bf16[8,16,4096]{2,1,0:T(8,128)(2,1)}, bf16[8,16,4096]{2,1,0:T(8,128)(2,1)S(1)}, u32[]{:S(2)}, u32[]{:S(2)}) collective-permute-start(bf16[8,16,4096]{2,1,0:T(8,128)(2,1)} %copy-done.8), channel_id=1, source_target_pairs={{0,1},{1,0},{2,3},{3,2},{4,5},{5,4},{6,7},{7,6},{8,9},{9,8},{10,11... | collective-permute-start | bytes 3145736 | tf_op jit(solution)/shard_map/ppermute | solution.py:273
  57.8 1.0 copy-start.3
  58.8 1.6 %copy-start.2 = (f32[8,16,4096]{2,1,0:T(8,128)S(1)}, f32[8,16,4096]{2,1,0:T(8,128)}, u32[]{:S(2)}) copy-start(f32[8,16,4096]{2,1,0:T(8,128)} %copy-done.1) | copy-start | bytes 6291460
  60.4 1.2 %copy-start.4 = (bf16[8,16,4096]{2,1,0:T(8,128)(2,1)S(1)}, bf16[8,16,4096]{2,1,0:T(8,128)(2,1)}, u32[]{:S(2)}) copy-start(bf16[8,16,4096]{2,1,0:T(8,128)(2,1)} %copy-done.3) | copy-start | bytes 3145732
  62.6 17.7 %collective-permute-start.1 = (bf16[4,16,4096]{2,1,0:T(8,128)(2,1)}, bf16[4,16,4096]{2,1,0:T(8,128)(2,1)S(1)}, u32[]{:S(2)}, u32[]{:S(2)}) collective-permute-start(bf16[4,16,4096]{2,1,0:T(8,128)(2,1)} %get-tuple-element.26), channel_id=1, source_target_pairs={{0,2},{1,3},{2,0},{3,1},{4,6},{5,7},{6,4},{7,5},{8,10},{9,11},{10,... | collective-permute-start | bytes 1572872 | tf_op jit(solution)/shard_map/ppermute | solution.py:273
  74.6 16.2 %all-to-all-start.2 = ((bf16[16,32,256]{2,1,0:T(8,128)(2,1)}), bf16[16,32,256]{2,1,0:T(8,128)(2,1)S(1)}, u32[]{:S(2)}, u32[]{:S(2)}) async-start(bf16[16,32,256]{2,1,0:T(8,128)(2,1)} %delta.1), calls=%async_computation.2 | async-start | bytes 524288 | tf_op jit(solution)/shard_map/all_to_all | solution.py:312
  80.4 14.9 %collective-permute-start.2 = (bf16[2,16,4096]{2,1,0:T(8,128)(2,1)S(1)}, bf16[2,16,4096]{2,1,0:T(8,128)(2,1)S(1)}, u32[]{:S(2)}, u32[]{:S(2)}) collective-permute-start(bf16[2,16,4096]{2,1,0:T(8,128)(2,1)S(1)} %get-tuple-element.28), channel_id=1, source_target_pairs={{0,4},{1,5},{2,6},{3,7},{4,0},{5,1},{6,2},{7,3},{8,12},{9,13},{10,... | collective-permute-start | bytes 786440 | tf_op jit(solution)/shard_map/ppermute | solution.py:273
  91.7 11.9 %all-to-all-start.3 = ((bf16[16,16,256]{2,1,0:T(8,128)(2,1)}), bf16[16,16,256]{2,1,0:T(8,128)(2,1)S(1)}, u32[]{:S(2)}, u32[]{:S(2)}) async-start(bf16[16,16,256]{2,1,0:T(8,128)(2,1)} %pick.1), calls=%async_computation.3 | async-start | bytes 262144 | tf_op jit(solution)/shard_map/all_to_all | solution.py:319
  95.3 12.3 %collective-permute-start.3 = (bf16[1,16,4096]{2,1,0:T(8,128)(2,1)S(1)}, bf16[1,16,4096]{2,1,0:T(8,128)(2,1)S(1)}, u32[]{:S(2)}, u32[]{:S(2)}) collective-permute-start(bf16[1,16,4096]{2,1,0:T(8,128)(2,1)S(1)} %get-tuple-element.30), channel_id=1, source_target_pairs={{0,8},{1,9},{2,10},{3,11},{4,12},{5,13},{6,14},{7,15},{8,0},{9,1},... | collective-permute-start | bytes 393224 | tf_op jit(solution)/shard_map/ppermute | solution.py:273

commit v3 on v2

v3 whole, which is shorter than its diff:
```python
import functools

import jax
import jax.numpy as jnp
from jax import lax
from jax.experimental import pallas as pl
from jax.experimental.pallas import tpu as pltpu
from jax.sharding import PartitionSpec as P

LANES = 128
BF16 = jnp.bfloat16
F32 = jnp.float32


def windows(width_f, peers):
    share = width_f // peers
    most = max((s * share) % LANES for s in range(peers))
    window = -(-(share + most) // LANES) * LANES
    if window == share:
        window += LANES
    last = (width_f - window) // LANES
    starts = [min(s * share // LANES, last) for s in range(peers)]
    return share, window, last, starts


def params(mib=16):
    return pltpu.CompilerParams(vmem_limit_bytes=mib * 1024 * 1024)


def lane_iota(rows, lanes):
    return lax.broadcasted_iota(jnp.int32, (rows, lanes), 1)


def split_kernel(plan, h_ref, id_ref, slot_ref, o_ref):
    share, window, _, starts = plan
    rows = h_ref.shape[0]
    variants = slot_ref.shape[1]
    lane = lane_iota(rows, window)
    diagonal = lax.broadcasted_iota(jnp.int32, (rows, rows), 0) == lane_iota(rows, rows)
    ids = jnp.sum(jnp.where(diagonal, id_ref[...].astype(F32), 0.0), axis=1, keepdims=True)
    named = ids.astype(jnp.int32) == lane_iota(rows, variants)
    slot = jnp.sum(jnp.where(named, slot_ref[...].astype(F32), 0.0), axis=1, keepdims=True)
    for s, b in enumerate(starts):
        spare = (s * share - b * LANES + share) % window
        piece = h_ref[:, b * LANES : b * LANES + window].astype(F32)
        o_ref[s] = jnp.where(lane == spare, slot, piece).astype(BF16)


def own_shift(plan):
    share, _, last, _ = plan
    start = lax.axis_index("cols") * share
    return start - jnp.minimum(start // LANES, last) * LANES


def route_kernel(plan, capacity, shift_ref, x_ref, o_ref, place_ref):
    share, window, _, _ = plan
    peers, row_dev, _ = x_ref.shape
    rows = peers * row_dev
    slots = o_ref.shape[0] * o_ref.shape[1]
    variants = slots // capacity
    shift = shift_ref[0]
    x = x_ref[...].reshape(rows, window).astype(F32)
    lane = lane_iota(rows, window)
    spare = lax.rem(shift + share, window)
    slot = jnp.sum(jnp.where(lane == spare, x, 0.0), axis=1, keepdims=True)
    data = jnp.where((lane >= shift) & (lane < shift + share), x, 0.0).astype(BF16)
    onehot = jnp.where(slot.astype(jnp.int32) == lane_iota(rows, variants), 1.0, 0.0)
    row_i = lax.broadcasted_iota(jnp.int32, (rows, rows), 0)
    row_j = lane_iota(rows, rows)
    earlier = jnp.where(row_j < row_i, 1.0, 0.0).astype(BF16)
    before = jnp.dot(earlier, onehot.astype(BF16), preferred_element_type=F32)
    rank = jnp.sum(before * onehot, axis=1, keepdims=True)
    place = slot * capacity + rank
    place_ref[...] = place.astype(jnp.int32)
    across = jnp.sum(jnp.where(row_i == row_j, place, 0.0), axis=0, keepdims=True)
    pick = across.astype(jnp.int32) == lax.broadcasted_iota(jnp.int32, (slots, rows), 0)
    pick = jnp.where(pick, 1.0, 0.0).astype(BF16)
    filled = jnp.dot(pick, data, preferred_element_type=F32).astype(BF16)
    o_ref[...] = filled.reshape(o_ref.shape)


def base_kernel(plan, scal_ref, x_ref, w_ref, place_ref, o_ref, own_ref, mine_ref):
    share, window, _, _ = plan
    peers, row_dev, _ = x_ref.shape

    @pl.when(pl.program_id(0) == 0)
    def _():
        bit = scal_ref[1]
        for side in (0, 1):
            which = bit if side == 0 else 1 - bit
            for q in range(peers // 2):
                piece = x_ref[2 * q + which].astype(F32)
                piece = pltpu.roll(piece, window - scal_ref[0], 1)
                at = (side * (peers // 2) + q) * row_dev
                mine_ref[at : at + row_dev] = piece[:, :share].astype(BF16)
                own_ref[at : at + row_dev] = place_ref[2 * q + which]

    o_ref[...] = jnp.dot(mine_ref[...], w_ref[...], preferred_element_type=F32)


def delta_kernel(
    plan, d_blocks, group, scal_ref, ids_ref, x_hbm, v_hbm, base_hbm, own_ref, *rest
):
    keeps, sends = rest[0:2], rest[2:4]
    rows_ref, acc_ref, held_ref, x_ref, base_ref, sems, x_sem, base_sem = rest[4:]
    _, window, _, starts = plan
    local_var, f_blocks, capacity, _ = rows_ref.shape
    chunks, _, size, _ = held_ref.shape
    per = chunks // local_var

    def fetch(c):
        source = v_hbm.at[c // per, pl.ds((c % per) * group, group)]
        return pltpu.make_async_copy(source, held_ref.at[c], sems.at[c])

    x_copy = pltpu.make_async_copy(x_hbm, x_ref, x_sem)
    x_copy.start()
    for c in range(chunks):
        fetch(c).start()
    base_copy = pltpu.make_async_copy(base_hbm, base_ref, base_sem)
    base_copy.start()

    acc_ref[...] = jnp.zeros_like(acc_ref)
    x_copy.wait()
    done = set()
    for s, b in enumerate(starts):
        for k in range(window // LANES):
            tile = x_ref[s, :, k * LANES : (k + 1) * LANES].astype(F32)
            for v in range(local_var):
                part = tile[v * capacity : (v + 1) * capacity]
                if b + k in done:
                    part = part + rows_ref[v, b + k]
                rows_ref[v, b + k] = part
            done.add(b + k)

    zeros = jnp.zeros((capacity, size), F32)

    def one_chunk(c, carry):
        var = lax.div(c, per)
        first = lax.rem(c, per) * group
        pltpu.make_async_copy(
            v_hbm.at[var, pl.ds(first, group)], held_ref.at[c], sems.at[c]
        ).wait()
        sums = []
        for n in range(0, group, 2):
            blocks = [ids_ref[var, first + m] for m in range(n, min(n + 2, group))]
            lhs = [rows_ref[var, lax.div(block, d_blocks)] for block in blocks]
            if len(blocks) == 2:
                upper = jnp.concatenate([lhs[0], zeros], axis=1)
                lower = jnp.concatenate([zeros, lhs[1]], axis=1)
                left = jnp.concatenate([upper, lower], axis=0).astype(BF16)
                right = held_ref[c, n : n + 2].reshape(2 * size, size)
            else:
                left = lhs[0].astype(BF16)
                right = held_ref[c, n]
            product = jnp.dot(left, right, preferred_element_type=F32)
            for q, block in enumerate(blocks):
                part = product[q * capacity : (q + 1) * capacity]
                sums.append((lax.rem(block, d_blocks), part))
        for column, part in sums:
            acc_ref[var, column] += part
        return carry

    lax.fori_loop(0, chunks, one_chunk, 0)

    all_rows = base_ref.shape[0]
    slots = local_var * capacity
    join = own_ref[...] - scal_ref[2] == lane_iota(all_rows, slots)
    join = jnp.where(join, 1.0, 0.0).astype(BF16)
    per_side = d_blocks // 2
    base_copy.wait()
    for j in range(d_blocks):
        whole = jnp.concatenate([acc_ref[v, j] for v in range(local_var)], axis=0).astype(BF16)
        total = base_ref[:, j * size : (j + 1) * size]
        total = total + jnp.dot(join, whole, preferred_element_type=F32)
        keep_ref, send_ref = keeps[j // per_side], sends[j // per_side]
        at = slice((j % per_side) * size, (j % per_side + 1) * size)
        tile = keep_ref.shape[:2] + (size,)
        keep_ref[:, :, at] = total[: all_rows // 2].reshape(tile)
        send_ref[:, :, at] = total[all_rows // 2 :].astype(BF16).reshape(tile)


def halve_kernel(stride, bit_ref, keep_ref, got_ref, next_ref, send_ref):
    bit = bit_ref[0]
    for q in range(next_ref.shape[0]):
        first = q // stride * 2 * stride + q % stride
        mine, other = first + stride * bit, first + stride * (1 - bit)
        next_ref[q] = keep_ref[mine] + got_ref[mine].astype(F32)
        send_ref[q] = (keep_ref[other] + got_ref[other].astype(F32)).astype(BF16)


def finish_kernel(*refs):
    o_ref = refs[-1]
    cols = o_ref.shape[1] // 2
    for side in (0, 1):
        keep_ref, got_ref = refs[2 * side : 2 * side + 2]
        total = keep_ref[0] + got_ref[0].astype(F32)
        o_ref[:, side * cols : (side + 1) * cols] = total.astype(BF16)


def split_factor(count, most):
    return max(g for g in range(1, most + 1) if count % g == 0)


def body(hidden, down_weight, delta_values, block_ids, variant_slot, row_variant):
    peers = lax.axis_size("cols")
    me = lax.axis_index("cols")
    row_dev, width_f = hidden.shape
    width_d = down_weight.shape[1]
    local_var, count, block_size, _ = delta_values.shape
    variants = variant_slot.shape[0]
    all_rows = row_dev * peers
    capacity = 2 * all_rows // variants
    d_blocks = width_d // block_size
    f_blocks = width_f // block_size
    local_slots = local_var * capacity
    plan = windows(width_f, peers)
    share, window, _, _ = plan
    half = peers // 2

    scal = jnp.stack([own_shift(plan), me % 2, me * local_slots]).astype(jnp.int32)
    smem = pl.BlockSpec(memory_space=pltpu.SMEM)
    vmem = pl.BlockSpec(memory_space=pltpu.VMEM)
    anywhere = pl.BlockSpec(memory_space=pl.ANY)

    outgoing = pl.pallas_call(
        functools.partial(split_kernel, plan),
        out_shape=jax.ShapeDtypeStruct((peers, row_dev, window), BF16),
        compiler_params=params(),
        name="split_rows",
    )(hidden, row_variant.reshape(1, row_dev), variant_slot.reshape(1, variants))
    x = lax.all_to_all(outgoing, "cols", 0, 0)

    slots, place = pl.pallas_call(
        functools.partial(route_kernel, plan, capacity),
        out_shape=(
            jax.ShapeDtypeStruct((peers, local_slots, window), BF16),
            jax.ShapeDtypeStruct((all_rows, 1), jnp.int32),
        ),
        in_specs=[smem, vmem],
        compiler_params=params(),
        name="route",
    )(scal, x)
    arrived = lax.all_to_all(slots, "cols", 0, 0)

    tile = min(512, width_d)
    base, own = pl.pallas_call(
        functools.partial(base_kernel, plan),
        grid=(width_d // tile,),
        out_shape=(
            jax.ShapeDtypeStruct((all_rows, width_d), F32),
            jax.ShapeDtypeStruct((all_rows, 1), jnp.int32),
        ),
        in_specs=[
            smem,
            pl.BlockSpec((peers, row_dev, window), lambda t: (0, 0, 0)),
            pl.BlockSpec((share, tile), lambda t: (0, t)),
            pl.BlockSpec((peers, row_dev, 1), lambda t: (0, 0, 0)),
        ],
        out_specs=(
            pl.BlockSpec((all_rows, tile), lambda t: (0, t)),
            pl.BlockSpec((all_rows, 1), lambda t: (0, 0)),
        ),
        scratch_shapes=[pltpu.VMEM((all_rows, share), BF16)],
        compiler_params=params(60),
        cost_estimate=pl.CostEstimate(
            flops=2 * all_rows * share * width_d,
            bytes_accessed=2 * share * width_d + 4 * all_rows * width_d,
            transcendentals=0,
        ),
        name="base",
    )(scal, x, down_weight, place.reshape(peers, row_dev, 1))

    group = split_factor(count, 64)
    chunks = local_var * (count // group)
    part = (half, row_dev, width_d // 2)
    joined = pl.pallas_call(
        functools.partial(delta_kernel, plan, d_blocks, group),
        in_specs=[smem, smem, anywhere, anywhere, anywhere, vmem],
        out_specs=[vmem] * 4,
        scratch_shapes=[
            pltpu.VMEM((local_var, f_blocks, capacity, block_size), F32),
            pltpu.VMEM((local_var, d_blocks, capacity, block_size), F32),
            pltpu.VMEM((chunks, group, block_size, block_size), BF16),
            pltpu.VMEM((peers, local_slots, window), BF16),
            pltpu.VMEM((all_rows, width_d), F32),
            pltpu.SemaphoreType.DMA((chunks,)),
            pltpu.SemaphoreType.DMA,
            pltpu.SemaphoreType.DMA,
        ],
        out_shape=[jax.ShapeDtypeStruct(part, F32)] * 2 + [jax.ShapeDtypeStruct(part, BF16)] * 2,
        compiler_params=params(60),
        cost_estimate=pl.CostEstimate(
            flops=2 * local_slots * count * block_size * block_size,
            bytes_accessed=2 * local_var * count * block_size * block_size,
            transcendentals=0,
        ),
        name="delta",
    )(scal, block_ids, arrived, delta_values, base, own)

    above = [1 << k for k in range(1, peers.bit_length() - 1)]
    ends = []
    for side, order in enumerate((above, above[1:] + above[:1])):
        keep, send = joined[side], joined[2 + side]
        open_bits = list(above)
        got = lax.ppermute(send, "cols", [(i, i ^ 1) for i in range(peers)])
        for step in order:
            stride = 1 << open_bits.index(step)
            open_bits.remove(step)
            bit = ((me // step) % 2).astype(jnp.int32).reshape(1)
            left = (keep.shape[0] // 2,) + part[1:]
            keep, send = pl.pallas_call(
                functools.partial(halve_kernel, stride),
                in_specs=[smem, vmem, vmem],
                out_shape=(jax.ShapeDtypeStruct(left, F32), jax.ShapeDtypeStruct(left, BF16)),
                compiler_params=params(),
                name="halve",
            )(bit, keep, got)
            got = lax.ppermute(send, "cols", [(i, i ^ step) for i in range(peers)])
        ends += [keep, got]
    return pl.pallas_call(
        finish_kernel,
        out_shape=jax.ShapeDtypeStruct((row_dev, width_d), BF16),
        compiler_params=params(),
        name="finish",
    )(*ends)


def solution(mesh):
    return jax.shard_map(
        body,
        mesh=mesh,
        in_specs=(
            P(("groups", "cols"), None),
            P("cols", None),
            P("cols", None, None, None),
            P("cols", None),
            P(),
            P(("groups", "cols"), None),
        ),
        out_specs=P(("groups", "cols"), None),
        check_vma=False,
    )
```

time: 109 us -> 107 us (0.982)
  Pallas kernels: 21.1 us -> 31 us
  waiting for transfers between devices: 47.2 us -> 41.9 us
  local copies, waits for them, and re-layouts: 11.7 us -> 6.4 us
  starting transfers between devices: 28.2 us -> 26.5 us
    all_to_all x2 -> x0, waiting for transfers between devices: 13.9 us -> none  [the longest x1 8.43 us: body(): columns = lax.all_to_all(deltas, 'cols', 0, 0)]
    all_to_all x2 -> x0, starting transfers between devices: 9.22 us -> none  [the longest x1 5.7 us: body(): columns = lax.all_to_all(deltas, 'cols', 0, 0)]
    pallas_call x1, Pallas kernels: 9.96 us -> 17.3 us  [body(): pl.pallas_call(functools.partial(delta_kernel, plan, d_blocks, group), in...]
    ppermute x4 -> x6, starting transfers between devices: 7.33 us -> 14.3 us  [body(): got = lax.ppermute(send, 'cols', [(i, i ^ step) for i in range(peers)])]
    ppermute x4 -> x6, waiting for transfers between devices: 6.51 us -> 12.2 us  [body(): got = lax.ppermute(send, 'cols', [(i, i ^ step) for i in range(peers)])]
    unnamed x19 -> x18, local copies, waits for them, and re-layouts: 11.7 us -> 6.4 us
    pallas_call x1, Pallas kernels: 5.11 us -> 9.32 us  [body(): pl.pallas_call(functools.partial(base_kernel, plan), grid=(width_d // til...]
    pallas_call x4 -> x6, Pallas kernels: 2.01 us -> 0.31 us  [body(): pl.pallas_call(functools.partial(halve_kernel, stride), in_specs=[smem, v...]
  transfers between devices with their start and end apart: 8 -> 10, of which waited for: 6 -> 8; matrix products, arithmetic and copies ran while one was open for 0% -> 0% of each run, Pallas kernels for 15% -> 9%
where the time goes in v3:
time: 107 us; the launch traced here: 106 us
  waiting for transfers between devices  41.9 us (39%)
  Pallas kernels  31 us (29%)
  starting transfers between devices  26.5 us (25%)
  local copies, waits for them, and re-layouts  6.4 us (6%)
    pallas_call x1, Pallas kernels, body(): pl.pallas_call(functools.partial(delta_kernel, plan, d_blocks, group), in...  17.3 us
    all_to_all x1, waiting for transfers between devices, body(): x = lax.all_to_all(outgoing, 'cols', 0, 0)  14.4 us
    ppermute x6, starting transfers between devices, body(): got = lax.ppermute(send, 'cols', [(i, i ^ step) for i in range(peers)])  14.3 us
    all_to_all x1, waiting for transfers between devices, body(): arrived = lax.all_to_all(slots, 'cols', 0, 0)  13.6 us
    ppermute x6, waiting for transfers between devices, body(): got = lax.ppermute(send, 'cols', [(i, i ^ step) for i in range(peers)])  12.2 us
    pallas_call x1, Pallas kernels, body(): pl.pallas_call(functools.partial(base_kernel, plan), grid=(width_d // til...  9.32 us
    all_to_all x1, starting transfers between devices, body(): x = lax.all_to_all(outgoing, 'cols', 0, 0)  7.39 us
    unnamed x18, local copies, waits for them, and re-layouts  6.4 us
  transfers between devices with their start and end apart: 10, of which 8 were waited for; matrix products, arithmetic and copies ran while one was open for 0% of the time, Pallas kernels for 9%

profile of v3, /device:TPU:0, one launch (start us, length us, event | category | flops | bytes accessed | tf_op | source)
XLA Modules:
  0.0 106.0 jit_solution(6010830202757574221)
XLA Ops:
  0.0 1.0 copy-done.3
  1.0 0.7 copy-done.6
  1.7 0.7 copy-done.7
  2.3 1.0 split_rows.1
  3.3 7.4 %all-to-all-start = ((bf16[16,16,1024]{2,1,0:T(8,128)(2,1)}), bf16[16,16,1024]{2,1,0:T(8,128)(2,1)S(1)}, u32[]{:S(2)}, u32[]{:S(2)}) async-start(bf16[16,16,1024]{2,1,0:T(8,128)(2,1)} %split_rows.1), calls=%async_computation | async-start | bytes 1048576 | tf_op jit(solution)/shard_map/all_to_all | solution.py:231
  10.8 14.4 %all-to-all-done.x_ref = bf16[16,16,1024]{2,1,0:T(8,128)(2,1)S(1)} async-done(((bf16[16,16,1024]{2,1,0:T(8,128)(2,1)}), bf16[16,16,1024]{2,1,0:T(8,128)(2,1)S(1)}, u32[]{:S(2)}, u32[]{:S(2)}) %all-to-all-start) | async-done | bytes 524320 | tf_op jit(solution)/shard_map/all_to_all | solution.py:231
  25.2 2.4 %route.1 = (bf16[16,32,1024]{2,1,0:T(8,128)(2,1)}, s32[256,1]{1,0:T(8,128)S(1)}) custom-call(s32[3]{0:T(128)S(1)} %pad_add_fusion.shift_ref.scal_ref, bf16[16,16,1024]{2,1,0:T(8,128)(2,1)S(1)} %all-to-all-done.x_ref), custom_call_target="tpu_custom_call" | custom-call | tf_op jit(solution)/shard_map/route/pallas_call | solution.py:233
  27.6 0.7 copy-done.4
  28.2 4.1 %all-to-all-start.1 = ((bf16[16,32,1024]{2,1,0:T(8,128)(2,1)}), bf16[16,32,1024]{2,1,0:T(8,128)(2,1)S(1)}, u32[]{:S(2)}, u32[]{:S(2)}) async-start(bf16[16,32,1024]{2,1,0:T(8,128)(2,1)} %get-tuple-element.25), calls=%async_computation.1 | async-start | bytes 2097152 | tf_op jit(solution)/shard_map/all_to_all | solution.py:243
  32.4 9.3 %base.1 = (f32[256,4096]{1,0:T(8,128)}, s32[256,1]{1,0:T(8,128)}) custom-call(s32[3]{0:T(128)} %copy-done.5, bf16[16,16,1024]{2,1,0:T(8,128)(2,1)} %copy-done, bf16[928,4096]{1,0:T(8,128)(2,1)} %w_ref.1, s32[16,16,1]{2,1,0:T(8,128)} %bitcast.9), custom_call_target="tpu_custom_call" | custom-call | flops 1946157056 | bytes 11796480 | tf_op jit(solution)/shard_map/base/pallas_call | solution.py:246
  41.7 13.6 %all-to-all-done.1.x_hbm = bf16[16,32,1024]{2,1,0:T(8,128)(2,1)S(1)} async-done(((bf16[16,32,1024]{2,1,0:T(8,128)(2,1)}), bf16[16,32,1024]{2,1,0:T(8,128)(2,1)S(1)}, u32[]{:S(2)}, u32[]{:S(2)}) %all-to-all-start.1) | async-done | bytes 1048608 | tf_op jit(solution)/shard_map/all_to_all | solution.py:243
  55.3 1.0 copy-done.8
  56.2 17.3 %delta.1 = (f32[8,16,2048]{2,1,0:T(8,128)}, f32[8,16,2048]{2,1,0:T(8,128)}, bf16[8,16,2048]{2,1,0:T(8,128)(2,1)}, bf16[8,16,2048]{2,1,0:T(8,128)(2,1)}) custom-call(s32[3]{0:T(128)} %copy-done.5, s32[4,186]{1,0:T(4,128)} %ids_ref.1, bf16[16,32,1024]{2,1,0:T(8,128)(2,1)} %copy-done.8, bf16[4,186,128,128]{3,2,1,0:T(8,128)(2,1)} %v_hbm.1, ...), custom_call_target="tpu_custom_call" | custom-call | flops 195035136 | bytes 24379392 | tf_op jit(solution)/shard_map/delta/pallas_call | solution.py:276
  73.5 0.7 collective-permute-start
  74.2 0.1 collective-permute-start.4
  74.3 1.7 %collective-permute-done.got_ref = bf16[8,16,2048]{2,1,0:T(8,128)(2,1)S(1)} collective-permute-done((bf16[8,16,2048]{2,1,0:T(8,128)(2,1)}, bf16[8,16,2048]{2,1,0:T(8,128)(2,1)S(1)}, u32[]{:S(2)}, u32[]{:S(2)}) %collective-permute-start) | collective-permute-done | bytes 524320 | tf_op jit(solution)/shard_map/ppermute | solution.py:305
  75.9 1.2 %copy-done.2 = f32[8,16,2048]{2,1,0:T(8,128)S(1)} copy-done((f32[8,16,2048]{2,1,0:T(8,128)S(1)}, f32[8,16,2048]{2,1,0:T(8,128)}, u32[]{:S(2)}) %copy-start.2) | copy-done | bytes 1048600
  77.2 0.1 halve.6
  77.3 2.1 %collective-permute-start.1 = (bf16[4,16,2048]{2,1,0:T(8,128)(2,1)S(1)}, bf16[4,16,2048]{2,1,0:T(8,128)(2,1)S(1)}, u32[]{:S(2)}, u32[]{:S(2)}) collective-permute-start(bf16[4,16,2048]{2,1,0:T(8,128)(2,1)S(1)} %get-tuple-element.32), channel_id=1, source_target_pairs={{0,2},{1,3},{2,0},{3,1},{4,6},{5,7},{6,4},{7,5},{8,10},{9,11},{10,... | collective-permute-start | bytes 786440 | tf_op jit(solution)/shard_map/ppermute | solution.py:318
  79.3 1.2 %copy-done.1 = f32[8,16,2048]{2,1,0:T(8,128)S(1)} copy-done((f32[8,16,2048]{2,1,0:T(8,128)S(1)}, f32[8,16,2048]{2,1,0:T(8,128)}, u32[]{:S(2)}) %copy-start.1) | copy-done | bytes 1048600
  80.5 0.1 halve.9
  80.6 3.0 %collective-permute-start.5 = (bf16[4,16,2048]{2,1,0:T(8,128)(2,1)S(1)}, bf16[4,16,2048]{2,1,0:T(8,128)(2,1)S(1)}, u32[]{:S(2)}, u32[]{:S(2)}) collective-permute-start(bf16[4,16,2048]{2,1,0:T(8,128)(2,1)S(1)} %get-tuple-element.40), channel_id=1, source_target_pairs={{0,4},{1,5},{2,6},{3,7},{4,0},{5,1},{6,2},{7,3},{8,12},{9,13},{10,... | collective-permute-start | bytes 786440 | tf_op jit(solution)/shard_map/ppermute | solution.py:318
  83.6 2.5 %collective-permute-done.1.got_ref = bf16[4,16,2048]{2,1,0:T(8,128)(2,1)S(1)} collective-permute-done((bf16[4,16,2048]{2,1,0:T(8,128)(2,1)S(1)}, bf16[4,16,2048]{2,1,0:T(8,128)(2,1)S(1)}, u32[]{:S(2)}, u32[]{:S(2)}) %collective-permute-start.1) | collective-permute-done | bytes 262176 | tf_op jit(solution)/shard_map/ppermute | solution.py:318
  86.2 3.2 %collective-permute-start.2 = (bf16[2,16,2048]{2,1,0:T(8,128)(2,1)S(1)}, bf16[2,16,2048]{2,1,0:T(8,128)(2,1)S(1)}, u32[]{:S(2)}, u32[]{:S(2)}) collective-permute-start(bf16[2,16,2048]{2,1,0:T(8,128)(2,1)S(1)} %get-tuple-element.34), channel_id=1, source_target_pairs={{0,4},{1,5},{2,6},{3,7},{4,0},{5,1},{6,2},{7,3},{8,12},{9,13},{10,... | collective-permute-start | bytes 393224 | tf_op jit(solution)/shard_map/ppermute | solution.py:318
  89.4 1.0 collective-permute-done.5.got_ref
  90.4 1.6 %collective-permute-start.6 = (bf16[2,16,2048]{2,1,0:T(8,128)(2,1)S(1)}, bf16[2,16,2048]{2,1,0:T(8,128)(2,1)S(1)}, u32[]{:S(2)}, u32[]{:S(2)}) collective-permute-start(bf16[2,16,2048]{2,1,0:T(8,128)(2,1)S(1)} %get-tuple-element.42), channel_id=1, source_target_pairs={{0,8},{1,9},{2,10},{3,11},{4,12},{5,13},{6,14},{7,15},{8,0},{9,1},... | collective-permute-start | bytes 393224 | tf_op jit(solution)/shard_map/ppermute | solution.py:318
  92.0 1.0 collective-permute-done.2.got_ref
  93.0 3.7 %collective-permute-start.3 = (bf16[1,16,2048]{2,1,0:T(8,128)(2,1)S(1)}, bf16[1,16,2048]{2,1,0:T(8,128)(2,1)S(1)}, u32[]{:S(2)}, u32[]{:S(2)}) collective-permute-start(bf16[1,16,2048]{2,1,0:T(8,128)(2,1)S(1)} %get-tuple-element.36), channel_id=1, source_target_pairs={{0,8},{1,9},{2,10},{3,11},{4,12},{5,13},{6,14},{7,15},{8,0},{9,1},... | collective-permute-start | bytes 196616 | tf_op jit(solution)/shard_map/ppermute | solution.py:318
  96.7 4.3 %collective-permute-done.6.got_ref = bf16[2,16,2048]{2,1,0:T(8,128)(2,1)S(1)} collective-permute-done((bf16[2,16,2048]{2,1,0:T(8,128)(2,1)S(1)}, bf16[2,16,2048]{2,1,0:T(8,128)(2,1)S(1)}, u32[]{:S(2)}, u32[]{:S(2)}) %collective-permute-start.6) | collective-permute-done | bytes 131104 | tf_op jit(solution)/shard_map/ppermute | solution.py:318
  101.0 0.8 collective-permute-start.7
  101.8 3.5 %collective-permute-done.7.refs_3_ = bf16[1,16,2048]{2,1,0:T(8,128)(2,1)S(1)} collective-permute-done((bf16[1,16,2048]{2,1,0:T(8,128)(2,1)S(1)}, bf16[1,16,2048]{2,1,0:T(8,128)(2,1)S(1)}, u32[]{:S(2)}, u32[]{:S(2)}) %collective-permute-start.7) | collective-permute-done | bytes 65568 | tf_op jit(solution)/shard_map/ppermute | solution.py:318
  105.3 0.7 finish.1
  (18 shorter events, 0.2 us)
Async XLA Ops:
  0.0 1.0 copy-start.3
  1.0 0.7 copy-start.6
  1.7 0.7 copy-start.7
  3.3 21.9 %all-to-all-start = ((bf16[16,16,1024]{2,1,0:T(8,128)(2,1)}), bf16[16,16,1024]{2,1,0:T(8,128)(2,1)S(1)}, u32[]{:S(2)}, u32[]{:S(2)}) async-start(bf16[16,16,1024]{2,1,0:T(8,128)(2,1)} %split_rows.1), calls=%async_computation | async-start | bytes 1048576 | tf_op jit(solution)/shard_map/all_to_all | solution.py:231
  10.8 21.5 %copy-start.5 = (s32[3]{0:T(128)}, s32[3]{0:T(128)S(1)}, u32[]{:S(2)}) copy-start(s32[3]{0:T(128)S(1)} %pad_add_fusion.shift_ref.scal_ref) | copy-start | bytes 40
  25.2 7.2 %copy-start = (bf16[16,16,1024]{2,1,0:T(8,128)(2,1)}, bf16[16,16,1024]{2,1,0:T(8,128)(2,1)S(1)}, u32[]{:S(2)}) copy-start(bf16[16,16,1024]{2,1,0:T(8,128)(2,1)S(1)} %all-to-all-done.x_ref) | copy-start | bytes 1572868
  27.6 0.7 copy-start.4
  28.2 27.1 %all-to-all-start.1 = ((bf16[16,32,1024]{2,1,0:T(8,128)(2,1)}), bf16[16,32,1024]{2,1,0:T(8,128)(2,1)S(1)}, u32[]{:S(2)}, u32[]{:S(2)}) async-start(bf16[16,32,1024]{2,1,0:T(8,128)(2,1)} %get-tuple-element.25), calls=%async_computation.1 | async-start | bytes 2097152 | tf_op jit(solution)/shard_map/all_to_all | solution.py:243
  55.3 1.0 copy-start.8
  73.5 2.4 %collective-permute-start = (bf16[8,16,2048]{2,1,0:T(8,128)(2,1)}, bf16[8,16,2048]{2,1,0:T(8,128)(2,1)S(1)}, u32[]{:S(2)}, u32[]{:S(2)}) collective-permute-start(bf16[8,16,2048]{2,1,0:T(8,128)(2,1)} %get-tuple-element.30), channel_id=1, source_target_pairs={{0,1},{1,0},{2,3},{3,2},{4,5},{5,4},{6,7},{7,6},{8,9},{9,8},{10,11... | collective-permute-start | bytes 1572872 | tf_op jit(solution)/shard_map/ppermute | solution.py:305
  74.2 5.1 %collective-permute-start.4 = (bf16[8,16,2048]{2,1,0:T(8,128)(2,1)}, bf16[8,16,2048]{2,1,0:T(8,128)(2,1)S(1)}, u32[]{:S(2)}, u32[]{:S(2)}) collective-permute-start(bf16[8,16,2048]{2,1,0:T(8,128)(2,1)} %get-tuple-element.38), channel_id=1, source_target_pairs={{0,1},{1,0},{2,3},{3,2},{4,5},{5,4},{6,7},{7,6},{8,9},{9,8},{10,11... | collective-permute-start | bytes 1572872 | tf_op jit(solution)/shard_map/ppermute | solution.py:305
  75.9 1.2 %copy-start.2 = (f32[8,16,2048]{2,1,0:T(8,128)S(1)}, f32[8,16,2048]{2,1,0:T(8,128)}, u32[]{:S(2)}) copy-start(f32[8,16,2048]{2,1,0:T(8,128)} %get-tuple-element.29.keep_ref) | copy-start | bytes 3145732
  77.3 8.9 %collective-permute-start.1 = (bf16[4,16,2048]{2,1,0:T(8,128)(2,1)S(1)}, bf16[4,16,2048]{2,1,0:T(8,128)(2,1)S(1)}, u32[]{:S(2)}, u32[]{:S(2)}) collective-permute-start(bf16[4,16,2048]{2,1,0:T(8,128)(2,1)S(1)} %get-tuple-element.32), channel_id=1, source_target_pairs={{0,2},{1,3},{2,0},{3,1},{4,6},{5,7},{6,4},{7,5},{8,10},{9,11},{10,... | collective-permute-start | bytes 786440 | tf_op jit(solution)/shard_map/ppermute | solution.py:318
  79.3 1.2 %copy-start.1 = (f32[8,16,2048]{2,1,0:T(8,128)S(1)}, f32[8,16,2048]{2,1,0:T(8,128)}, u32[]{:S(2)}) copy-start(f32[8,16,2048]{2,1,0:T(8,128)} %get-tuple-element.37.keep_ref) | copy-start | bytes 3145732
  80.6 9.8 %collective-permute-start.5 = (bf16[4,16,2048]{2,1,0:T(8,128)(2,1)S(1)}, bf16[4,16,2048]{2,1,0:T(8,128)(2,1)S(1)}, u32[]{:S(2)}, u32[]{:S(2)}) collective-permute-start(bf16[4,16,2048]{2,1,0:T(8,128)(2,1)S(1)} %get-tuple-element.40), channel_id=1, source_target_pairs={{0,4},{1,5},{2,6},{3,7},{4,0},{5,1},{6,2},{7,3},{8,12},{9,13},{10,... | collective-permute-start | bytes 786440 | tf_op jit(solution)/shard_map/ppermute | solution.py:318
  86.2 6.8 %collective-permute-start.2 = (bf16[2,16,2048]{2,1,0:T(8,128)(2,1)S(1)}, bf16[2,16,2048]{2,1,0:T(8,128)(2,1)S(1)}, u32[]{:S(2)}, u32[]{:S(2)}) collective-permute-start(bf16[2,16,2048]{2,1,0:T(8,128)(2,1)S(1)} %get-tuple-element.34), channel_id=1, source_target_pairs={{0,4},{1,5},{2,6},{3,7},{4,0},{5,1},{6,2},{7,3},{8,12},{9,13},{10,... | collective-permute-start | bytes 393224 | tf_op jit(solution)/shard_map/ppermute | solution.py:318
  90.4 10.5 %collective-permute-start.6 = (bf16[2,16,2048]{2,1,0:T(8,128)(2,1)S(1)}, bf16[2,16,2048]{2,1,0:T(8,128)(2,1)S(1)}, u32[]{:S(2)}, u32[]{:S(2)}) collective-permute-start(bf16[2,16,2048]{2,1,0:T(8,128)(2,1)S(1)} %get-tuple-element.42), channel_id=1, source_target_pairs={{0,8},{1,9},{2,10},{3,11},{4,12},{5,13},{6,14},{7,15},{8,0},{9,1},... | collective-permute-start | bytes 393224 | tf_op jit(solution)/shard_map/ppermute | solution.py:318
  93.0 8.8 %collective-permute-start.3 = (bf16[1,16,2048]{2,1,0:T(8,128)(2,1)S(1)}, bf16[1,16,2048]{2,1,0:T(8,128)(2,1)S(1)}, u32[]{:S(2)}, u32[]{:S(2)}) collective-permute-start(bf16[1,16,2048]{2,1,0:T(8,128)(2,1)S(1)} %get-tuple-element.36), channel_id=1, source_target_pairs={{0,8},{1,9},{2,10},{3,11},{4,12},{5,13},{6,14},{7,15},{8,0},{9,1},... | collective-permute-start | bytes 196616 | tf_op jit(solution)/shard_map/ppermute | solution.py:318
  101.0 4.3 %collective-permute-start.7 = (bf16[1,16,2048]{2,1,0:T(8,128)(2,1)S(1)}, bf16[1,16,2048]{2,1,0:T(8,128)(2,1)S(1)}, u32[]{:S(2)}, u32[]{:S(2)}) collective-permute-start(bf16[1,16,2048]{2,1,0:T(8,128)(2,1)S(1)} %get-tuple-element.44), channel_id=1, source_target_pairs={{0,2},{1,3},{2,0},{3,1},{4,6},{5,7},{6,4},{7,5},{8,10},{9,11},{10,... | collective-permute-start | bytes 196616 | tf_op jit(solution)/shard_map/ppermute | solution.py:318

commit v4 on v2

--- a/solution.py
+++ b/solution.py
@@ -31,18 +31,19 @@
     return lax.broadcasted_iota(jnp.int32, (rows, lanes), 1)
 
 
-def split_kernel(plan, h_ref, id_ref, o_ref):
+def split_kernel(plan, h_ref, id_ref, slot_ref, o_ref):
     share, window, _, starts = plan
     rows = h_ref.shape[0]
+    variants = slot_ref.shape[1]
     lane = lane_iota(rows, window)
-    ids = id_ref[...].astype(F32)
+    diagonal = lax.broadcasted_iota(jnp.int32, (rows, rows), 0) == lane_iota(rows, rows)
+    ids = jnp.sum(jnp.where(diagonal, id_ref[...].astype(F32), 0.0), axis=1, keepdims=True)
+    named = ids.astype(jnp.int32) == lane_iota(rows, variants)
+    slot = jnp.sum(jnp.where(named, slot_ref[...].astype(F32), 0.0), axis=1, keepdims=True)
     for s, b in enumerate(starts):
-        shift = s * share - b * LANES
+        spare = (s * share - b * LANES + share) % window
         piece = h_ref[:, b * LANES : b * LANES + window].astype(F32)
-        keep = (lane >= shift) & (lane < shift + share)
-        spare = (shift + share) % window
-        piece = jnp.where(keep, piece, jnp.where(lane == spare, ids, 0.0))
-        o_ref[s] = piece.astype(BF16)
+        o_ref[s] = jnp.where(lane == spare, slot, piece).astype(BF16)
 
 
 def own_shift(plan):
@@ -51,27 +52,25 @@
     return start - jnp.minimum(start // LANES, last) * LANES
 
 
-def route_kernel(plan, capacity, shift_ref, x_ref, slot_ref, o_ref, place_ref):
+def route_kernel(plan, capacity, shift_ref, x_ref, o_ref, place_ref):
     share, window, _, _ = plan
     peers, row_dev, _ = x_ref.shape
     rows = peers * row_dev
-    variants = slot_ref.shape[1]
-    slots = variants * capacity
+    slots = o_ref.shape[0] * o_ref.shape[1]
+    variants = slots // capacity
     shift = shift_ref[0]
     x = x_ref[...].reshape(rows, window).astype(F32)
     lane = lane_iota(rows, window)
     spare = lax.rem(shift + share, window)
-    ids = jnp.sum(jnp.where(lane == spare, x, 0.0), axis=1, keepdims=True)
+    slot = jnp.sum(jnp.where(lane == spare, x, 0.0), axis=1, keepdims=True)
     data = jnp.where((lane >= shift) & (lane < shift + share), x, 0.0).astype(BF16)
-    onehot = ids.astype(jnp.int32) == lane_iota(rows, variants)
-    onehot_f = jnp.where(onehot, 1.0, 0.0)
+    onehot = jnp.where(slot.astype(jnp.int32) == lane_iota(rows, variants), 1.0, 0.0)
     row_i = lax.broadcasted_iota(jnp.int32, (rows, rows), 0)
     row_j = lane_iota(rows, rows)
     earlier = jnp.where(row_j < row_i, 1.0, 0.0).astype(BF16)
-    before = jnp.dot(earlier, onehot_f.astype(BF16), preferred_element_type=F32)
-    rank = jnp.sum(before * onehot_f, axis=1, keepdims=True)
-    slot_of = jnp.sum(onehot_f * slot_ref[...].astype(F32), axis=1, keepdims=True)
-    place = slot_of * capacity + rank
+    before = jnp.dot(earlier, onehot.astype(BF16), preferred_element_type=F32)
+    rank = jnp.sum(before * onehot, axis=1, keepdims=True)
+    place = slot * capacity + rank
     place_ref[...] = place.astype(jnp.int32)
     across = jnp.sum(jnp.where(row_i == row_j, place, 0.0), axis=0, keepdims=True)
     pick = across.astype(jnp.int32) == lax.broadcasted_iota(jnp.int32, (slots, rows), 0)
@@ -225,7 +224,7 @@
         out_shape=jax.ShapeDtypeStruct((peers, row_dev, window), BF16),
         compiler_params=params(),
         name="split_rows",
-    )(hidden, row_variant)
+    )(hidden, row_variant.reshape(1, row_dev), variant_slot.reshape(1, variants))
     x = lax.all_to_all(outgoing, "cols", 0, 0)
 
     slots, place = pl.pallas_call(
@@ -234,10 +233,10 @@
             jax.ShapeDtypeStruct((peers, local_slots, window), BF16),
             jax.ShapeDtypeStruct((all_rows, 1), jnp.int32),
         ),
-        in_specs=[smem, vmem, vmem],
+        in_specs=[smem, vmem],
         compiler_params=params(),
         name="route",
-    )(scal, x, variant_slot.reshape(1, variants))
+    )(scal, x)
     arrived = lax.all_to_all(slots, "cols", 0, 0)
     x, place = lax.optimization_barrier((x, place))
 
@@ -267,7 +266,6 @@
         ),
         name="base",
     )(scal, x, down_weight)
-    send, arrived = lax.optimization_barrier((send, arrived))
     step = 1
     while True:
         got = lax.ppermute(send, "cols", [(i, i ^ step) for i in range(peers)])
@@ -283,6 +281,8 @@
             compiler_params=params(),
             name="halve",
         )(bit, keep, got)
+        if step == 2:
+            send, arrived = lax.optimization_barrier((send, arrived))
 
     group = split_factor(count, 64)
     aligned = slice_d % LANES == 0

time: 109 us -> 101 us (0.927)
  waiting for transfers between devices: 47.2 us -> 39.5 us
  local copies, waits for them, and re-layouts: 11.7 us -> 10.6 us
    all_to_all x1, waiting for transfers between devices: 12.4 us -> 4.68 us  [body(): arrived = lax.all_to_all(slots, 'cols', 0, 0)]
    unnamed x19 -> x18, local copies, waits for them, and re-layouts: 11.7 us -> 10.6 us
  transfers between devices with their start and end apart: 8 -> 8, of which waited for: 6 -> 6; matrix products, arithmetic and copies ran while one was open for 0% -> 0% of each run, Pallas kernels for 15% -> 18%
where the time goes in v4:
time: 101 us
  waiting for transfers between devices  39.5 us (39%)
  starting transfers between devices  28.2 us (28%)
  Pallas kernels  22.1 us (22%)
  local copies, waits for them, and re-layouts  10.6 us (10%)
    all_to_all x1, waiting for transfers between devices, body(): x = lax.all_to_all(outgoing, 'cols', 0, 0)  14.4 us
    unnamed x18, local copies, waits for them, and re-layouts  10.6 us
    pallas_call x1, Pallas kernels, body(): pl.pallas_call(functools.partial(delta_kernel, plan, d_blocks, group), in...  9.96 us
    all_to_all x1, waiting for transfers between devices, body(): columns = lax.all_to_all(deltas, 'cols', 0, 0)  8.43 us
    all_to_all x1, starting transfers between devices, body(): x = lax.all_to_all(outgoing, 'cols', 0, 0)  7.52 us
    ppermute x4, starting transfers between devices, body(): got = lax.ppermute(send, 'cols', [(i, i ^ step) for i in range(peers)])  6.96 us
    ppermute x4, waiting for transfers between devices, body(): got = lax.ppermute(send, 'cols', [(i, i ^ step) for i in range(peers)])  6.51 us
    all_to_all x1, starting transfers between devices, body(): columns = lax.all_to_all(deltas, 'cols', 0, 0)  6.11 us
  transfers between devices with their start and end apart: 8, of which 6 were waited for; matrix products, arithmetic and copies ran while one was open for 0% of the time, Pallas kernels for 18%

profile of v4, /device:TPU:0, one launch (start us, length us, event | category | flops | bytes accessed | tf_op | source)
XLA Modules:
  0.0 100.7 jit_solution(4808189235327030955)
XLA Ops:
  0.0 1.0 %copy-done.5 = bf16[16,14848]{1,0:T(8,128)(2,1)S(1)} copy-done((bf16[16,14848]{1,0:T(8,128)(2,1)S(1)}, bf16[16,14848]{1,0:T(8,128)(2,1)}, u32[]{:S(2)}) %copy-start.5) | copy-done | bytes 475160
  1.0 0.7 copy-done.7
  1.7 0.7 copy-done.8
  2.3 1.0 split_rows.1
  3.3 7.5 %all-to-all-start = ((bf16[16,16,1024]{2,1,0:T(8,128)(2,1)}), bf16[16,16,1024]{2,1,0:T(8,128)(2,1)S(1)}, u32[]{:S(2)}, u32[]{:S(2)}) async-start(bf16[16,16,1024]{2,1,0:T(8,128)(2,1)} %split_rows.1), calls=%async_computation | async-start | bytes 1048576 | tf_op jit(solution)/shard_map/all_to_all | solution.py:228
  10.9 0.1 pad_add_fusion.shift_ref.scal_ref
  10.9 14.4 %all-to-all-done.x_ref = bf16[16,16,1024]{2,1,0:T(8,128)(2,1)S(1)} async-done(((bf16[16,16,1024]{2,1,0:T(8,128)(2,1)}), bf16[16,16,1024]{2,1,0:T(8,128)(2,1)S(1)}, u32[]{:S(2)}, u32[]{:S(2)}) %all-to-all-start) | async-done | bytes 524320 | tf_op jit(solution)/shard_map/all_to_all | solution.py:228
  25.3 2.4 %route.1 = (bf16[16,32,1024]{2,1,0:T(8,128)(2,1)}, s32[256,1]{1,0:T(8,128)S(1)}) custom-call(s32[2]{0:T(128)S(1)} %pad_add_fusion.shift_ref.scal_ref, bf16[16,16,1024]{2,1,0:T(8,128)(2,1)S(1)} %all-to-all-done.x_ref), custom_call_target="tpu_custom_call" | custom-call | tf_op jit(solution)/shard_map/route/pallas_call | solution.py:230
  27.7 4.1 %all-to-all-start.1 = ((bf16[16,32,1024]{2,1,0:T(8,128)(2,1)}), bf16[16,32,1024]{2,1,0:T(8,128)(2,1)S(1)}, u32[]{:S(2)}, u32[]{:S(2)}) async-start(bf16[16,32,1024]{2,1,0:T(8,128)(2,1)} %get-tuple-element.25), calls=%async_computation.1 | async-start | bytes 2097152 | tf_op jit(solution)/shard_map/all_to_all | solution.py:240
  31.8 0.0 copy-start
  31.8 3.1 %copy-done = bf16[928,4096]{1,0:T(8,128)(2,1)S(1)} copy-done((bf16[928,4096]{1,0:T(8,128)(2,1)S(1)}, bf16[928,4096]{1,0:T(8,128)(2,1)}, u32[]{:S(2)}) %copy-start) | copy-done | bytes 7602200
  34.9 6.0 %base.1 = (f32[8,16,4096]{2,1,0:T(8,128)S(1)}, bf16[8,16,4096]{2,1,0:T(8,128)(2,1)}) custom-call(s32[2]{0:T(128)S(1)} %pad_add_fusion.shift_ref.scal_ref, bf16[16,16,1024]{2,1,0:T(8,128)(2,1)S(1)} %all-to-all-done.x_ref, bf16[928,4096]{1,0:T(8,128)(2,1)S(1)} %copy-done), custom_call_target="tpu_custom_call" | custom-call | flops 1946157056 | bytes 10747904 | tf_op jit(solution)/shard_map/base/pallas_call | solution.py:244
  41.0 1.3 %copy-done.1 = f32[8,16,4096]{2,1,0:T(8,128)} copy-done((f32[8,16,4096]{2,1,0:T(8,128)}, f32[8,16,4096]{2,1,0:T(8,128)S(1)}, u32[]{:S(2)}) %copy-start.1) | copy-done | bytes 2097176
  42.3 0.4 collective-permute-start
  42.7 2.5 %collective-permute-done.got_ref = bf16[8,16,4096]{2,1,0:T(8,128)(2,1)S(1)} collective-permute-done((bf16[8,16,4096]{2,1,0:T(8,128)(2,1)}, bf16[8,16,4096]{2,1,0:T(8,128)(2,1)S(1)}, u32[]{:S(2)}, u32[]{:S(2)}) %collective-permute-start) | collective-permute-done | bytes 1048608 | tf_op jit(solution)/shard_map/ppermute | solution.py:271
  45.2 1.0 copy-done.3
  46.2 1.6 %copy-done.2 = f32[8,16,4096]{2,1,0:T(8,128)S(1)} copy-done((f32[8,16,4096]{2,1,0:T(8,128)S(1)}, f32[8,16,4096]{2,1,0:T(8,128)}, u32[]{:S(2)}) %copy-start.2) | copy-done | bytes 2097176
  47.8 1.2 %copy-done.4 = bf16[8,16,4096]{2,1,0:T(8,128)(2,1)S(1)} copy-done((bf16[8,16,4096]{2,1,0:T(8,128)(2,1)S(1)}, bf16[8,16,4096]{2,1,0:T(8,128)(2,1)}, u32[]{:S(2)}) %copy-start.4) | copy-done | bytes 1048600
  49.0 1.0 %halve.3 = (f32[4,16,4096]{2,1,0:T(8,128)S(1)}, bf16[4,16,4096]{2,1,0:T(8,128)(2,1)}) custom-call(s32[1]{0:T(128)} %bitcast.2.bit_ref, f32[8,16,4096]{2,1,0:T(8,128)S(1)} %copy-done.2, bf16[8,16,4096]{2,1,0:T(8,128)(2,1)S(1)} %copy-done.4), custom_call_target="tpu_custom_call" | custom-call | tf_op jit(solution)/shard_map/halve/pallas_call | solution.py:277
  50.0 4.7 %all-to-all-done.1.x_ref = bf16[16,32,1024]{2,1,0:T(8,128)(2,1)S(1)} async-done(((bf16[16,32,1024]{2,1,0:T(8,128)(2,1)}), bf16[16,32,1024]{2,1,0:T(8,128)(2,1)S(1)}, u32[]{:S(2)}, u32[]{:S(2)}) %all-to-all-start.1) | async-done | bytes 1048608 | tf_op jit(solution)/shard_map/all_to_all | solution.py:240
  54.7 1.8 %collective-permute-start.1 = (bf16[4,16,4096]{2,1,0:T(8,128)(2,1)}, bf16[4,16,4096]{2,1,0:T(8,128)(2,1)S(1)}, u32[]{:S(2)}, u32[]{:S(2)}) collective-permute-start(bf16[4,16,4096]{2,1,0:T(8,128)(2,1)} %get-tuple-element.26), channel_id=1, source_target_pairs={{0,2},{1,3},{2,0},{3,1},{4,6},{5,7},{6,4},{7,5},{8,10},{9,11},{10,... | collective-permute-start | bytes 1572872 | tf_op jit(solution)/shard_map/ppermute | solution.py:271
  56.5 10.0 %delta.1 = bf16[16,32,256]{2,1,0:T(8,128)(2,1)} custom-call(s32[4,186]{1,0:T(4,128)S(1)} %copy-done.6, bf16[16,32,1024]{2,1,0:T(8,128)(2,1)S(1)} %all-to-all-done.1.x_ref, bf16[4,186,128,128]{3,2,1,0:T(8,128)(2,1)} %v_hbm.1), custom_call_target="tpu_custom_call" | custom-call | flops 195035136 | bytes 24379392 | tf_op jit(solution)/shard_map/delta/pallas_call | solution.py:291
  66.5 6.1 %all-to-all-start.2 = ((bf16[16,32,256]{2,1,0:T(8,128)(2,1)}), bf16[16,32,256]{2,1,0:T(8,128)(2,1)S(1)}, u32[]{:S(2)}, u32[]{:S(2)}) async-start(bf16[16,32,256]{2,1,0:T(8,128)(2,1)} %delta.1), calls=%async_computation.2 | async-start | bytes 524288 | tf_op jit(solution)/shard_map/all_to_all | solution.py:312
  72.7 0.1 halve.4
  72.8 2.0 %collective-permute-start.2 = (bf16[2,16,4096]{2,1,0:T(8,128)(2,1)S(1)}, bf16[2,16,4096]{2,1,0:T(8,128)(2,1)S(1)}, u32[]{:S(2)}, u32[]{:S(2)}) collective-permute-start(bf16[2,16,4096]{2,1,0:T(8,128)(2,1)S(1)} %get-tuple-element.28), channel_id=1, source_target_pairs={{0,4},{1,5},{2,6},{3,7},{4,0},{5,1},{6,2},{7,3},{8,12},{9,13},{10,... | collective-permute-start | bytes 786440 | tf_op jit(solution)/shard_map/ppermute | solution.py:271
  74.7 8.4 %all-to-all-done.2.c_ref = bf16[16,32,256]{2,1,0:T(8,128)(2,1)S(1)} async-done(((bf16[16,32,256]{2,1,0:T(8,128)(2,1)}), bf16[16,32,256]{2,1,0:T(8,128)(2,1)S(1)}, u32[]{:S(2)}, u32[]{:S(2)}) %all-to-all-start.2) | async-done | bytes 262176 | tf_op jit(solution)/shard_map/all_to_all | solution.py:312
  83.1 0.9 pick.1
  84.1 3.5 %all-to-all-start.3 = ((bf16[16,16,256]{2,1,0:T(8,128)(2,1)}), bf16[16,16,256]{2,1,0:T(8,128)(2,1)S(1)}, u32[]{:S(2)}, u32[]{:S(2)}) async-start(bf16[16,16,256]{2,1,0:T(8,128)(2,1)} %pick.1), calls=%async_computation.3 | async-start | bytes 262144 | tf_op jit(solution)/shard_map/all_to_all | solution.py:319
  87.7 2.8 %collective-permute-start.3 = (bf16[1,16,4096]{2,1,0:T(8,128)(2,1)S(1)}, bf16[1,16,4096]{2,1,0:T(8,128)(2,1)S(1)}, u32[]{:S(2)}, u32[]{:S(2)}) collective-permute-start(bf16[1,16,4096]{2,1,0:T(8,128)(2,1)S(1)} %get-tuple-element.30), channel_id=1, source_target_pairs={{0,8},{1,9},{2,10},{3,11},{4,12},{5,13},{6,14},{7,15},{8,0},{9,1},... | collective-permute-start | bytes 393224 | tf_op jit(solution)/shard_map/ppermute | solution.py:271
  90.5 5.5 %all-to-all-done.3.own_ref = bf16[16,16,256]{2,1,0:T(8,128)(2,1)S(1)} async-done(((bf16[16,16,256]{2,1,0:T(8,128)(2,1)}), bf16[16,16,256]{2,1,0:T(8,128)(2,1)S(1)}, u32[]{:S(2)}, u32[]{:S(2)}) %all-to-all-start.3) | async-done | bytes 131104 | tf_op jit(solution)/shard_map/all_to_all | solution.py:319
  96.0 4.0 %collective-permute-done.3.got_ref = bf16[1,16,4096]{2,1,0:T(8,128)(2,1)S(1)} collective-permute-done((bf16[1,16,4096]{2,1,0:T(8,128)(2,1)S(1)}, bf16[1,16,4096]{2,1,0:T(8,128)(2,1)S(1)}, u32[]{:S(2)}, u32[]{:S(2)}) %collective-permute-start.3) | collective-permute-done | bytes 131104 | tf_op jit(solution)/shard_map/ppermute | solution.py:271
  100.0 0.7 finish.1
  (12 shorter events, 0.1 us)
Async XLA Ops:
  0.0 1.0 %copy-start.5 = (bf16[16,14848]{1,0:T(8,128)(2,1)S(1)}, bf16[16,14848]{1,0:T(8,128)(2,1)}, u32[]{:S(2)}) copy-start(bf16[16,14848]{1,0:T(8,128)(2,1)} %h_ref.1) | copy-start | bytes 1425412
  1.0 0.7 copy-start.7
  1.7 0.7 copy-start.8
  3.3 53.2 %copy-start.6 = (s32[4,186]{1,0:T(4,128)S(1)}, s32[4,186]{1,0:T(4,128)}, u32[]{:S(2)}) copy-start(s32[4,186]{1,0:T(4,128)} %ids_ref.1) | copy-start | bytes 8932
  3.3 22.0 %all-to-all-start = ((bf16[16,16,1024]{2,1,0:T(8,128)(2,1)}), bf16[16,16,1024]{2,1,0:T(8,128)(2,1)S(1)}, u32[]{:S(2)}, u32[]{:S(2)}) async-start(bf16[16,16,1024]{2,1,0:T(8,128)(2,1)} %split_rows.1), calls=%async_computation | async-start | bytes 1048576 | tf_op jit(solution)/shard_map/all_to_all | solution.py:228
  27.7 27.0 %all-to-all-start.1 = ((bf16[16,32,1024]{2,1,0:T(8,128)(2,1)}), bf16[16,32,1024]{2,1,0:T(8,128)(2,1)S(1)}, u32[]{:S(2)}, u32[]{:S(2)}) async-start(bf16[16,32,1024]{2,1,0:T(8,128)(2,1)} %get-tuple-element.25), calls=%async_computation.1 | async-start | bytes 2097152 | tf_op jit(solution)/shard_map/all_to_all | solution.py:240
  31.8 3.2 %copy-start = (bf16[928,4096]{1,0:T(8,128)(2,1)S(1)}, bf16[928,4096]{1,0:T(8,128)(2,1)}, u32[]{:S(2)}) copy-start(bf16[928,4096]{1,0:T(8,128)(2,1)} %w_ref.1) | copy-start | bytes 22806532
  41.0 1.3 %copy-start.1 = (f32[8,16,4096]{2,1,0:T(8,128)}, f32[8,16,4096]{2,1,0:T(8,128)S(1)}, u32[]{:S(2)}) copy-start(f32[8,16,4096]{2,1,0:T(8,128)S(1)} %get-tuple-element.21.keep_ref) | copy-start | bytes 6291460
  42.3 2.9 %collective-permute-start = (bf16[8,16,4096]{2,1,0:T(8,128)(2,1)}, bf16[8,16,4096]{2,1,0:T(8,128)(2,1)S(1)}, u32[]{:S(2)}, u32[]{:S(2)}) collective-permute-start(bf16[8,16,4096]{2,1,0:T(8,128)(2,1)} %get-tuple-element.22), channel_id=1, source_target_pairs={{0,1},{1,0},{2,3},{3,2},{4,5},{5,4},{6,7},{7,6},{8,9},{9,8},{10,11... | collective-permute-start | bytes 3145736 | tf_op jit(solution)/shard_map/ppermute | solution.py:271
  45.2 1.0 copy-start.3
  46.2 1.6 %copy-start.2 = (f32[8,16,4096]{2,1,0:T(8,128)S(1)}, f32[8,16,4096]{2,1,0:T(8,128)}, u32[]{:S(2)}) copy-start(f32[8,16,4096]{2,1,0:T(8,128)} %copy-done.1) | copy-start | bytes 6291460
  47.8 1.2 %copy-start.4 = (bf16[8,16,4096]{2,1,0:T(8,128)(2,1)S(1)}, bf16[8,16,4096]{2,1,0:T(8,128)(2,1)}, u32[]{:S(2)}) copy-start(bf16[8,16,4096]{2,1,0:T(8,128)(2,1)} %copy-done.3) | copy-start | bytes 3145732
  54.7 17.9 %collective-permute-start.1 = (bf16[4,16,4096]{2,1,0:T(8,128)(2,1)}, bf16[4,16,4096]{2,1,0:T(8,128)(2,1)S(1)}, u32[]{:S(2)}, u32[]{:S(2)}) collective-permute-start(bf16[4,16,4096]{2,1,0:T(8,128)(2,1)} %get-tuple-element.26), channel_id=1, source_target_pairs={{0,2},{1,3},{2,0},{3,1},{4,6},{5,7},{6,4},{7,5},{8,10},{9,11},{10,... | collective-permute-start | bytes 1572872 | tf_op jit(solution)/shard_map/ppermute | solution.py:271
  66.5 16.6 %all-to-all-start.2 = ((bf16[16,32,256]{2,1,0:T(8,128)(2,1)}), bf16[16,32,256]{2,1,0:T(8,128)(2,1)S(1)}, u32[]{:S(2)}, u32[]{:S(2)}) async-start(bf16[16,32,256]{2,1,0:T(8,128)(2,1)} %delta.1), calls=%async_computation.2 | async-start | bytes 524288 | tf_op jit(solution)/shard_map/all_to_all | solution.py:312
  72.8 14.9 %collective-permute-start.2 = (bf16[2,16,4096]{2,1,0:T(8,128)(2,1)S(1)}, bf16[2,16,4096]{2,1,0:T(8,128)(2,1)S(1)}, u32[]{:S(2)}, u32[]{:S(2)}) collective-permute-start(bf16[2,16,4096]{2,1,0:T(8,128)(2,1)S(1)} %get-tuple-element.28), channel_id=1, source_target_pairs={{0,4},{1,5},{2,6},{3,7},{4,0},{5,1},{6,2},{7,3},{8,12},{9,13},{10,... | collective-permute-start | bytes 786440 | tf_op jit(solution)/shard_map/ppermute | solution.py:271
  84.1 11.9 %all-to-all-start.3 = ((bf16[16,16,256]{2,1,0:T(8,128)(2,1)}), bf16[16,16,256]{2,1,0:T(8,128)(2,1)S(1)}, u32[]{:S(2)}, u32[]{:S(2)}) async-start(bf16[16,16,256]{2,1,0:T(8,128)(2,1)} %pick.1), calls=%async_computation.3 | async-start | bytes 262144 | tf_op jit(solution)/shard_map/all_to_all | solution.py:319
  87.7 12.3 %collective-permute-start.3 = (bf16[1,16,4096]{2,1,0:T(8,128)(2,1)S(1)}, bf16[1,16,4096]{2,1,0:T(8,128)(2,1)S(1)}, u32[]{:S(2)}, u32[]{:S(2)}) collective-permute-start(bf16[1,16,4096]{2,1,0:T(8,128)(2,1)S(1)} %get-tuple-element.30), channel_id=1, source_target_pairs={{0,8},{1,9},{2,10},{3,11},{4,12},{5,13},{6,14},{7,15},{8,0},{9,1},... | collective-permute-start | bytes 393224 | tf_op jit(solution)/shard_map/ppermute | solution.py:271

commit v5 on v4

--- a/solution.py
+++ b/solution.py
@@ -31,16 +31,33 @@
     return lax.broadcasted_iota(jnp.int32, (rows, lanes), 1)
 
 
-def split_kernel(plan, h_ref, id_ref, slot_ref, o_ref):
+def split_kernel(plan, h_hbm, id_hbm, slot_hbm, o_ref, h_ref, id_ref, slot_ref, sems):
     share, window, _, starts = plan
-    rows = h_ref.shape[0]
+    rows, width = h_ref.shape
     variants = slot_ref.shape[1]
+    cut = width // LANES // 2 * LANES
+    halves = (slice(0, cut), slice(cut, width))
+    copies = [
+        pltpu.make_async_copy(id_hbm, id_ref, sems.at[0]),
+        pltpu.make_async_copy(slot_hbm, slot_ref, sems.at[1]),
+        pltpu.make_async_copy(h_hbm.at[:, halves[0]], h_ref.at[:, halves[0]], sems.at[2]),
+        pltpu.make_async_copy(h_hbm.at[:, halves[1]], h_ref.at[:, halves[1]], sems.at[3]),
+    ]
+    for copy in copies:
+        copy.start()
+    copies[0].wait()
+    copies[1].wait()
     lane = lane_iota(rows, window)
     diagonal = lax.broadcasted_iota(jnp.int32, (rows, rows), 0) == lane_iota(rows, rows)
     ids = jnp.sum(jnp.where(diagonal, id_ref[...].astype(F32), 0.0), axis=1, keepdims=True)
     named = ids.astype(jnp.int32) == lane_iota(rows, variants)
     slot = jnp.sum(jnp.where(named, slot_ref[...].astype(F32), 0.0), axis=1, keepdims=True)
+    copies[2].wait()
+    late = True
     for s, b in enumerate(starts):
+        if late and b * LANES + window > cut:
+            copies[3].wait()
+            late = False
         spare = (s * share - b * LANES + share) % window
         piece = h_ref[:, b * LANES : b * LANES + window].astype(F32)
         o_ref[s] = jnp.where(lane == spare, slot, piece).astype(BF16)
@@ -218,11 +235,19 @@
     scal = jnp.stack([own_shift(plan), me % 2]).astype(jnp.int32)
     smem = pl.BlockSpec(memory_space=pltpu.SMEM)
     vmem = pl.BlockSpec(memory_space=pltpu.VMEM)
+    anywhere = pl.BlockSpec(memory_space=pl.ANY)
 
     outgoing = pl.pallas_call(
         functools.partial(split_kernel, plan),
+        in_specs=[anywhere] * 3,
         out_shape=jax.ShapeDtypeStruct((peers, row_dev, window), BF16),
-        compiler_params=params(),
+        scratch_shapes=[
+            pltpu.VMEM((row_dev, width_f), BF16),
+            pltpu.VMEM((1, row_dev), jnp.int32),
+            pltpu.VMEM((1, variants), jnp.int32),
+            pltpu.SemaphoreType.DMA((4,)),
+        ],
+        compiler_params=params(60),
         name="split_rows",
     )(hidden, row_variant.reshape(1, row_dev), variant_slot.reshape(1, variants))
     x = lax.all_to_all(outgoing, "cols", 0, 0)
@@ -266,23 +291,24 @@
         ),
         name="base",
     )(scal, x, down_weight)
-    step = 1
-    while True:
-        got = lax.ppermute(send, "cols", [(i, i ^ step) for i in range(peers)])
-        step *= 2
-        if step == peers:
-            break
+    pairs = lambda step: [(i, i ^ step) for i in range(peers)]
+
+    def halve(step, keep, got):
         bit = ((me // step) % 2).astype(jnp.int32).reshape(1)
         left = (keep.shape[0] // 2, row_dev, width_d)
-        keep, send = pl.pallas_call(
+        return pl.pallas_call(
             halve_kernel,
             in_specs=[smem, vmem, vmem],
             out_shape=(jax.ShapeDtypeStruct(left, F32), jax.ShapeDtypeStruct(left, BF16)),
             compiler_params=params(),
             name="halve",
         )(bit, keep, got)
-        if step == 2:
-            send, arrived = lax.optimization_barrier((send, arrived))
+
+    got = lax.ppermute(send, "cols", pairs(1))
+    step = 2
+    if step < peers:
+        keep, send = halve(step, keep, got)
+        send, arrived = lax.optimization_barrier((send, arrived))
 
     group = split_factor(count, 64)
     aligned = slice_d % LANES == 0
@@ -290,7 +316,7 @@
     chunks = local_var * (count // group)
     deltas = pl.pallas_call(
         functools.partial(delta_kernel, plan, d_blocks, group),
-        in_specs=[smem, vmem, pl.BlockSpec(memory_space=pl.ANY)],
+        in_specs=[smem, vmem, anywhere],
         out_specs=vmem,
         scratch_shapes=[
             pltpu.VMEM((local_var, f_blocks, capacity, block_size), F32),
@@ -310,6 +336,13 @@
     if not aligned:
         deltas = deltas.reshape(local_slots, peers, slice_d).transpose(1, 0, 2)
     columns = lax.all_to_all(deltas, "cols", 0, 0)
+    while step < peers:
+        got = lax.ppermute(send, "cols", pairs(step))
+        step *= 2
+        if step < peers:
+            keep, send = halve(step, keep, got)
+        if step == peers // 2:
+            send, place = lax.optimization_barrier((send, place))
     by_row = pl.pallas_call(
         pick_kernel,
         out_shape=jax.ShapeDtypeStruct((peers, row_dev, slice_d), BF16),

time: 101 us -> 104 us (1.030)
  waiting for transfers between devices: 39.5 us -> 42.1 us
  local copies, waits for them, and re-layouts: 10.6 us -> 8.27 us
    ppermute x4, waiting for transfers between devices: 6.51 us -> 23 us  [the longest x3 20.5 us: body(): got = lax.ppermute(send, 'cols', pairs(step))]
    all_to_all x1, waiting for transfers between devices: 8.43 us -> 0.01 us  [body(): columns = lax.all_to_all(deltas, 'cols', 0, 0)]
    all_to_all x1, waiting for transfers between devices: 5.49 us -> 0.01 us  [body(): own = lax.all_to_all(by_row, 'cols', 0, 0)]
    unnamed x18 -> x12, local copies, waits for them, and re-layouts: 10.6 us -> 8.27 us
    all_to_all x1, starting transfers between devices: 3.51 us -> 4.65 us  [body(): own = lax.all_to_all(by_row, 'cols', 0, 0)]
  transfers between devices with their start and end apart: 8 -> 8, of which waited for: 6 -> 5; matrix products, arithmetic and copies ran while one was open for 0% -> 0% of each run, Pallas kernels for 18% -> 17%
where the time goes in v5:
time: 104 us; the launch traced here: 103 us
  waiting for transfers between devices  42.1 us (40%)
  starting transfers between devices  29.2 us (28%)
  Pallas kernels  23.1 us (22%)
  local copies, waits for them, and re-layouts  8.27 us (8%)
    ppermute x3, waiting for transfers between devices, body(): got = lax.ppermute(send, 'cols', pairs(step))  20.5 us
    all_to_all x1, waiting for transfers between devices, body(): x = lax.all_to_all(outgoing, 'cols', 0, 0)  14.4 us
    pallas_call x1, Pallas kernels, body(): pl.pallas_call(functools.partial(delta_kernel, plan, d_blocks, group), in...  9.97 us
    unnamed x12, local copies, waits for them, and re-layouts  8.27 us
    all_to_all x1, starting transfers between devices, body(): x = lax.all_to_all(outgoing, 'cols', 0, 0)  7.4 us
    ppermute x3, starting transfers between devices, body(): got = lax.ppermute(send, 'cols', pairs(step))  6.59 us
    all_to_all x1, starting transfers between devices, body(): columns = lax.all_to_all(deltas, 'cols', 0, 0)  6.11 us
    pallas_call x1, Pallas kernels, body(): pl.pallas_call(functools.partial(base_kernel, plan), grid=(width_d // til...  6.07 us
  transfers between devices with their start and end apart: 8, of which 5 were waited for; matrix products, arithmetic and copies ran while one was open for 0% of the time, Pallas kernels for 17%

profile of v5, /device:TPU:0, one launch (start us, length us, event | category | flops | bytes accessed | tf_op | source)
XLA Modules:
  0.0 102.9 jit_solution(9592133126999132304)
XLA Ops:
  0.0 1.9 %split_rows.1 = bf16[16,16,1024]{2,1,0:T(8,128)(2,1)} custom-call(bf16[16,14848]{1,0:T(8,128)(2,1)} %h_hbm.1, s32[1,16]{1,0:T(1,128)} %bitcast.7, s32[1,64]{1,0:T(1,128)} %bitcast.8), custom_call_target="tpu_custom_call" | custom-call | tf_op jit(solution)/shard_map/split_rows/pallas_call | solution.py:240
  2.0 0.0 copy-start.5
  2.0 7.4 %all-to-all-start = ((bf16[16,16,1024]{2,1,0:T(8,128)(2,1)}), bf16[16,16,1024]{2,1,0:T(8,128)(2,1)S(1)}, u32[]{:S(2)}, u32[]{:S(2)}) async-start(bf16[16,16,1024]{2,1,0:T(8,128)(2,1)} %split_rows.1), calls=%async_computation | async-start | bytes 1048576 | tf_op jit(solution)/shard_map/all_to_all | solution.py:253
  9.4 0.1 pad_add_fusion.shift_ref.scal_ref
  9.5 14.4 %all-to-all-done.x_ref = bf16[16,16,1024]{2,1,0:T(8,128)(2,1)S(1)} async-done(((bf16[16,16,1024]{2,1,0:T(8,128)(2,1)}), bf16[16,16,1024]{2,1,0:T(8,128)(2,1)S(1)}, u32[]{:S(2)}, u32[]{:S(2)}) %all-to-all-start) | async-done | bytes 524320 | tf_op jit(solution)/shard_map/all_to_all | solution.py:253
  23.8 2.4 %route.1 = (bf16[16,32,1024]{2,1,0:T(8,128)(2,1)}, s32[256,1]{1,0:T(8,128)S(1)}) custom-call(s32[2]{0:T(128)S(1)} %pad_add_fusion.shift_ref.scal_ref, bf16[16,16,1024]{2,1,0:T(8,128)(2,1)S(1)} %all-to-all-done.x_ref), custom_call_target="tpu_custom_call" | custom-call | tf_op jit(solution)/shard_map/route/pallas_call | solution.py:255
  26.2 4.1 %all-to-all-start.1 = ((bf16[16,32,1024]{2,1,0:T(8,128)(2,1)}), bf16[16,32,1024]{2,1,0:T(8,128)(2,1)S(1)}, u32[]{:S(2)}, u32[]{:S(2)}) async-start(bf16[16,32,1024]{2,1,0:T(8,128)(2,1)} %get-tuple-element.27), calls=%async_computation.1 | async-start | bytes 2097152 | tf_op jit(solution)/shard_map/all_to_all | solution.py:265
  30.3 0.0 copy-start
  30.3 3.1 %copy-done = bf16[928,4096]{1,0:T(8,128)(2,1)S(1)} copy-done((bf16[928,4096]{1,0:T(8,128)(2,1)S(1)}, bf16[928,4096]{1,0:T(8,128)(2,1)}, u32[]{:S(2)}) %copy-start) | copy-done | bytes 7602200
  33.5 6.1 %base.1 = (f32[8,16,4096]{2,1,0:T(8,128)S(1)}, bf16[8,16,4096]{2,1,0:T(8,128)(2,1)}) custom-call(s32[2]{0:T(128)S(1)} %pad_add_fusion.shift_ref.scal_ref, bf16[16,16,1024]{2,1,0:T(8,128)(2,1)S(1)} %all-to-all-done.x_ref, bf16[928,4096]{1,0:T(8,128)(2,1)S(1)} %copy-done), custom_call_target="tpu_custom_call" | custom-call | flops 1946157056 | bytes 10747904 | tf_op jit(solution)/shard_map/base/pallas_call | solution.py:269
  39.5 1.3 %copy-done.1 = f32[8,16,4096]{2,1,0:T(8,128)} copy-done((f32[8,16,4096]{2,1,0:T(8,128)}, f32[8,16,4096]{2,1,0:T(8,128)S(1)}, u32[]{:S(2)}) %copy-start.1) | copy-done | bytes 2097176
  40.9 0.4 collective-permute-start
  41.3 2.5 %collective-permute-done.got_ref = bf16[8,16,4096]{2,1,0:T(8,128)(2,1)S(1)} collective-permute-done((bf16[8,16,4096]{2,1,0:T(8,128)(2,1)}, bf16[8,16,4096]{2,1,0:T(8,128)(2,1)S(1)}, u32[]{:S(2)}, u32[]{:S(2)}) %collective-permute-start) | collective-permute-done | bytes 1048608 | tf_op jit(solution)/shard_map/ppermute | solution.py:307
  43.8 1.0 copy-done.3
  44.7 1.6 %copy-done.2 = f32[8,16,4096]{2,1,0:T(8,128)S(1)} copy-done((f32[8,16,4096]{2,1,0:T(8,128)S(1)}, f32[8,16,4096]{2,1,0:T(8,128)}, u32[]{:S(2)}) %copy-start.2) | copy-done | bytes 2097176
  46.3 1.2 %copy-done.4 = bf16[8,16,4096]{2,1,0:T(8,128)(2,1)S(1)} copy-done((bf16[8,16,4096]{2,1,0:T(8,128)(2,1)S(1)}, bf16[8,16,4096]{2,1,0:T(8,128)(2,1)}, u32[]{:S(2)}) %copy-start.4) | copy-done | bytes 1048600
  47.6 1.0 halve.3
  48.5 4.7 %all-to-all-done.1.x_ref = bf16[16,32,1024]{2,1,0:T(8,128)(2,1)S(1)} async-done(((bf16[16,32,1024]{2,1,0:T(8,128)(2,1)}), bf16[16,32,1024]{2,1,0:T(8,128)(2,1)S(1)}, u32[]{:S(2)}, u32[]{:S(2)}) %all-to-all-start.1) | async-done | bytes 1048608 | tf_op jit(solution)/shard_map/all_to_all | solution.py:265
  53.2 1.8 %collective-permute-start.1 = (bf16[4,16,4096]{2,1,0:T(8,128)(2,1)}, bf16[4,16,4096]{2,1,0:T(8,128)(2,1)S(1)}, u32[]{:S(2)}, u32[]{:S(2)}) collective-permute-start(bf16[4,16,4096]{2,1,0:T(8,128)(2,1)} %get-tuple-element.28), channel_id=1, source_target_pairs={{0,2},{1,3},{2,0},{3,1},{4,6},{5,7},{6,4},{7,5},{8,10},{9,11},{10,... | collective-permute-start | bytes 1572872 | tf_op jit(solution)/shard_map/ppermute | solution.py:340
  55.0 10.0 %delta.1 = bf16[16,32,256]{2,1,0:T(8,128)(2,1)} custom-call(s32[4,186]{1,0:T(4,128)S(1)} %copy-done.5, bf16[16,32,1024]{2,1,0:T(8,128)(2,1)S(1)} %all-to-all-done.1.x_ref, bf16[4,186,128,128]{3,2,1,0:T(8,128)(2,1)} %v_hbm.1), custom_call_target="tpu_custom_call" | custom-call | flops 195035136 | bytes 24379392 | tf_op jit(solution)/shard_map/delta/pallas_call | solution.py:317
  65.0 6.1 %all-to-all-start.2 = ((bf16[16,32,256]{2,1,0:T(8,128)(2,1)}), bf16[16,32,256]{2,1,0:T(8,128)(2,1)S(1)}, u32[]{:S(2)}, u32[]{:S(2)}) async-start(bf16[16,32,256]{2,1,0:T(8,128)(2,1)} %delta.1), calls=%async_computation.2 | async-start | bytes 524288 | tf_op jit(solution)/shard_map/all_to_all | solution.py:338
  71.2 0.0 collective-permute-done.1.got_ref
  71.2 0.1 halve.4
  71.3 2.0 %collective-permute-start.2 = (bf16[2,16,4096]{2,1,0:T(8,128)(2,1)S(1)}, bf16[2,16,4096]{2,1,0:T(8,128)(2,1)S(1)}, u32[]{:S(2)}, u32[]{:S(2)}) collective-permute-start(bf16[2,16,4096]{2,1,0:T(8,128)(2,1)S(1)} %get-tuple-element.30), channel_id=1, source_target_pairs={{0,4},{1,5},{2,6},{3,7},{4,0},{5,1},{6,2},{7,3},{8,12},{9,13},{10,... | collective-permute-start | bytes 786440 | tf_op jit(solution)/shard_map/ppermute | solution.py:340
  73.2 10.9 %collective-permute-done.2.got_ref = bf16[2,16,4096]{2,1,0:T(8,128)(2,1)S(1)} collective-permute-done((bf16[2,16,4096]{2,1,0:T(8,128)(2,1)S(1)}, bf16[2,16,4096]{2,1,0:T(8,128)(2,1)S(1)}, u32[]{:S(2)}, u32[]{:S(2)}) %collective-permute-start.2) | collective-permute-done | bytes 262176 | tf_op jit(solution)/shard_map/ppermute | solution.py:340
  84.2 0.0 all-to-all-done.2.c_ref
  84.2 0.9 pick.1
  85.1 4.6 %all-to-all-start.3 = ((bf16[16,16,256]{2,1,0:T(8,128)(2,1)}), bf16[16,16,256]{2,1,0:T(8,128)(2,1)S(1)}, u32[]{:S(2)}, u32[]{:S(2)}) async-start(bf16[16,16,256]{2,1,0:T(8,128)(2,1)} %pick.1), calls=%async_computation.3 | async-start | bytes 262144 | tf_op jit(solution)/shard_map/all_to_all | solution.py:352
  89.7 2.8 %collective-permute-start.3 = (bf16[1,16,4096]{2,1,0:T(8,128)(2,1)S(1)}, bf16[1,16,4096]{2,1,0:T(8,128)(2,1)S(1)}, u32[]{:S(2)}, u32[]{:S(2)}) collective-permute-start(bf16[1,16,4096]{2,1,0:T(8,128)(2,1)S(1)} %get-tuple-element.34), channel_id=1, source_target_pairs={{0,8},{1,9},{2,10},{3,11},{4,12},{5,13},{6,14},{7,15},{8,0},{9,1},... | collective-permute-start | bytes 393224 | tf_op jit(solution)/shard_map/ppermute | solution.py:340
  92.6 9.6 %collective-permute-done.3.got_ref = bf16[1,16,4096]{2,1,0:T(8,128)(2,1)S(1)} collective-permute-done((bf16[1,16,4096]{2,1,0:T(8,128)(2,1)S(1)}, bf16[1,16,4096]{2,1,0:T(8,128)(2,1)S(1)}, u32[]{:S(2)}, u32[]{:S(2)}) %collective-permute-start.3) | collective-permute-done | bytes 131104 | tf_op jit(solution)/shard_map/ppermute | solution.py:340
  102.2 0.0 all-to-all-done.3.own_ref
  102.2 0.7 finish.1
  (6 shorter events, 0.1 us)
Async XLA Ops:
  2.0 53.1 %copy-start.5 = (s32[4,186]{1,0:T(4,128)S(1)}, s32[4,186]{1,0:T(4,128)}, u32[]{:S(2)}) copy-start(s32[4,186]{1,0:T(4,128)} %ids_ref.1) | copy-start | bytes 8932
  2.0 21.9 %all-to-all-start = ((bf16[16,16,1024]{2,1,0:T(8,128)(2,1)}), bf16[16,16,1024]{2,1,0:T(8,128)(2,1)S(1)}, u32[]{:S(2)}, u32[]{:S(2)}) async-start(bf16[16,16,1024]{2,1,0:T(8,128)(2,1)} %split_rows.1), calls=%async_computation | async-start | bytes 1048576 | tf_op jit(solution)/shard_map/all_to_all | solution.py:253
  26.2 27.0 %all-to-all-start.1 = ((bf16[16,32,1024]{2,1,0:T(8,128)(2,1)}), bf16[16,32,1024]{2,1,0:T(8,128)(2,1)S(1)}, u32[]{:S(2)}, u32[]{:S(2)}) async-start(bf16[16,32,1024]{2,1,0:T(8,128)(2,1)} %get-tuple-element.27), calls=%async_computation.1 | async-start | bytes 2097152 | tf_op jit(solution)/shard_map/all_to_all | solution.py:265
  30.3 3.2 %copy-start = (bf16[928,4096]{1,0:T(8,128)(2,1)S(1)}, bf16[928,4096]{1,0:T(8,128)(2,1)}, u32[]{:S(2)}) copy-start(bf16[928,4096]{1,0:T(8,128)(2,1)} %w_ref.1) | copy-start | bytes 22806532
  39.5 1.3 %copy-start.1 = (f32[8,16,4096]{2,1,0:T(8,128)}, f32[8,16,4096]{2,1,0:T(8,128)S(1)}, u32[]{:S(2)}) copy-start(f32[8,16,4096]{2,1,0:T(8,128)S(1)} %get-tuple-element.23.keep_ref) | copy-start | bytes 6291460
  40.9 2.9 %collective-permute-start = (bf16[8,16,4096]{2,1,0:T(8,128)(2,1)}, bf16[8,16,4096]{2,1,0:T(8,128)(2,1)S(1)}, u32[]{:S(2)}, u32[]{:S(2)}) collective-permute-start(bf16[8,16,4096]{2,1,0:T(8,128)(2,1)} %get-tuple-element.24), channel_id=1, source_target_pairs={{0,1},{1,0},{2,3},{3,2},{4,5},{5,4},{6,7},{7,6},{8,9},{9,8},{10,11... | collective-permute-start | bytes 3145736 | tf_op jit(solution)/shard_map/ppermute | solution.py:307
  43.8 1.0 copy-start.3
  44.7 1.6 %copy-start.2 = (f32[8,16,4096]{2,1,0:T(8,128)S(1)}, f32[8,16,4096]{2,1,0:T(8,128)}, u32[]{:S(2)}) copy-start(f32[8,16,4096]{2,1,0:T(8,128)} %copy-done.1) | copy-start | bytes 6291460
  46.3 1.2 %copy-start.4 = (bf16[8,16,4096]{2,1,0:T(8,128)(2,1)S(1)}, bf16[8,16,4096]{2,1,0:T(8,128)(2,1)}, u32[]{:S(2)}) copy-start(bf16[8,16,4096]{2,1,0:T(8,128)(2,1)} %copy-done.3) | copy-start | bytes 3145732
  53.2 17.9 %collective-permute-start.1 = (bf16[4,16,4096]{2,1,0:T(8,128)(2,1)}, bf16[4,16,4096]{2,1,0:T(8,128)(2,1)S(1)}, u32[]{:S(2)}, u32[]{:S(2)}) collective-permute-start(bf16[4,16,4096]{2,1,0:T(8,128)(2,1)} %get-tuple-element.28), channel_id=1, source_target_pairs={{0,2},{1,3},{2,0},{3,1},{4,6},{5,7},{6,4},{7,5},{8,10},{9,11},{10,... | collective-permute-start | bytes 1572872 | tf_op jit(solution)/shard_map/ppermute | solution.py:340
  65.0 19.1 %all-to-all-start.2 = ((bf16[16,32,256]{2,1,0:T(8,128)(2,1)}), bf16[16,32,256]{2,1,0:T(8,128)(2,1)S(1)}, u32[]{:S(2)}, u32[]{:S(2)}) async-start(bf16[16,32,256]{2,1,0:T(8,128)(2,1)} %delta.1), calls=%async_computation.2 | async-start | bytes 524288 | tf_op jit(solution)/shard_map/all_to_all | solution.py:338
  71.3 12.8 %collective-permute-start.2 = (bf16[2,16,4096]{2,1,0:T(8,128)(2,1)S(1)}, bf16[2,16,4096]{2,1,0:T(8,128)(2,1)S(1)}, u32[]{:S(2)}, u32[]{:S(2)}) collective-permute-start(bf16[2,16,4096]{2,1,0:T(8,128)(2,1)S(1)} %get-tuple-element.30), channel_id=1, source_target_pairs={{0,4},{1,5},{2,6},{3,7},{4,0},{5,1},{6,2},{7,3},{8,12},{9,13},{10,... | collective-permute-start | bytes 786440 | tf_op jit(solution)/shard_map/ppermute | solution.py:340
  85.1 17.1 %all-to-all-start.3 = ((bf16[16,16,256]{2,1,0:T(8,128)(2,1)}), bf16[16,16,256]{2,1,0:T(8,128)(2,1)S(1)}, u32[]{:S(2)}, u32[]{:S(2)}) async-start(bf16[16,16,256]{2,1,0:T(8,128)(2,1)} %pick.1), calls=%async_computation.3 | async-start | bytes 262144 | tf_op jit(solution)/shard_map/all_to_all | solution.py:352
  89.7 12.5 %collective-permute-start.3 = (bf16[1,16,4096]{2,1,0:T(8,128)(2,1)S(1)}, bf16[1,16,4096]{2,1,0:T(8,128)(2,1)S(1)}, u32[]{:S(2)}, u32[]{:S(2)}) collective-permute-start(bf16[1,16,4096]{2,1,0:T(8,128)(2,1)S(1)} %get-tuple-element.34), channel_id=1, source_target_pairs={{0,8},{1,9},{2,10},{3,11},{4,12},{5,13},{6,14},{7,15},{8,0},{9,1},... | collective-permute-start | bytes 393224 | tf_op jit(solution)/shard_map/ppermute | solution.py:340

commit v6 on v5

--- a/solution.py
+++ b/solution.py
@@ -75,12 +75,12 @@
     rows = peers * row_dev
     slots = o_ref.shape[0] * o_ref.shape[1]
     variants = slots // capacity
-    shift = shift_ref[0]
-    x = x_ref[...].reshape(rows, window).astype(F32)
-    lane = lane_iota(rows, window)
-    spare = lax.rem(shift + share, window)
-    slot = jnp.sum(jnp.where(lane == spare, x, 0.0), axis=1, keepdims=True)
-    data = jnp.where((lane >= shift) & (lane < shift + share), x, 0.0).astype(BF16)
+    spare = lax.rem(shift_ref[0] + share, window)
+    tile = pl.multiple_of(spare // LANES * LANES, LANES)
+    near = x_ref[:, :, pl.ds(tile, LANES)].reshape(rows, LANES).astype(F32)
+    at = lane_iota(rows, LANES) == spare - tile
+    slot = jnp.sum(jnp.where(at, near, 0.0), axis=1, keepdims=True)
+    data = x_ref[...].reshape(rows, window)
     onehot = jnp.where(slot.astype(jnp.int32) == lane_iota(rows, variants), 1.0, 0.0)
     row_i = lax.broadcasted_iota(jnp.int32, (rows, rows), 0)
     row_j = lane_iota(rows, rows)
@@ -96,29 +96,35 @@
     o_ref[...] = filled.reshape(o_ref.shape)
 
 
-def base_kernel(plan, scal_ref, x_ref, w_ref, keep_ref, send_ref, mine_ref):
+def base_kernel(plan, scal_ref, x_ref, w_hbm, keep_ref, send_ref, mine_ref, w_ref, sems):
     share, window, _, _ = plan
     peers, row_dev, _ = x_ref.shape
     half = peers // 2 * row_dev
-
-    @pl.when(pl.program_id(0) == 0)
-    def _():
-        bit = scal_ref[1]
-        for side in (0, 1):
-            which = bit if side == 0 else 1 - bit
-            for q in range(peers // 2):
-                piece = x_ref[2 * q + which].astype(F32)
-                piece = pltpu.roll(piece, window - scal_ref[0], 1)
-                at = side * half + q * row_dev
-                mine_ref[at : at + row_dev] = piece[:, :share].astype(BF16)
-
-    both = jnp.dot(mine_ref[...], w_ref[...], preferred_element_type=F32)
-    keep_ref[...] = both[:half].reshape(keep_ref.shape)
-    send_ref[...] = both[half:].astype(BF16).reshape(send_ref.shape)
+    parts, _, cols = w_ref.shape
+
+    def fetch(p):
+        return pltpu.make_async_copy(w_hbm.at[:, pl.ds(p * cols, cols)], w_ref.at[p], sems.at[p])
+
+    for p in range(parts):
+        fetch(p).start()
+    bit = scal_ref[1]
+    for side in (0, 1):
+        which = bit if side == 0 else 1 - bit
+        for q in range(peers // 2):
+            piece = x_ref[2 * q + which].astype(F32)
+            piece = pltpu.roll(piece, window - scal_ref[0], 1)
+            at = side * half + q * row_dev
+            mine_ref[at : at + row_dev] = piece[:, :share].astype(BF16)
+    for p in range(parts):
+        fetch(p).wait()
+        both = jnp.dot(mine_ref[...], w_ref[p], preferred_element_type=F32)
+        at = slice(p * cols, (p + 1) * cols)
+        keep_ref[:, :, at] = both[:half].reshape(keep_ref.shape[:2] + (cols,))
+        send_ref[:, :, at] = both[half:].astype(BF16).reshape(send_ref.shape[:2] + (cols,))
 
 
 def delta_kernel(plan, d_blocks, group, ids_ref, x_ref, v_hbm, o_ref, rows_ref, acc_ref, held_ref, sems):
-    _, window, _, starts = plan
+    share, window, _, starts = plan
     local_var, f_blocks, capacity, _ = rows_ref.shape
     chunks, _, size, _ = held_ref.shape
     per = chunks // local_var
@@ -135,6 +141,10 @@
     for s, b in enumerate(starts):
         for k in range(window // LANES):
             tile = x_ref[s, :, k * LANES : (k + 1) * LANES].astype(F32)
+            low = s * share - (b + k) * LANES
+            if low > 0 or low + share < LANES:
+                lane = lane_iota(tile.shape[0], LANES)
+                tile = jnp.where((lane >= low) & (lane < low + share), tile, 0.0)
             for v in range(local_var):
                 part = tile[v * capacity : (v + 1) * capacity]
                 if b + k in done:
@@ -265,28 +275,22 @@
     arrived = lax.all_to_all(slots, "cols", 0, 0)
     x, place = lax.optimization_barrier((x, place))
 
-    tile = min(512, width_d)
+    cols = min(512, width_d)
+    part = (half, row_dev, width_d)
     keep, send = pl.pallas_call(
         functools.partial(base_kernel, plan),
-        grid=(width_d // tile,),
-        out_shape=(
-            jax.ShapeDtypeStruct((half, row_dev, width_d), F32),
-            jax.ShapeDtypeStruct((half, row_dev, width_d), BF16),
-        ),
-        in_specs=[
-            smem,
-            pl.BlockSpec((peers, row_dev, window), lambda t: (0, 0, 0)),
-            pl.BlockSpec((share, tile), lambda t: (0, t)),
+        in_specs=[smem, vmem, anywhere],
+        out_specs=(vmem, vmem),
+        out_shape=(jax.ShapeDtypeStruct(part, F32), jax.ShapeDtypeStruct(part, BF16)),
+        scratch_shapes=[
+            pltpu.VMEM((all_rows, share), BF16),
+            pltpu.VMEM((width_d // cols, share, cols), BF16),
+            pltpu.SemaphoreType.DMA((width_d // cols,)),
         ],
-        out_specs=(
-            pl.BlockSpec((half, row_dev, tile), lambda t: (0, 0, t)),
-            pl.BlockSpec((half, row_dev, tile), lambda t: (0, 0, t)),
-        ),
-        scratch_shapes=[pltpu.VMEM((all_rows, share), BF16)],
-        compiler_params=params(),
+        compiler_params=params(48),
         cost_estimate=pl.CostEstimate(
             flops=2 * all_rows * share * width_d,
-            bytes_accessed=2 * share * width_d + 6 * all_rows // 2 * width_d,
+            bytes_accessed=2 * share * width_d,
             transcendentals=0,
         ),
         name="base",
@@ -300,7 +304,7 @@
             halve_kernel,
             in_specs=[smem, vmem, vmem],
             out_shape=(jax.ShapeDtypeStruct(left, F32), jax.ShapeDtypeStruct(left, BF16)),
-            compiler_params=params(),
+            compiler_params=params(60 if step == 2 else 16),
             name="halve",
         )(bit, keep, got)
 
@@ -308,7 +312,6 @@
     step = 2
     if step < peers:
         keep, send = halve(step, keep, got)
-        send, arrived = lax.optimization_barrier((send, arrived))
 
     group = split_factor(count, 64)
     aligned = slice_d % LANES == 0
@@ -341,8 +344,6 @@
         step *= 2
         if step < peers:
             keep, send = halve(step, keep, got)
-        if step == peers // 2:
-            send, place = lax.optimization_barrier((send, place))
     by_row = pl.pallas_call(
         pick_kernel,
         out_shape=jax.ShapeDtypeStruct((peers, row_dev, slice_d), BF16),

time: 104 us -> 98.7 us (0.949)
  local copies, waits for them, and re-layouts: 8.27 us -> 1.35 us
  Pallas kernels: 23.1 us -> 24.6 us
    ppermute x3, waiting for transfers between devices: 20.5 us -> 9.5 us  [body(): got = lax.ppermute(send, 'cols', pairs(step))]
    all_to_all x1, waiting for transfers between devices: 0.01 us -> 8.42 us  [body(): columns = lax.all_to_all(deltas, 'cols', 0, 0)]
    unnamed x12 -> x6, local copies, waits for them, and re-layouts: 8.27 us -> 1.35 us
    all_to_all x1, waiting for transfers between devices: 4.73 us -> 8.34 us  [body(): arrived = lax.all_to_all(slots, 'cols', 0, 0)]
    pallas_call x3, Pallas kernels: 1.09 us -> 3.3 us  [halve(): pl.pallas_call(halve_kernel, in_specs=[smem, vmem, vmem], out_shape=(jax....]
    all_to_all x1, starting transfers between devices: 4.65 us -> 3.51 us  [body(): own = lax.all_to_all(by_row, 'cols', 0, 0)]
  transfers between devices with their start and end apart: 8 -> 8, of which waited for: 5 -> 5; matrix products, arithmetic and copies ran while one was open for 0% -> 0% of each run, Pallas kernels for 17% -> 20%
where the time goes in v6:
time: 98.7 us; the launch traced here: 98.2 us
  waiting for transfers between devices  43.1 us (44%)
  starting transfers between devices  29 us (29%)
  Pallas kernels  24.6 us (25%)
  local copies, waits for them, and re-layouts  1.35 us (1%)
    all_to_all x1, waiting for transfers between devices, body(): x = lax.all_to_all(outgoing, 'cols', 0, 0)  14.4 us
    pallas_call x1, Pallas kernels, body(): pl.pallas_call(functools.partial(delta_kernel, plan, d_blocks, group), in...  9.98 us
    ppermute x3, waiting for transfers between devices, body(): got = lax.ppermute(send, 'cols', pairs(step))  9.5 us
    all_to_all x1, waiting for transfers between devices, body(): columns = lax.all_to_all(deltas, 'cols', 0, 0)  8.42 us
    all_to_all x1, waiting for transfers between devices, body(): arrived = lax.all_to_all(slots, 'cols', 0, 0)  8.34 us
    all_to_all x1, starting transfers between devices, body(): x = lax.all_to_all(outgoing, 'cols', 0, 0)  7.4 us
    all_to_all x1, starting transfers between devices, body(): columns = lax.all_to_all(deltas, 'cols', 0, 0)  6.91 us
    ppermute x3, starting transfers between devices, body(): got = lax.ppermute(send, 'cols', pairs(step))  6.64 us
  transfers between devices with their start and end apart: 8, of which 5 were waited for; matrix products, arithmetic and copies ran while one was open for 0% of the time, Pallas kernels for 20%

profile of v6, /device:TPU:0, one launch (start us, length us, event | category | flops | bytes accessed | tf_op | source)
XLA Modules:
  0.0 98.2 jit_solution(433816091175583351)
XLA Ops:
  0.0 1.9 %split_rows.1 = bf16[16,16,1024]{2,1,0:T(8,128)(2,1)} custom-call(bf16[16,14848]{1,0:T(8,128)(2,1)} %h_hbm.1, s32[1,16]{1,0:T(1,128)} %bitcast.7, s32[1,64]{1,0:T(1,128)} %bitcast.8), custom_call_target="tpu_custom_call" | custom-call | tf_op jit(solution)/shard_map/split_rows/pallas_call | solution.py:250
  1.9 0.0 copy-start.2
  2.0 7.4 %all-to-all-start = ((bf16[16,16,1024]{2,1,0:T(8,128)(2,1)}), bf16[16,16,1024]{2,1,0:T(8,128)(2,1)S(1)}, u32[]{:S(2)}, u32[]{:S(2)}) async-start(bf16[16,16,1024]{2,1,0:T(8,128)(2,1)} %split_rows.1), calls=%async_computation | async-start | bytes 1048576 | tf_op jit(solution)/shard_map/all_to_all | solution.py:263
  9.4 0.1 pad_add_fusion.shift_ref.scal_ref
  9.5 14.4 %all-to-all-done.x_ref = bf16[16,16,1024]{2,1,0:T(8,128)(2,1)S(1)} async-done(((bf16[16,16,1024]{2,1,0:T(8,128)(2,1)}), bf16[16,16,1024]{2,1,0:T(8,128)(2,1)S(1)}, u32[]{:S(2)}, u32[]{:S(2)}) %all-to-all-start) | async-done | bytes 524320 | tf_op jit(solution)/shard_map/all_to_all | solution.py:263
  23.8 2.3 %route.1 = (bf16[16,32,1024]{2,1,0:T(8,128)(2,1)}, s32[256,1]{1,0:T(8,128)S(1)}) custom-call(s32[2]{0:T(128)S(1)} %pad_add_fusion.shift_ref.scal_ref, bf16[16,16,1024]{2,1,0:T(8,128)(2,1)S(1)} %all-to-all-done.x_ref), custom_call_target="tpu_custom_call" | custom-call | tf_op jit(solution)/shard_map/route/pallas_call | solution.py:265
  26.1 4.1 %all-to-all-start.1 = ((bf16[16,32,1024]{2,1,0:T(8,128)(2,1)}), bf16[16,32,1024]{2,1,0:T(8,128)(2,1)S(1)}, u32[]{:S(2)}, u32[]{:S(2)}) async-start(bf16[16,32,1024]{2,1,0:T(8,128)(2,1)} %get-tuple-element.28), calls=%async_computation.1 | async-start | bytes 2097152 | tf_op jit(solution)/shard_map/all_to_all | solution.py:275
  30.2 5.4 %base.1 = (f32[8,16,4096]{2,1,0:T(8,128)S(1)}, bf16[8,16,4096]{2,1,0:T(8,128)(2,1)S(1)}) custom-call(s32[2]{0:T(128)S(1)} %pad_add_fusion.shift_ref.scal_ref, bf16[16,16,1024]{2,1,0:T(8,128)(2,1)S(1)} %all-to-all-done.x_ref, bf16[928,4096]{1,0:T(8,128)(2,1)} %w_hbm.1), custom_call_target="tpu_custom_call" | custom-call | flops 1946157056 | bytes 7602176 | tf_op jit(solution)/shard_map/base/pallas_call | solution.py:280
  35.7 0.0 copy-start
  35.7 1.3 %copy-done = f32[8,16,4096]{2,1,0:T(8,128)} copy-done((f32[8,16,4096]{2,1,0:T(8,128)}, f32[8,16,4096]{2,1,0:T(8,128)S(1)}, u32[]{:S(2)}) %copy-start) | copy-done | bytes 2097176
  37.0 0.4 collective-permute-start
  37.4 2.4 %collective-permute-done.got_ref = bf16[8,16,4096]{2,1,0:T(8,128)(2,1)} collective-permute-done((bf16[8,16,4096]{2,1,0:T(8,128)(2,1)S(1)}, bf16[8,16,4096]{2,1,0:T(8,128)(2,1)}, u32[]{:S(2)}, u32[]{:S(2)}) %collective-permute-start) | collective-permute-done | bytes 1048608 | tf_op jit(solution)/shard_map/ppermute | solution.py:311
  39.8 3.2 %halve.3 = (f32[4,16,4096]{2,1,0:T(8,128)}, bf16[4,16,4096]{2,1,0:T(8,128)(2,1)}) custom-call(s32[1]{0:T(128)} %bitcast.2.bit_ref, f32[8,16,4096]{2,1,0:T(8,128)} %copy-done, bf16[8,16,4096]{2,1,0:T(8,128)(2,1)} %collective-permute-done.got_ref), custom_call_target="tpu_custom_call" | custom-call | tf_op jit(solution)/shard_map/halve/pallas_call | solution.py:303
  43.0 0.0 copy-start.1
  43.0 1.9 %collective-permute-start.1 = (bf16[4,16,4096]{2,1,0:T(8,128)(2,1)}, bf16[4,16,4096]{2,1,0:T(8,128)(2,1)S(1)}, u32[]{:S(2)}, u32[]{:S(2)}) collective-permute-start(bf16[4,16,4096]{2,1,0:T(8,128)(2,1)} %get-tuple-element.22), channel_id=1, source_target_pairs={{0,2},{1,3},{2,0},{3,1},{4,6},{5,7},{6,4},{7,5},{8,10},{9,11},{10,... | collective-permute-start | bytes 1572872 | tf_op jit(solution)/shard_map/ppermute | solution.py:343
  44.9 8.3 %all-to-all-done.1.x_ref = bf16[16,32,1024]{2,1,0:T(8,128)(2,1)S(1)} async-done(((bf16[16,32,1024]{2,1,0:T(8,128)(2,1)}), bf16[16,32,1024]{2,1,0:T(8,128)(2,1)S(1)}, u32[]{:S(2)}, u32[]{:S(2)}) %all-to-all-start.1) | async-done | bytes 1048608 | tf_op jit(solution)/shard_map/all_to_all | solution.py:275
  53.2 0.0 copy-done.2
  53.2 10.0 %delta.1 = bf16[16,32,256]{2,1,0:T(8,128)(2,1)} custom-call(s32[4,186]{1,0:T(4,128)S(1)} %copy-done.2, bf16[16,32,1024]{2,1,0:T(8,128)(2,1)S(1)} %all-to-all-done.1.x_ref, bf16[4,186,128,128]{3,2,1,0:T(8,128)(2,1)} %v_hbm.1), custom_call_target="tpu_custom_call" | custom-call | flops 195035136 | bytes 24379392 | tf_op jit(solution)/shard_map/delta/pallas_call | solution.py:320
  63.2 6.9 %all-to-all-start.2 = ((bf16[16,32,256]{2,1,0:T(8,128)(2,1)}), bf16[16,32,256]{2,1,0:T(8,128)(2,1)S(1)}, u32[]{:S(2)}, u32[]{:S(2)}) async-start(bf16[16,32,256]{2,1,0:T(8,128)(2,1)} %delta.1), calls=%async_computation.2 | async-start | bytes 524288 | tf_op jit(solution)/shard_map/all_to_all | solution.py:341
  70.2 0.0 collective-permute-done.1.got_ref
  70.2 0.0 copy-done.1
  70.2 0.1 halve.4
  70.3 2.0 %collective-permute-start.2 = (bf16[2,16,4096]{2,1,0:T(8,128)(2,1)S(1)}, bf16[2,16,4096]{2,1,0:T(8,128)(2,1)S(1)}, u32[]{:S(2)}, u32[]{:S(2)}) collective-permute-start(bf16[2,16,4096]{2,1,0:T(8,128)(2,1)S(1)} %get-tuple-element.24), channel_id=1, source_target_pairs={{0,4},{1,5},{2,6},{3,7},{4,0},{5,1},{6,2},{7,3},{8,12},{9,13},{10,... | collective-permute-start | bytes 786440 | tf_op jit(solution)/shard_map/ppermute | solution.py:343
  72.2 8.4 %all-to-all-done.2.c_ref = bf16[16,32,256]{2,1,0:T(8,128)(2,1)S(1)} async-done(((bf16[16,32,256]{2,1,0:T(8,128)(2,1)}), bf16[16,32,256]{2,1,0:T(8,128)(2,1)S(1)}, u32[]{:S(2)}, u32[]{:S(2)}) %all-to-all-start.2) | async-done | bytes 262176 | tf_op jit(solution)/shard_map/all_to_all | solution.py:341
  80.7 0.9 pick.1
  81.6 3.5 %all-to-all-start.3 = ((bf16[16,16,256]{2,1,0:T(8,128)(2,1)}), bf16[16,16,256]{2,1,0:T(8,128)(2,1)S(1)}, u32[]{:S(2)}, u32[]{:S(2)}) async-start(bf16[16,16,256]{2,1,0:T(8,128)(2,1)} %pick.1), calls=%async_computation.3 | async-start | bytes 262144 | tf_op jit(solution)/shard_map/all_to_all | solution.py:353
  85.1 0.0 collective-permute-done.2.got_ref
  85.2 2.8 %collective-permute-start.3 = (bf16[1,16,4096]{2,1,0:T(8,128)(2,1)S(1)}, bf16[1,16,4096]{2,1,0:T(8,128)(2,1)S(1)}, u32[]{:S(2)}, u32[]{:S(2)}) collective-permute-start(bf16[1,16,4096]{2,1,0:T(8,128)(2,1)S(1)} %get-tuple-element.26), channel_id=1, source_target_pairs={{0,8},{1,9},{2,10},{3,11},{4,12},{5,13},{6,14},{7,15},{8,0},{9,1},... | collective-permute-start | bytes 393224 | tf_op jit(solution)/shard_map/ppermute | solution.py:343
  88.0 9.5 %collective-permute-done.3.got_ref = bf16[1,16,4096]{2,1,0:T(8,128)(2,1)S(1)} collective-permute-done((bf16[1,16,4096]{2,1,0:T(8,128)(2,1)S(1)}, bf16[1,16,4096]{2,1,0:T(8,128)(2,1)S(1)}, u32[]{:S(2)}, u32[]{:S(2)}) %collective-permute-start.3) | collective-permute-done | bytes 131104 | tf_op jit(solution)/shard_map/ppermute | solution.py:343
  97.5 0.0 all-to-all-done.3.own_ref
  97.5 0.7 finish.1
  (1 shorter events, 0.0 us)
Async XLA Ops:
  1.9 51.3 %copy-start.2 = (s32[4,186]{1,0:T(4,128)S(1)}, s32[4,186]{1,0:T(4,128)}, u32[]{:S(2)}) copy-start(s32[4,186]{1,0:T(4,128)} %ids_ref.1) | copy-start | bytes 8932
  2.0 21.9 %all-to-all-start = ((bf16[16,16,1024]{2,1,0:T(8,128)(2,1)}), bf16[16,16,1024]{2,1,0:T(8,128)(2,1)S(1)}, u32[]{:S(2)}, u32[]{:S(2)}) async-start(bf16[16,16,1024]{2,1,0:T(8,128)(2,1)} %split_rows.1), calls=%async_computation | async-start | bytes 1048576 | tf_op jit(solution)/shard_map/all_to_all | solution.py:263
  26.1 27.1 %all-to-all-start.1 = ((bf16[16,32,1024]{2,1,0:T(8,128)(2,1)}), bf16[16,32,1024]{2,1,0:T(8,128)(2,1)S(1)}, u32[]{:S(2)}, u32[]{:S(2)}) async-start(bf16[16,32,1024]{2,1,0:T(8,128)(2,1)} %get-tuple-element.28), calls=%async_computation.1 | async-start | bytes 2097152 | tf_op jit(solution)/shard_map/all_to_all | solution.py:275
  35.7 1.3 %copy-start = (f32[8,16,4096]{2,1,0:T(8,128)}, f32[8,16,4096]{2,1,0:T(8,128)S(1)}, u32[]{:S(2)}) copy-start(f32[8,16,4096]{2,1,0:T(8,128)S(1)} %get-tuple-element.19.keep_ref) | copy-start | bytes 6291460
  37.0 2.8 %collective-permute-start = (bf16[8,16,4096]{2,1,0:T(8,128)(2,1)S(1)}, bf16[8,16,4096]{2,1,0:T(8,128)(2,1)}, u32[]{:S(2)}, u32[]{:S(2)}) collective-permute-start(bf16[8,16,4096]{2,1,0:T(8,128)(2,1)S(1)} %get-tuple-element.20), channel_id=1, source_target_pairs={{0,1},{1,0},{2,3},{3,2},{4,5},{5,4},{6,7},{7,6},{8,9},{9,8},{10,11... | collective-permute-start | bytes 3145736 | tf_op jit(solution)/shard_map/ppermute | solution.py:311
  43.0 27.2 %copy-start.1 = (f32[4,16,4096]{2,1,0:T(8,128)S(1)}, f32[4,16,4096]{2,1,0:T(8,128)}, u32[]{:S(2)}) copy-start(f32[4,16,4096]{2,1,0:T(8,128)} %get-tuple-element.21.keep_ref) | copy-start | bytes 3145732
  43.0 27.2 %collective-permute-start.1 = (bf16[4,16,4096]{2,1,0:T(8,128)(2,1)}, bf16[4,16,4096]{2,1,0:T(8,128)(2,1)S(1)}, u32[]{:S(2)}, u32[]{:S(2)}) collective-permute-start(bf16[4,16,4096]{2,1,0:T(8,128)(2,1)} %get-tuple-element.22), channel_id=1, source_target_pairs={{0,2},{1,3},{2,0},{3,1},{4,6},{5,7},{6,4},{7,5},{8,10},{9,11},{10,... | collective-permute-start | bytes 1572872 | tf_op jit(solution)/shard_map/ppermute | solution.py:343
  63.2 17.4 %all-to-all-start.2 = ((bf16[16,32,256]{2,1,0:T(8,128)(2,1)}), bf16[16,32,256]{2,1,0:T(8,128)(2,1)S(1)}, u32[]{:S(2)}, u32[]{:S(2)}) async-start(bf16[16,32,256]{2,1,0:T(8,128)(2,1)} %delta.1), calls=%async_computation.2 | async-start | bytes 524288 | tf_op jit(solution)/shard_map/all_to_all | solution.py:341
  70.3 14.9 %collective-permute-start.2 = (bf16[2,16,4096]{2,1,0:T(8,128)(2,1)S(1)}, bf16[2,16,4096]{2,1,0:T(8,128)(2,1)S(1)}, u32[]{:S(2)}, u32[]{:S(2)}) collective-permute-start(bf16[2,16,4096]{2,1,0:T(8,128)(2,1)S(1)} %get-tuple-element.24), channel_id=1, source_target_pairs={{0,4},{1,5},{2,6},{3,7},{4,0},{5,1},{6,2},{7,3},{8,12},{9,13},{10,... | collective-permute-start | bytes 786440 | tf_op jit(solution)/shard_map/ppermute | solution.py:343
  81.6 15.9 %all-to-all-start.3 = ((bf16[16,16,256]{2,1,0:T(8,128)(2,1)}), bf16[16,16,256]{2,1,0:T(8,128)(2,1)S(1)}, u32[]{:S(2)}, u32[]{:S(2)}) async-start(bf16[16,16,256]{2,1,0:T(8,128)(2,1)} %pick.1), calls=%async_computation.3 | async-start | bytes 262144 | tf_op jit(solution)/shard_map/all_to_all | solution.py:353
  85.2 12.3 %collective-permute-start.3 = (bf16[1,16,4096]{2,1,0:T(8,128)(2,1)S(1)}, bf16[1,16,4096]{2,1,0:T(8,128)(2,1)S(1)}, u32[]{:S(2)}, u32[]{:S(2)}) collective-permute-start(bf16[1,16,4096]{2,1,0:T(8,128)(2,1)S(1)} %get-tuple-element.26), channel_id=1, source_target_pairs={{0,8},{1,9},{2,10},{3,11},{4,12},{5,13},{6,14},{7,15},{8,0},{9,1},... | collective-permute-start | bytes 393224 | tf_op jit(solution)/shard_map/ppermute | solution.py:343

commit v7 on v6

--- a/solution.py
+++ b/solution.py
@@ -183,42 +183,48 @@
     lax.fori_loop(0, chunks, one_chunk, 0)
     for j in range(d_blocks):
         whole = jnp.concatenate([acc_ref[v, j] for v in range(local_var)], axis=0)
-        if len(o_ref.shape) == 3:
-            per_peer = o_ref.shape[2] // LANES
-            k = j % per_peer
-            o_ref[j // per_peer, :, k * LANES : (k + 1) * LANES] = whole.astype(BF16)
+        o_ref[:, j * LANES : (j + 1) * LANES] = whole.astype(BF16)
+
+
+def pair_kernel(keep_ref, got_ref, o_ref):
+    o_ref[...] = keep_ref[...] + got_ref[...].astype(F32)
+
+
+def join_kernel(stride, scal_ref, bit_ref, base_ref, place_ref, own_ref, got_ref, *rest):
+    next_ref, send_ref, sum_ref = rest
+    rows = place_ref.shape[0]
+    slots, cols = own_ref.shape
+    lane = lane_iota(rows, slots)
+    for source, (first, d_ref) in enumerate(((scal_ref[2], own_ref), (scal_ref[3], got_ref))):
+        pick = jnp.where(place_ref[...] - first == lane, 1.0, 0.0).astype(BF16)
+        part = jnp.dot(pick, d_ref[...], preferred_element_type=F32).reshape(sum_ref.shape)
+        if source == 0:
+            sum_ref[...] = base_ref[...] + part
         else:
-            o_ref[:, j * LANES : (j + 1) * LANES] = whole.astype(BF16)
-
-
-def pick_kernel(place_ref, c_ref, o_ref):
-    peers, per_owner, cols = c_ref.shape
-    slots = peers * per_owner
-    rows = place_ref.shape[0]
-    pick = place_ref[...] == lane_iota(rows, slots)
-    pick = jnp.where(pick, 1.0, 0.0).astype(BF16)
-    found = jnp.dot(pick, c_ref[...].reshape(slots, cols), preferred_element_type=F32)
-    o_ref[...] = found.astype(BF16).reshape(o_ref.shape)
-
-
-def halve_kernel(bit_ref, keep_ref, got_ref, next_ref, send_ref):
+            sum_ref[...] += part
     bit = bit_ref[0]
     for q in range(next_ref.shape[0]):
-        mine, other = 2 * q + bit, 2 * q + 1 - bit
+        at = q // stride * 2 * stride + q % stride
+        next_ref[q] = sum_ref[at + stride * bit]
+        send_ref[q] = sum_ref[at + stride * (1 - bit)].astype(BF16)
+
+
+def halve_kernel(stride, bit_ref, keep_ref, got_ref, next_ref, send_ref):
+    bit = bit_ref[0]
+    for q in range(next_ref.shape[0]):
+        first = q // stride * 2 * stride + q % stride
+        mine, other = first + stride * bit, first + stride * (1 - bit)
         next_ref[q] = keep_ref[mine] + got_ref[mine].astype(F32)
         send_ref[q] = (keep_ref[other] + got_ref[other].astype(F32)).astype(BF16)
 
 
-def finish_kernel(keep_ref, got_ref, own_ref, o_ref):
-    peers, _, cols = own_ref.shape
-    base = keep_ref[0] + got_ref[0].astype(F32)
-    if cols % LANES == 0:
-        for s in range(peers):
-            at = slice(s * cols, (s + 1) * cols)
-            o_ref[:, at] = (base[:, at] + own_ref[s].astype(F32)).astype(BF16)
-    else:
-        own = jnp.concatenate([own_ref[s].astype(F32) for s in range(peers)], axis=1)
-        o_ref[...] = (base + own).astype(BF16)
+def finish_kernel(*refs):
+    o_ref = refs[-1]
+    cols = o_ref.shape[1] // 2
+    for side in (0, 1):
+        keep_ref, got_ref = refs[2 * side : 2 * side + 2]
+        total = keep_ref[0] + got_ref[0].astype(F32)
+        o_ref[:, side * cols : (side + 1) * cols] = total.astype(BF16)
 
 
 def split_factor(count, most):
@@ -240,9 +246,9 @@
     plan = windows(width_f, peers)
     share, window, _, _ = plan
     half = peers // 2
-    slice_d = width_d // peers
-
-    scal = jnp.stack([own_shift(plan), me % 2]).astype(jnp.int32)
+
+    firsts = [me * local_slots, (me ^ 1) * local_slots]
+    scal = jnp.stack([own_shift(plan), me % 2] + firsts).astype(jnp.int32)
     smem = pl.BlockSpec(memory_space=pltpu.SMEM)
     vmem = pl.BlockSpec(memory_space=pltpu.VMEM)
     anywhere = pl.BlockSpec(memory_space=pl.ANY)
@@ -296,26 +302,18 @@
         name="base",
     )(scal, x, down_weight)
     pairs = lambda step: [(i, i ^ step) for i in range(peers)]
-
-    def halve(step, keep, got):
-        bit = ((me // step) % 2).astype(jnp.int32).reshape(1)
-        left = (keep.shape[0] // 2, row_dev, width_d)
-        return pl.pallas_call(
-            halve_kernel,
-            in_specs=[smem, vmem, vmem],
-            out_shape=(jax.ShapeDtypeStruct(left, F32), jax.ShapeDtypeStruct(left, BF16)),
-            compiler_params=params(60 if step == 2 else 16),
-            name="halve",
-        )(bit, keep, got)
-
-    got = lax.ppermute(send, "cols", pairs(1))
-    step = 2
-    if step < peers:
-        keep, send = halve(step, keep, got)
+    base = pl.pallas_call(
+        pair_kernel,
+        out_shape=jax.ShapeDtypeStruct(keep.shape, F32),
+        compiler_params=params(60),
+        name="pair",
+    )(keep, lax.ppermute(send, "cols", pairs(1)))
+    base, arrived = lax.optimization_barrier((base, arrived))
+    place = lax.dynamic_index_in_dim(place.reshape(half, 2, row_dev, 1), me % 2, 1, keepdims=False)
+    place = place.reshape(half * row_dev, 1)
 
     group = split_factor(count, 64)
-    aligned = slice_d % LANES == 0
-    shape = (peers, local_slots, slice_d) if aligned else (local_slots, width_d)
+    shape = (local_slots, width_d)
     chunks = local_var * (count // group)
     deltas = pl.pallas_call(
         functools.partial(delta_kernel, plan, d_blocks, group),
@@ -336,27 +334,55 @@
         ),
         name="delta",
     )(block_ids, arrived, delta_values)
-    if not aligned:
-        deltas = deltas.reshape(local_slots, peers, slice_d).transpose(1, 0, 2)
-    columns = lax.all_to_all(deltas, "cols", 0, 0)
-    while step < peers:
-        got = lax.ppermute(send, "cols", pairs(step))
-        step *= 2
-        if step < peers:
-            keep, send = halve(step, keep, got)
-    by_row = pl.pallas_call(
-        pick_kernel,
-        out_shape=jax.ShapeDtypeStruct((peers, row_dev, slice_d), BF16),
-        compiler_params=params(),
-        name="pick",
-    )(place, columns)
-    own = lax.all_to_all(by_row, "cols", 0, 0)
+    others = lax.ppermute(deltas, "cols", pairs(1))
+
+    cols = width_d // 2
+    above = [1 << k for k in range(1, peers.bit_length() - 1)]
+    ends = []
+    for side, order in enumerate((above, above[1:] + above[:1])):
+        open_bits = list(above)
+        for count, step in enumerate(order):
+            stride = 1 << open_bits.index(step)
+            open_bits.remove(step)
+            bit = ((me // step) % 2).astype(jnp.int32).reshape(1)
+            left = (half >> (count + 1), row_dev, cols)
+            outs = (jax.ShapeDtypeStruct(left, F32), jax.ShapeDtypeStruct(left, BF16))
+            if count == 0:
+                whole = lambda shape: pl.BlockSpec(shape, lambda i: (0,) * len(shape))
+                part = lambda shape, n=side: pl.BlockSpec(shape, lambda i: (0,) * (len(shape) - 1) + (n,))
+                keep, send = pl.pallas_call(
+                    functools.partial(join_kernel, stride),
+                    grid=(1,),
+                    in_specs=[
+                        smem,
+                        smem,
+                        part((half, row_dev, cols)),
+                        whole(place.shape),
+                        part((local_slots, cols)),
+                        part((local_slots, cols)),
+                    ],
+                    out_specs=(whole(left), whole(left)),
+                    out_shape=outs,
+                    scratch_shapes=[pltpu.VMEM((half, row_dev, cols), F32)],
+                    compiler_params=params(32),
+                    name="join",
+                )(scal, bit, base, place, deltas, others)
+            else:
+                keep, send = pl.pallas_call(
+                    functools.partial(halve_kernel, stride),
+                    in_specs=[smem, vmem, vmem],
+                    out_shape=outs,
+                    compiler_params=params(),
+                    name="halve",
+                )(bit, keep, got)
+            got = lax.ppermute(send, "cols", pairs(step))
+        ends += [keep, got]
     return pl.pallas_call(
         finish_kernel,
         out_shape=jax.ShapeDtypeStruct((row_dev, width_d), BF16),
         compiler_params=params(),
         name="finish",
-    )(keep, got, own)
+    )(*ends)
 
 
 def solution(mesh):

time: 98.7 us -> 96.7 us (0.980)
  starting transfers between devices: 29 us -> 22.6 us
  Pallas kernels: 24.6 us -> 27.6 us
  local copies, waits for them, and re-layouts: 1.35 us -> 4.34 us
  waiting for transfers between devices: 43.1 us -> 41.4 us
    all_to_all x2 -> x0, starting transfers between devices: 10.4 us -> none  [the longest x1 6.91 us: body(): columns = lax.all_to_all(deltas, 'cols', 0, 0)]
    all_to_all x2 -> x0, waiting for transfers between devices: 8.42 us -> none  [the longest x1 8.42 us: body(): columns = lax.all_to_all(deltas, 'cols', 0, 0)]
    ppermute x3 -> x6, waiting for transfers between devices: 9.5 us -> 14.8 us  [body(): got = lax.ppermute(send, 'cols', pairs(step))]
    pallas_call x4 -> x7, Pallas kernels: 4.23 us -> 8.05 us  [the longest x2 3.58 us: body(): pl.pallas_call(functools.partial(join_kernel, stride), grid=(1,), in_spec...]
    ppermute x3 -> x6, starting transfers between devices: 6.64 us -> 9.87 us  [body(): got = lax.ppermute(send, 'cols', pairs(step))]
    unnamed x6 -> x12, local copies, waits for them, and re-layouts: 1.35 us -> 4.15 us
    ppermute x1 -> x2, waiting for transfers between devices: 2.42 us -> 3.12 us  [the longest x1 2.29 us: body(): lax.ppermute(send, 'cols', pairs(1))]
  transfers between devices with their start and end apart: 8 -> 10, of which waited for: 5 -> 8; matrix products, arithmetic and copies ran while one was open for 0% -> 0% of each run, Pallas kernels for 20% -> 12%
where the time goes in v7:
time: 96.7 us; the launch traced here: 96.3 us
  waiting for transfers between devices  41.4 us (43%)
  Pallas kernels  27.6 us (29%)
  starting transfers between devices  22.6 us (23%)
  local copies, waits for them, and re-layouts  4.34 us (4%)
    ppermute x6, waiting for transfers between devices, body(): got = lax.ppermute(send, 'cols', pairs(step))  14.8 us
    all_to_all x1, waiting for transfers between devices, body(): x = lax.all_to_all(outgoing, 'cols', 0, 0)  14.4 us
    ppermute x6, starting transfers between devices, body(): got = lax.ppermute(send, 'cols', pairs(step))  9.87 us
    pallas_call x1, Pallas kernels, body(): pl.pallas_call(functools.partial(delta_kernel, plan, d_blocks, group), in...  9.27 us
    all_to_all x1, waiting for transfers between devices, body(): arrived = lax.all_to_all(slots, 'cols', 0, 0)  9.13 us
    all_to_all x1, starting transfers between devices, body(): x = lax.all_to_all(outgoing, 'cols', 0, 0)  7.4 us
    pallas_call x1, Pallas kernels, body(): pl.pallas_call(functools.partial(base_kernel, plan), in_specs=[smem, vmem...  5.43 us
    all_to_all x1, starting transfers between devices, body(): arrived = lax.all_to_all(slots, 'cols', 0, 0)  4.23 us
  transfers between devices with their start and end apart: 10, of which 8 were waited for; matrix products, arithmetic and copies ran while one was open for 0% of the time, Pallas kernels for 12%

profile of v7, /device:TPU:0, one launch (start us, length us, event | category | flops | bytes accessed | tf_op | source)
XLA Modules:
  0.0 96.3 jit_solution(4058727426563419701)
XLA Ops:
  0.0 1.9 %split_rows.1 = bf16[16,16,1024]{2,1,0:T(8,128)(2,1)} custom-call(bf16[16,14848]{1,0:T(8,128)(2,1)} %h_hbm.1, s32[1,16]{1,0:T(1,128)} %bitcast.9, s32[1,64]{1,0:T(1,128)} %bitcast.10), custom_call_target="tpu_custom_call" | custom-call | tf_op jit(solution)/shard_map/split_rows/pallas_call | solution.py:256
  1.9 7.4 %all-to-all-start = ((bf16[16,16,1024]{2,1,0:T(8,128)(2,1)}), bf16[16,16,1024]{2,1,0:T(8,128)(2,1)S(1)}, u32[]{:S(2)}, u32[]{:S(2)}) async-start(bf16[16,16,1024]{2,1,0:T(8,128)(2,1)} %split_rows.1), calls=%async_computation | async-start | bytes 1048576 | tf_op jit(solution)/shard_map/all_to_all | solution.py:269
  9.4 14.4 %all-to-all-done.x_ref = bf16[16,16,1024]{2,1,0:T(8,128)(2,1)S(1)} async-done(((bf16[16,16,1024]{2,1,0:T(8,128)(2,1)}), bf16[16,16,1024]{2,1,0:T(8,128)(2,1)S(1)}, u32[]{:S(2)}, u32[]{:S(2)}) %all-to-all-start) | async-done | bytes 524320 | tf_op jit(solution)/shard_map/all_to_all | solution.py:269
  23.8 2.3 %route.1 = (bf16[16,32,1024]{2,1,0:T(8,128)(2,1)}, s32[256,1]{1,0:T(8,128)S(1)}) custom-call(s32[4]{0:T(128)S(1)} %pad_add_fusion.shift_ref.scal_ref, bf16[16,16,1024]{2,1,0:T(8,128)(2,1)S(1)} %all-to-all-done.x_ref), custom_call_target="tpu_custom_call" | custom-call | tf_op jit(solution)/shard_map/route/pallas_call | solution.py:271
  26.1 4.2 %all-to-all-start.1 = ((bf16[16,32,1024]{2,1,0:T(8,128)(2,1)}), bf16[16,32,1024]{2,1,0:T(8,128)(2,1)S(1)}, u32[]{:S(2)}, u32[]{:S(2)}) async-start(bf16[16,32,1024]{2,1,0:T(8,128)(2,1)} %get-tuple-element.29), calls=%async_computation.1 | async-start | bytes 2097152 | tf_op jit(solution)/shard_map/all_to_all | solution.py:281
  30.3 5.4 %base.1 = (f32[8,16,4096]{2,1,0:T(8,128)S(1)}, bf16[8,16,4096]{2,1,0:T(8,128)(2,1)S(1)}) custom-call(s32[4]{0:T(128)S(1)} %pad_add_fusion.shift_ref.scal_ref, bf16[16,16,1024]{2,1,0:T(8,128)(2,1)S(1)} %all-to-all-done.x_ref, bf16[928,4096]{1,0:T(8,128)(2,1)} %w_hbm.1), custom_call_target="tpu_custom_call" | custom-call | flops 1946157056 | bytes 7602176 | tf_op jit(solution)/shard_map/base/pallas_call | solution.py:286
  35.8 1.3 %copy-done.1 = f32[8,16,4096]{2,1,0:T(8,128)} copy-done((f32[8,16,4096]{2,1,0:T(8,128)}, f32[8,16,4096]{2,1,0:T(8,128)S(1)}, u32[]{:S(2)}) %copy-start.1) | copy-done | bytes 2097176
  37.1 0.4 collective-permute-start
  37.5 2.3 %collective-permute-done.got_ref = bf16[8,16,4096]{2,1,0:T(8,128)(2,1)S(1)} collective-permute-done((bf16[8,16,4096]{2,1,0:T(8,128)(2,1)S(1)}, bf16[8,16,4096]{2,1,0:T(8,128)(2,1)S(1)}, u32[]{:S(2)}, u32[]{:S(2)}) %collective-permute-start) | collective-permute-done | bytes 1048608 | tf_op jit(solution)/shard_map/ppermute | solution.py:310
  39.8 1.0 %copy-done.5 = bf16[8,16,4096]{2,1,0:T(8,128)(2,1)} copy-done((bf16[8,16,4096]{2,1,0:T(8,128)(2,1)}, bf16[8,16,4096]{2,1,0:T(8,128)(2,1)S(1)}, u32[]{:S(2)}) %copy-start.5) | copy-done | bytes 1048600
  40.8 3.4 %pair.1.base_ref = f32[8,16,4096]{2,1,0:T(8,128)} custom-call(f32[8,16,4096]{2,1,0:T(8,128)} %copy-done.1, bf16[8,16,4096]{2,1,0:T(8,128)(2,1)} %copy-done.5), custom_call_target="tpu_custom_call" | custom-call | tf_op jit(solution)/shard_map/pair/pallas_call | solution.py:305
  44.2 9.1 %all-to-all-done.1.x_ref = bf16[16,32,1024]{2,1,0:T(8,128)(2,1)S(1)} async-done(((bf16[16,32,1024]{2,1,0:T(8,128)(2,1)}), bf16[16,32,1024]{2,1,0:T(8,128)(2,1)S(1)}, u32[]{:S(2)}, u32[]{:S(2)}) %all-to-all-start.1) | async-done | bytes 1048608 | tf_op jit(solution)/shard_map/all_to_all | solution.py:281
  53.3 9.3 %delta.1.own_ref = bf16[32,4096]{1,0:T(8,128)(2,1)S(1)} custom-call(s32[4,186]{1,0:T(4,128)S(1)} %copy-done.4, bf16[16,32,1024]{2,1,0:T(8,128)(2,1)S(1)} %all-to-all-done.1.x_ref, bf16[4,186,128,128]{3,2,1,0:T(8,128)(2,1)} %v_hbm.1), custom_call_target="tpu_custom_call" | custom-call | flops 195035136 | bytes 24379392 | tf_op jit(solution)/shard_map/delta/pallas_call | solution.py:318
  62.6 0.7 collective-permute-start.1
  63.2 0.1 reduce
  63.3 0.1 reshape.30
  63.6 0.8 collective-permute-done.1.got_ref
  64.4 1.8 %join.3 = (f32[4,16,2048]{2,1,0:T(8,128)S(1)}, bf16[4,16,2048]{2,1,0:T(8,128)(2,1)}) custom-call(s32[4]{0:T(128)S(1)} %pad_add_fusion.shift_ref.scal_ref, s32[1]{0:T(128)} %bitcast.1.bit_ref, f32[8,16,4096]{2,1,0:T(8,128)S(1)} %copy-done, s32[128,1]{1,0:T(8,128)S(1)} %reshape.32.place_ref, bf16[32,4096]{1,0:T(8,128)(2,1)S(1)} %delta.1.own_ref, ...), custom_call_target="tpu_custom_call" | custom-call | tf_op jit(solution)/shard_map/join/pallas_call | solution.py:353
  66.2 0.8 copy-done.2
  67.0 3.4 %collective-permute-start.5 = (bf16[4,16,2048]{2,1,0:T(8,128)(2,1)}, bf16[4,16,2048]{2,1,0:T(8,128)(2,1)}, u32[]{:S(2)}, u32[]{:S(2)}) collective-permute-start(bf16[4,16,2048]{2,1,0:T(8,128)(2,1)} %get-tuple-element.40), channel_id=1, source_target_pairs={{0,4},{1,5},{2,6},{3,7},{4,0},{5,1},{6,2},{7,3},{8,12},{9,13},{10,... | collective-permute-start | bytes 786440 | tf_op jit(solution)/shard_map/ppermute | solution.py:378
  70.4 1.8 %join.2 = (f32[4,16,2048]{2,1,0:T(8,128)S(1)}, bf16[4,16,2048]{2,1,0:T(8,128)(2,1)}) custom-call(s32[4]{0:T(128)S(1)} %pad_add_fusion.shift_ref.scal_ref, s32[1]{0:T(128)} %bitcast.6.bit_ref, f32[8,16,4096]{2,1,0:T(8,128)S(1)} %copy-done, s32[128,1]{1,0:T(8,128)S(1)} %reshape.32.place_ref, bf16[32,4096]{1,0:T(8,128)(2,1)S(1)} %delta.1.own_ref, ...), custom_call_target="tpu_custom_call" | custom-call | tf_op jit(solution)/shard_map/join/pallas_call | solution.py:353
  72.2 1.6 %collective-permute-start.2 = (bf16[4,16,2048]{2,1,0:T(8,128)(2,1)}, bf16[4,16,2048]{2,1,0:T(8,128)(2,1)S(1)}, u32[]{:S(2)}, u32[]{:S(2)}) collective-permute-start(bf16[4,16,2048]{2,1,0:T(8,128)(2,1)} %get-tuple-element.34), channel_id=1, source_target_pairs={{0,2},{1,3},{2,0},{3,1},{4,6},{5,7},{6,4},{7,5},{8,10},{9,11},{10,... | collective-permute-start | bytes 786440 | tf_op jit(solution)/shard_map/ppermute | solution.py:378
  73.7 3.8 %collective-permute-done.5.got_ref = bf16[4,16,2048]{2,1,0:T(8,128)(2,1)} collective-permute-done((bf16[4,16,2048]{2,1,0:T(8,128)(2,1)}, bf16[4,16,2048]{2,1,0:T(8,128)(2,1)}, u32[]{:S(2)}, u32[]{:S(2)}) %collective-permute-start.5) | collective-permute-done | bytes 262176 | tf_op jit(solution)/shard_map/ppermute | solution.py:378
  77.5 1.0 %copy-done.3 = f32[4,16,2048]{2,1,0:T(8,128)S(1)} copy-done((f32[4,16,2048]{2,1,0:T(8,128)S(1)}, f32[4,16,2048]{2,1,0:T(8,128)}, u32[]{:S(2)}) %copy-start.3) | copy-done | bytes 524312
  78.6 1.0 %halve.6 = (f32[2,16,2048]{2,1,0:T(8,128)S(1)}, bf16[2,16,2048]{2,1,0:T(8,128)(2,1)S(1)}) custom-call(s32[1]{0:T(128)} %bitcast.bit_ref, f32[4,16,2048]{2,1,0:T(8,128)S(1)} %copy-done.3, bf16[4,16,2048]{2,1,0:T(8,128)(2,1)} %collective-permute-done.5.got_ref), custom_call_target="tpu_custom_call" | custom-call | tf_op jit(solution)/shard_map/halve/pallas_call | solution.py:371
  79.6 3.0 %collective-permute-start.6 = (bf16[2,16,2048]{2,1,0:T(8,128)(2,1)S(1)}, bf16[2,16,2048]{2,1,0:T(8,128)(2,1)S(1)}, u32[]{:S(2)}, u32[]{:S(2)}) collective-permute-start(bf16[2,16,2048]{2,1,0:T(8,128)(2,1)S(1)} %get-tuple-element.42), channel_id=1, source_target_pairs={{0,8},{1,9},{2,10},{3,11},{4,12},{5,13},{6,14},{7,15},{8,0},{9,1},... | collective-permute-start | bytes 393224 | tf_op jit(solution)/shard_map/ppermute | solution.py:378
  82.6 0.3 collective-permute-start.3
  83.0 5.6 %collective-permute-done.6.got_ref = bf16[2,16,2048]{2,1,0:T(8,128)(2,1)S(1)} collective-permute-done((bf16[2,16,2048]{2,1,0:T(8,128)(2,1)S(1)}, bf16[2,16,2048]{2,1,0:T(8,128)(2,1)S(1)}, u32[]{:S(2)}, u32[]{:S(2)}) %collective-permute-start.6) | collective-permute-done | bytes 131104 | tf_op jit(solution)/shard_map/ppermute | solution.py:378
  88.7 1.5 %collective-permute-start.7 = (bf16[1,16,2048]{2,1,0:T(8,128)(2,1)S(1)}, bf16[1,16,2048]{2,1,0:T(8,128)(2,1)S(1)}, u32[]{:S(2)}, u32[]{:S(2)}) collective-permute-start(bf16[1,16,2048]{2,1,0:T(8,128)(2,1)S(1)} %get-tuple-element.44), channel_id=1, source_target_pairs={{0,2},{1,3},{2,0},{3,1},{4,6},{5,7},{6,4},{7,5},{8,10},{9,11},{10,... | collective-permute-start | bytes 196616 | tf_op jit(solution)/shard_map/ppermute | solution.py:378
  90.2 2.7 %collective-permute-done.7.refs_3_ = bf16[1,16,2048]{2,1,0:T(8,128)(2,1)S(1)} collective-permute-done((bf16[1,16,2048]{2,1,0:T(8,128)(2,1)S(1)}, bf16[1,16,2048]{2,1,0:T(8,128)(2,1)S(1)}, u32[]{:S(2)}, u32[]{:S(2)}) %collective-permute-start.7) | collective-permute-done | bytes 65568 | tf_op jit(solution)/shard_map/ppermute | solution.py:378
  93.0 2.6 %collective-permute-done.4.refs_1_ = bf16[1,16,2048]{2,1,0:T(8,128)(2,1)S(1)} collective-permute-done((bf16[1,16,2048]{2,1,0:T(8,128)(2,1)S(1)}, bf16[1,16,2048]{2,1,0:T(8,128)(2,1)S(1)}, u32[]{:S(2)}, u32[]{:S(2)}) %collective-permute-start.4) | collective-permute-done | bytes 65568 | tf_op jit(solution)/shard_map/ppermute | solution.py:378
  95.6 0.7 finish.1
  (17 shorter events, 0.4 us)
Async XLA Ops:
  1.9 21.9 %all-to-all-start = ((bf16[16,16,1024]{2,1,0:T(8,128)(2,1)}), bf16[16,16,1024]{2,1,0:T(8,128)(2,1)S(1)}, u32[]{:S(2)}, u32[]{:S(2)}) async-start(bf16[16,16,1024]{2,1,0:T(8,128)(2,1)} %split_rows.1), calls=%async_computation | async-start | bytes 1048576 | tf_op jit(solution)/shard_map/all_to_all | solution.py:269
  26.1 27.2 %copy-start.4 = (s32[4,186]{1,0:T(4,128)S(1)}, s32[4,186]{1,0:T(4,128)}, u32[]{:S(2)}) copy-start(s32[4,186]{1,0:T(4,128)} %ids_ref.1) | copy-start | bytes 8932
  26.1 27.2 %all-to-all-start.1 = ((bf16[16,32,1024]{2,1,0:T(8,128)(2,1)}), bf16[16,32,1024]{2,1,0:T(8,128)(2,1)S(1)}, u32[]{:S(2)}, u32[]{:S(2)}) async-start(bf16[16,32,1024]{2,1,0:T(8,128)(2,1)} %get-tuple-element.29), calls=%async_computation.1 | async-start | bytes 2097152 | tf_op jit(solution)/shard_map/all_to_all | solution.py:281
  35.8 1.3 %copy-start.1 = (f32[8,16,4096]{2,1,0:T(8,128)}, f32[8,16,4096]{2,1,0:T(8,128)S(1)}, u32[]{:S(2)}) copy-start(f32[8,16,4096]{2,1,0:T(8,128)S(1)} %get-tuple-element.27.keep_ref) | copy-start | bytes 6291460
  37.1 2.7 %collective-permute-start = (bf16[8,16,4096]{2,1,0:T(8,128)(2,1)S(1)}, bf16[8,16,4096]{2,1,0:T(8,128)(2,1)S(1)}, u32[]{:S(2)}, u32[]{:S(2)}) collective-permute-start(bf16[8,16,4096]{2,1,0:T(8,128)(2,1)S(1)} %get-tuple-element.28), channel_id=1, source_target_pairs={{0,1},{1,0},{2,3},{3,2},{4,5},{5,4},{6,7},{7,6},{8,9},{9,8},{10,11... | collective-permute-start | bytes 3145736 | tf_op jit(solution)/shard_map/ppermute | solution.py:310
  39.8 1.0 %copy-start.5 = (bf16[8,16,4096]{2,1,0:T(8,128)(2,1)}, bf16[8,16,4096]{2,1,0:T(8,128)(2,1)S(1)}, u32[]{:S(2)}) copy-start(bf16[8,16,4096]{2,1,0:T(8,128)(2,1)S(1)} %collective-permute-done.got_ref) | copy-start | bytes 3145732
  44.2 20.3 %copy-start = (f32[8,16,4096]{2,1,0:T(8,128)S(1)}, f32[8,16,4096]{2,1,0:T(8,128)}, u32[]{:S(2)}) copy-start(f32[8,16,4096]{2,1,0:T(8,128)} %pair.1.base_ref) | copy-start | bytes 6291460
  62.6 1.8 %collective-permute-start.1 = (bf16[32,4096]{1,0:T(8,128)(2,1)S(1)}, bf16[32,4096]{1,0:T(8,128)(2,1)S(1)}, u32[]{:S(2)}, u32[]{:S(2)}) collective-permute-start(bf16[32,4096]{1,0:T(8,128)(2,1)S(1)} %delta.1.own_ref), channel_id=1, source_target_pairs={{0,1},{1,0},{2,3},{3,2},{4,5},{5,4},{6,7},{7,6},{8,9},{9,8},{10,11... | collective-permute-start | bytes 786440 | tf_op jit(solution)/shard_map/ppermute | solution.py:337
  66.2 0.8 copy-start.2
  67.0 10.5 %collective-permute-start.5 = (bf16[4,16,2048]{2,1,0:T(8,128)(2,1)}, bf16[4,16,2048]{2,1,0:T(8,128)(2,1)}, u32[]{:S(2)}, u32[]{:S(2)}) collective-permute-start(bf16[4,16,2048]{2,1,0:T(8,128)(2,1)} %get-tuple-element.40), channel_id=1, source_target_pairs={{0,4},{1,5},{2,6},{3,7},{4,0},{5,1},{6,2},{7,3},{8,12},{9,13},{10,... | collective-permute-start | bytes 786440 | tf_op jit(solution)/shard_map/ppermute | solution.py:378
  72.2 10.4 %collective-permute-start.2 = (bf16[4,16,2048]{2,1,0:T(8,128)(2,1)}, bf16[4,16,2048]{2,1,0:T(8,128)(2,1)S(1)}, u32[]{:S(2)}, u32[]{:S(2)}) collective-permute-start(bf16[4,16,2048]{2,1,0:T(8,128)(2,1)} %get-tuple-element.34), channel_id=1, source_target_pairs={{0,2},{1,3},{2,0},{3,1},{4,6},{5,7},{6,4},{7,5},{8,10},{9,11},{10,... | collective-permute-start | bytes 786440 | tf_op jit(solution)/shard_map/ppermute | solution.py:378
  77.5 1.0 %copy-start.3 = (f32[4,16,2048]{2,1,0:T(8,128)S(1)}, f32[4,16,2048]{2,1,0:T(8,128)}, u32[]{:S(2)}) copy-start(f32[4,16,2048]{2,1,0:T(8,128)} %copy-done.2) | copy-start | bytes 1572868
  79.6 9.1 %collective-permute-start.6 = (bf16[2,16,2048]{2,1,0:T(8,128)(2,1)S(1)}, bf16[2,16,2048]{2,1,0:T(8,128)(2,1)S(1)}, u32[]{:S(2)}, u32[]{:S(2)}) collective-permute-start(bf16[2,16,2048]{2,1,0:T(8,128)(2,1)S(1)} %get-tuple-element.42), channel_id=1, source_target_pairs={{0,8},{1,9},{2,10},{3,11},{4,12},{5,13},{6,14},{7,15},{8,0},{9,1},... | collective-permute-start | bytes 393224 | tf_op jit(solution)/shard_map/ppermute | solution.py:378
  82.6 7.5 %collective-permute-start.3 = (bf16[2,16,2048]{2,1,0:T(8,128)(2,1)S(1)}, bf16[2,16,2048]{2,1,0:T(8,128)(2,1)S(1)}, u32[]{:S(2)}, u32[]{:S(2)}) collective-permute-start(bf16[2,16,2048]{2,1,0:T(8,128)(2,1)S(1)} %get-tuple-element.36), channel_id=1, source_target_pairs={{0,4},{1,5},{2,6},{3,7},{4,0},{5,1},{6,2},{7,3},{8,12},{9,13},{10,... | collective-permute-start | bytes 393224 | tf_op jit(solution)/shard_map/ppermute | solution.py:378
  88.7 4.3 %collective-permute-start.7 = (bf16[1,16,2048]{2,1,0:T(8,128)(2,1)S(1)}, bf16[1,16,2048]{2,1,0:T(8,128)(2,1)S(1)}, u32[]{:S(2)}, u32[]{:S(2)}) collective-permute-start(bf16[1,16,2048]{2,1,0:T(8,128)(2,1)S(1)} %get-tuple-element.44), channel_id=1, source_target_pairs={{0,2},{1,3},{2,0},{3,1},{4,6},{5,7},{6,4},{7,5},{8,10},{9,11},{10,... | collective-permute-start | bytes 196616 | tf_op jit(solution)/shard_map/ppermute | solution.py:378
  90.2 5.4 %collective-permute-start.4 = (bf16[1,16,2048]{2,1,0:T(8,128)(2,1)S(1)}, bf16[1,16,2048]{2,1,0:T(8,128)(2,1)S(1)}, u32[]{:S(2)}, u32[]{:S(2)}) collective-permute-start(bf16[1,16,2048]{2,1,0:T(8,128)(2,1)S(1)} %get-tuple-element.38), channel_id=1, source_target_pairs={{0,8},{1,9},{2,10},{3,11},{4,12},{5,13},{6,14},{7,15},{8,0},{9,1},... | collective-permute-start | bytes 196616 | tf_op jit(solution)/shard_map/ppermute | solution.py:378

commit v8 on v7

--- a/solution.py
+++ b/solution.py
@@ -190,18 +190,21 @@
     o_ref[...] = keep_ref[...] + got_ref[...].astype(F32)
 
 
-def join_kernel(stride, scal_ref, bit_ref, base_ref, place_ref, own_ref, got_ref, *rest):
+def join_kernel(stride, first, scal_ref, bit_ref, base_ref, place_ref, own_ref, got_ref, *rest):
     next_ref, send_ref, sum_ref = rest
     rows = place_ref.shape[0]
-    slots, cols = own_ref.shape
+    slots = own_ref.shape[0]
+    cols = next_ref.shape[2]
     lane = lane_iota(rows, slots)
-    for source, (first, d_ref) in enumerate(((scal_ref[2], own_ref), (scal_ref[3], got_ref))):
-        pick = jnp.where(place_ref[...] - first == lane, 1.0, 0.0).astype(BF16)
-        part = jnp.dot(pick, d_ref[...], preferred_element_type=F32).reshape(sum_ref.shape)
-        if source == 0:
-            sum_ref[...] = base_ref[...] + part
-        else:
-            sum_ref[...] += part
+    picks = [place_ref[...] - scal_ref[k] == lane for k in (2, 3)]
+    picks = [jnp.where(pick, 1.0, 0.0).astype(BF16) for pick in picks]
+    step = cols // (cols // 512) if cols % 512 == 0 else cols
+    for c in range(0, cols, step):
+        at = slice(first + c, first + c + step)
+        part = jnp.dot(picks[0], own_ref[:, at], preferred_element_type=F32)
+        part += jnp.dot(picks[1], got_ref[:, at], preferred_element_type=F32)
+        part = part.reshape(sum_ref.shape[:2] + (step,))
+        sum_ref[:, :, c : c + step] = base_ref[:, :, at] + part
     bit = bit_ref[0]
     for q in range(next_ref.shape[0]):
         at = q // stride * 2 * stride + q % stride
@@ -220,11 +223,13 @@
 
 def finish_kernel(*refs):
     o_ref = refs[-1]
-    cols = o_ref.shape[1] // 2
+    first = 0
     for side in (0, 1):
         keep_ref, got_ref = refs[2 * side : 2 * side + 2]
+        cols = keep_ref.shape[2]
         total = keep_ref[0] + got_ref[0].astype(F32)
-        o_ref[:, side * cols : (side + 1) * cols] = total.astype(BF16)
+        o_ref[:, first : first + cols] = total.astype(BF16)
+        first += cols
 
 
 def split_factor(count, most):
@@ -336,10 +341,12 @@
     )(block_ids, arrived, delta_values)
     others = lax.ppermute(deltas, "cols", pairs(1))
 
-    cols = width_d // 2
+    tile = width_d // 8
     above = [1 << k for k in range(1, peers.bit_length() - 1)]
     ends = []
     for side, order in enumerate((above, above[1:] + above[:1])):
+        first, tiles = ((0, 5), (5, 8 - 5))[side]
+        cols = tiles * tile
         open_bits = list(above)
         for count, step in enumerate(order):
             stride = 1 << open_bits.index(step)
@@ -348,23 +355,12 @@
             left = (half >> (count + 1), row_dev, cols)
             outs = (jax.ShapeDtypeStruct(left, F32), jax.ShapeDtypeStruct(left, BF16))
             if count == 0:
-                whole = lambda shape: pl.BlockSpec(shape, lambda i: (0,) * len(shape))
-                part = lambda shape, n=side: pl.BlockSpec(shape, lambda i: (0,) * (len(shape) - 1) + (n,))
                 keep, send = pl.pallas_call(
-                    functools.partial(join_kernel, stride),
-                    grid=(1,),
-                    in_specs=[
-                        smem,
-                        smem,
-                        part((half, row_dev, cols)),
-                        whole(place.shape),
-                        part((local_slots, cols)),
-                        part((local_slots, cols)),
-                    ],
-                    out_specs=(whole(left), whole(left)),
+                    functools.partial(join_kernel, stride, first * tile),
+                    in_specs=[smem, smem, vmem, vmem, vmem, vmem],
                     out_shape=outs,
                     scratch_shapes=[pltpu.VMEM((half, row_dev, cols), F32)],
-                    compiler_params=params(32),
+                    compiler_params=params(12),
                     name="join",
                 )(scal, bit, base, place, deltas, others)
             else:

time: 96.7 us -> 96 us (level)
  waiting for transfers between devices: 41.4 us -> 36 us
  starting transfers between devices: 22.6 us -> 27.3 us
    ppermute x6, waiting for transfers between devices: 14.8 us -> 9.41 us  [body(): got = lax.ppermute(send, 'cols', pairs(step))]
    ppermute x6, starting transfers between devices: 9.87 us -> 14.6 us  [body(): got = lax.ppermute(send, 'cols', pairs(step))]
where the time goes in v8:
time: 96 us; the launch traced here: 95.5 us
  waiting for transfers between devices  36 us (38%)
  Pallas kernels  27.7 us (29%)
  starting transfers between devices  27.3 us (28%)
  local copies, waits for them, and re-layouts  4.26 us (4%)
    ppermute x6, starting transfers between devices, body(): got = lax.ppermute(send, 'cols', pairs(step))  14.6 us
    all_to_all x1, waiting for transfers between devices, body(): x = lax.all_to_all(outgoing, 'cols', 0, 0)  14.4 us
    ppermute x6, waiting for transfers between devices, body(): got = lax.ppermute(send, 'cols', pairs(step))  9.41 us
    pallas_call x1, Pallas kernels, body(): pl.pallas_call(functools.partial(delta_kernel, plan, d_blocks, group), in...  9.27 us
    all_to_all x1, waiting for transfers between devices, body(): arrived = lax.all_to_all(slots, 'cols', 0, 0)  9.13 us
    all_to_all x1, starting transfers between devices, body(): x = lax.all_to_all(outgoing, 'cols', 0, 0)  7.4 us
    pallas_call x1, Pallas kernels, body(): pl.pallas_call(functools.partial(base_kernel, plan), in_specs=[smem, vmem...  5.43 us
    all_to_all x1, starting transfers between devices, body(): arrived = lax.all_to_all(slots, 'cols', 0, 0)  4.23 us
  transfers between devices with their start and end apart: 10, of which 8 were waited for; matrix products, arithmetic and copies ran while one was open for 0% of the time, Pallas kernels for 12%

profile of v8, /device:TPU:0, one launch (start us, length us, event | category | flops | bytes accessed | tf_op | source)
XLA Modules:
  0.0 95.5 jit_solution(8721999687478718055)
XLA Ops:
  0.0 1.9 %split_rows.1 = bf16[16,16,1024]{2,1,0:T(8,128)(2,1)} custom-call(bf16[16,14848]{1,0:T(8,128)(2,1)} %h_hbm.1, s32[1,16]{1,0:T(1,128)} %bitcast.9, s32[1,64]{1,0:T(1,128)} %bitcast.10), custom_call_target="tpu_custom_call" | custom-call | tf_op jit(solution)/shard_map/split_rows/pallas_call | solution.py:261
  1.9 7.4 %all-to-all-start = ((bf16[16,16,1024]{2,1,0:T(8,128)(2,1)}), bf16[16,16,1024]{2,1,0:T(8,128)(2,1)S(1)}, u32[]{:S(2)}, u32[]{:S(2)}) async-start(bf16[16,16,1024]{2,1,0:T(8,128)(2,1)} %split_rows.1), calls=%async_computation | async-start | bytes 1048576 | tf_op jit(solution)/shard_map/all_to_all | solution.py:274
  9.4 14.4 %all-to-all-done.x_ref = bf16[16,16,1024]{2,1,0:T(8,128)(2,1)S(1)} async-done(((bf16[16,16,1024]{2,1,0:T(8,128)(2,1)}), bf16[16,16,1024]{2,1,0:T(8,128)(2,1)S(1)}, u32[]{:S(2)}, u32[]{:S(2)}) %all-to-all-start) | async-done | bytes 524320 | tf_op jit(solution)/shard_map/all_to_all | solution.py:274
  23.8 2.3 %route.1 = (bf16[16,32,1024]{2,1,0:T(8,128)(2,1)}, s32[256,1]{1,0:T(8,128)S(1)}) custom-call(s32[4]{0:T(128)S(1)} %pad_add_fusion.shift_ref.scal_ref, bf16[16,16,1024]{2,1,0:T(8,128)(2,1)S(1)} %all-to-all-done.x_ref), custom_call_target="tpu_custom_call" | custom-call | tf_op jit(solution)/shard_map/route/pallas_call | solution.py:276
  26.1 4.2 %all-to-all-start.1 = ((bf16[16,32,1024]{2,1,0:T(8,128)(2,1)}), bf16[16,32,1024]{2,1,0:T(8,128)(2,1)S(1)}, u32[]{:S(2)}, u32[]{:S(2)}) async-start(bf16[16,32,1024]{2,1,0:T(8,128)(2,1)} %get-tuple-element.29), calls=%async_computation.1 | async-start | bytes 2097152 | tf_op jit(solution)/shard_map/all_to_all | solution.py:286
  30.3 5.4 %base.1 = (f32[8,16,4096]{2,1,0:T(8,128)S(1)}, bf16[8,16,4096]{2,1,0:T(8,128)(2,1)S(1)}) custom-call(s32[4]{0:T(128)S(1)} %pad_add_fusion.shift_ref.scal_ref, bf16[16,16,1024]{2,1,0:T(8,128)(2,1)S(1)} %all-to-all-done.x_ref, bf16[928,4096]{1,0:T(8,128)(2,1)} %w_hbm.1), custom_call_target="tpu_custom_call" | custom-call | flops 1946157056 | bytes 7602176 | tf_op jit(solution)/shard_map/base/pallas_call | solution.py:291
  35.8 1.3 %copy-done.1 = f32[8,16,4096]{2,1,0:T(8,128)} copy-done((f32[8,16,4096]{2,1,0:T(8,128)}, f32[8,16,4096]{2,1,0:T(8,128)S(1)}, u32[]{:S(2)}) %copy-start.1) | copy-done | bytes 2097176
  37.1 0.4 collective-permute-start
  37.5 2.3 %collective-permute-done.got_ref = bf16[8,16,4096]{2,1,0:T(8,128)(2,1)S(1)} collective-permute-done((bf16[8,16,4096]{2,1,0:T(8,128)(2,1)S(1)}, bf16[8,16,4096]{2,1,0:T(8,128)(2,1)S(1)}, u32[]{:S(2)}, u32[]{:S(2)}) %collective-permute-start) | collective-permute-done | bytes 1048608 | tf_op jit(solution)/shard_map/ppermute | solution.py:315
  39.8 1.0 %copy-done.5 = bf16[8,16,4096]{2,1,0:T(8,128)(2,1)} copy-done((bf16[8,16,4096]{2,1,0:T(8,128)(2,1)}, bf16[8,16,4096]{2,1,0:T(8,128)(2,1)S(1)}, u32[]{:S(2)}) %copy-start.5) | copy-done | bytes 1048600
  40.8 3.4 %pair.1.base_ref = f32[8,16,4096]{2,1,0:T(8,128)} custom-call(f32[8,16,4096]{2,1,0:T(8,128)} %copy-done.1, bf16[8,16,4096]{2,1,0:T(8,128)(2,1)} %copy-done.5), custom_call_target="tpu_custom_call" | custom-call | tf_op jit(solution)/shard_map/pair/pallas_call | solution.py:310
  44.2 9.1 %all-to-all-done.1.x_ref = bf16[16,32,1024]{2,1,0:T(8,128)(2,1)S(1)} async-done(((bf16[16,32,1024]{2,1,0:T(8,128)(2,1)}), bf16[16,32,1024]{2,1,0:T(8,128)(2,1)S(1)}, u32[]{:S(2)}, u32[]{:S(2)}) %all-to-all-start.1) | async-done | bytes 1048608 | tf_op jit(solution)/shard_map/all_to_all | solution.py:286
  53.3 9.3 %delta.1.own_ref = bf16[32,4096]{1,0:T(8,128)(2,1)S(1)} custom-call(s32[4,186]{1,0:T(4,128)S(1)} %copy-done.4, bf16[16,32,1024]{2,1,0:T(8,128)(2,1)S(1)} %all-to-all-done.1.x_ref, bf16[4,186,128,128]{3,2,1,0:T(8,128)(2,1)} %v_hbm.1), custom_call_target="tpu_custom_call" | custom-call | flops 195035136 | bytes 24379392 | tf_op jit(solution)/shard_map/delta/pallas_call | solution.py:323
  62.6 0.7 collective-permute-start.1
  63.2 0.1 reduce
  63.6 0.8 collective-permute-done.1.got_ref
  64.4 1.9 %join.2 = (f32[4,16,2560]{2,1,0:T(8,128)S(1)}, bf16[4,16,2560]{2,1,0:T(8,128)(2,1)}) custom-call(s32[4]{0:T(128)S(1)} %pad_add_fusion.shift_ref.scal_ref, s32[1]{0:T(128)} %bitcast.6.bit_ref, f32[8,16,4096]{2,1,0:T(8,128)S(1)} %copy-done, s32[128,1]{1,0:T(8,128)S(1)} %reshape.32.place_ref, bf16[32,4096]{1,0:T(8,128)(2,1)S(1)} %delta.1.own_ref, ...), custom_call_target="tpu_custom_call" | custom-call | tf_op jit(solution)/shard_map/join/pallas_call | solution.py:358
  66.3 2.0 %collective-permute-start.2 = (bf16[4,16,2560]{2,1,0:T(8,128)(2,1)}, bf16[4,16,2560]{2,1,0:T(8,128)(2,1)}, u32[]{:S(2)}, u32[]{:S(2)}) collective-permute-start(bf16[4,16,2560]{2,1,0:T(8,128)(2,1)} %get-tuple-element.34), channel_id=1, source_target_pairs={{0,2},{1,3},{2,0},{3,1},{4,6},{5,7},{6,4},{7,5},{8,10},{9,11},{10,... | collective-permute-start | bytes 983048 | tf_op jit(solution)/shard_map/ppermute | solution.py:374
  68.3 1.7 %join.3 = (f32[4,16,1536]{2,1,0:T(8,128)S(1)}, bf16[4,16,1536]{2,1,0:T(8,128)(2,1)}) custom-call(s32[4]{0:T(128)S(1)} %pad_add_fusion.shift_ref.scal_ref, s32[1]{0:T(128)} %bitcast.1.bit_ref, f32[8,16,4096]{2,1,0:T(8,128)S(1)} %copy-done, s32[128,1]{1,0:T(8,128)S(1)} %reshape.32.place_ref, bf16[32,4096]{1,0:T(8,128)(2,1)S(1)} %delta.1.own_ref, ...), custom_call_target="tpu_custom_call" | custom-call | tf_op jit(solution)/shard_map/join/pallas_call | solution.py:358
  70.0 0.8 copy-done.2
  70.7 3.0 %collective-permute-start.5 = (bf16[4,16,1536]{2,1,0:T(8,128)(2,1)}, bf16[4,16,1536]{2,1,0:T(8,128)(2,1)S(1)}, u32[]{:S(2)}, u32[]{:S(2)}) collective-permute-start(bf16[4,16,1536]{2,1,0:T(8,128)(2,1)} %get-tuple-element.40), channel_id=1, source_target_pairs={{0,4},{1,5},{2,6},{3,7},{4,0},{5,1},{6,2},{7,3},{8,12},{9,13},{10,... | collective-permute-start | bytes 589832 | tf_op jit(solution)/shard_map/ppermute | solution.py:374
  73.7 3.1 %collective-permute-done.2.got_ref = bf16[4,16,2560]{2,1,0:T(8,128)(2,1)} collective-permute-done((bf16[4,16,2560]{2,1,0:T(8,128)(2,1)}, bf16[4,16,2560]{2,1,0:T(8,128)(2,1)}, u32[]{:S(2)}, u32[]{:S(2)}) %collective-permute-start.2) | collective-permute-done | bytes 327712 | tf_op jit(solution)/shard_map/ppermute | solution.py:374
  76.8 1.0 %halve.4 = (f32[2,16,2560]{2,1,0:T(8,128)S(1)}, bf16[2,16,2560]{2,1,0:T(8,128)(2,1)S(1)}) custom-call(s32[1]{0:T(128)} %bitcast.1.bit_ref, f32[4,16,2560]{2,1,0:T(8,128)S(1)} %get-tuple-element.33.keep_ref, bf16[4,16,2560]{2,1,0:T(8,128)(2,1)} %collective-permute-done.2.got_ref), custom_call_target="tpu_custom_call" | custom-call | tf_op jit(solution)/shard_map/halve/pallas_call | solution.py:367
  77.9 3.2 %collective-permute-start.3 = (bf16[2,16,2560]{2,1,0:T(8,128)(2,1)S(1)}, bf16[2,16,2560]{2,1,0:T(8,128)(2,1)S(1)}, u32[]{:S(2)}, u32[]{:S(2)}) collective-permute-start(bf16[2,16,2560]{2,1,0:T(8,128)(2,1)S(1)} %get-tuple-element.36), channel_id=1, source_target_pairs={{0,4},{1,5},{2,6},{3,7},{4,0},{5,1},{6,2},{7,3},{8,12},{9,13},{10,... | collective-permute-start | bytes 491528 | tf_op jit(solution)/shard_map/ppermute | solution.py:374
  81.1 1.0 %copy-done.3 = f32[4,16,1536]{2,1,0:T(8,128)S(1)} copy-done((f32[4,16,1536]{2,1,0:T(8,128)S(1)}, f32[4,16,1536]{2,1,0:T(8,128)}, u32[]{:S(2)}) %copy-start.3) | copy-done | bytes 393240
  82.1 1.3 %collective-permute-start.6 = (bf16[2,16,1536]{2,1,0:T(8,128)(2,1)S(1)}, bf16[2,16,1536]{2,1,0:T(8,128)(2,1)S(1)}, u32[]{:S(2)}, u32[]{:S(2)}) collective-permute-start(bf16[2,16,1536]{2,1,0:T(8,128)(2,1)S(1)} %get-tuple-element.42), channel_id=1, source_target_pairs={{0,8},{1,9},{2,10},{3,11},{4,12},{5,13},{6,14},{7,15},{8,0},{9,1},... | collective-permute-start | bytes 294920 | tf_op jit(solution)/shard_map/ppermute | solution.py:374
  83.5 1.8 %collective-permute-done.3.got_ref = bf16[2,16,2560]{2,1,0:T(8,128)(2,1)S(1)} collective-permute-done((bf16[2,16,2560]{2,1,0:T(8,128)(2,1)S(1)}, bf16[2,16,2560]{2,1,0:T(8,128)(2,1)S(1)}, u32[]{:S(2)}, u32[]{:S(2)}) %collective-permute-start.3) | collective-permute-done | bytes 163872 | tf_op jit(solution)/shard_map/ppermute | solution.py:374
  85.3 3.5 %collective-permute-start.4 = (bf16[1,16,2560]{2,1,0:T(8,128)(2,1)S(1)}, bf16[1,16,2560]{2,1,0:T(8,128)(2,1)S(1)}, u32[]{:S(2)}, u32[]{:S(2)}) collective-permute-start(bf16[1,16,2560]{2,1,0:T(8,128)(2,1)S(1)} %get-tuple-element.38), channel_id=1, source_target_pairs={{0,8},{1,9},{2,10},{3,11},{4,12},{5,13},{6,14},{7,15},{8,0},{9,1},... | collective-permute-start | bytes 245768 | tf_op jit(solution)/shard_map/ppermute | solution.py:374
  88.9 1.8 %collective-permute-done.6.got_ref = bf16[2,16,1536]{2,1,0:T(8,128)(2,1)S(1)} collective-permute-done((bf16[2,16,1536]{2,1,0:T(8,128)(2,1)S(1)}, bf16[2,16,1536]{2,1,0:T(8,128)(2,1)S(1)}, u32[]{:S(2)}, u32[]{:S(2)}) %collective-permute-start.6) | collective-permute-done | bytes 98336 | tf_op jit(solution)/shard_map/ppermute | solution.py:374
  90.7 1.5 %collective-permute-start.7 = (bf16[1,16,1536]{2,1,0:T(8,128)(2,1)S(1)}, bf16[1,16,1536]{2,1,0:T(8,128)(2,1)S(1)}, u32[]{:S(2)}, u32[]{:S(2)}) collective-permute-start(bf16[1,16,1536]{2,1,0:T(8,128)(2,1)S(1)} %get-tuple-element.44), channel_id=1, source_target_pairs={{0,2},{1,3},{2,0},{3,1},{4,6},{5,7},{6,4},{7,5},{8,10},{9,11},{10,... | collective-permute-start | bytes 147464 | tf_op jit(solution)/shard_map/ppermute | solution.py:374
  92.2 2.6 %collective-permute-done.7.refs_3_ = bf16[1,16,1536]{2,1,0:T(8,128)(2,1)S(1)} collective-permute-done((bf16[1,16,1536]{2,1,0:T(8,128)(2,1)S(1)}, bf16[1,16,1536]{2,1,0:T(8,128)(2,1)S(1)}, u32[]{:S(2)}, u32[]{:S(2)}) %collective-permute-start.7) | collective-permute-done | bytes 49184 | tf_op jit(solution)/shard_map/ppermute | solution.py:374
  94.9 0.7 finish.1
  (17 shorter events, 0.4 us)
Async XLA Ops:
  1.9 21.9 %all-to-all-start = ((bf16[16,16,1024]{2,1,0:T(8,128)(2,1)}), bf16[16,16,1024]{2,1,0:T(8,128)(2,1)S(1)}, u32[]{:S(2)}, u32[]{:S(2)}) async-start(bf16[16,16,1024]{2,1,0:T(8,128)(2,1)} %split_rows.1), calls=%async_computation | async-start | bytes 1048576 | tf_op jit(solution)/shard_map/all_to_all | solution.py:274
  26.1 27.2 %copy-start.4 = (s32[4,186]{1,0:T(4,128)S(1)}, s32[4,186]{1,0:T(4,128)}, u32[]{:S(2)}) copy-start(s32[4,186]{1,0:T(4,128)} %ids_ref.1) | copy-start | bytes 8932
  26.1 27.2 %all-to-all-start.1 = ((bf16[16,32,1024]{2,1,0:T(8,128)(2,1)}), bf16[16,32,1024]{2,1,0:T(8,128)(2,1)S(1)}, u32[]{:S(2)}, u32[]{:S(2)}) async-start(bf16[16,32,1024]{2,1,0:T(8,128)(2,1)} %get-tuple-element.29), calls=%async_computation.1 | async-start | bytes 2097152 | tf_op jit(solution)/shard_map/all_to_all | solution.py:286
  35.8 1.3 %copy-start.1 = (f32[8,16,4096]{2,1,0:T(8,128)}, f32[8,16,4096]{2,1,0:T(8,128)S(1)}, u32[]{:S(2)}) copy-start(f32[8,16,4096]{2,1,0:T(8,128)S(1)} %get-tuple-element.27.keep_ref) | copy-start | bytes 6291460
  37.1 2.7 %collective-permute-start = (bf16[8,16,4096]{2,1,0:T(8,128)(2,1)S(1)}, bf16[8,16,4096]{2,1,0:T(8,128)(2,1)S(1)}, u32[]{:S(2)}, u32[]{:S(2)}) collective-permute-start(bf16[8,16,4096]{2,1,0:T(8,128)(2,1)S(1)} %get-tuple-element.28), channel_id=1, source_target_pairs={{0,1},{1,0},{2,3},{3,2},{4,5},{5,4},{6,7},{7,6},{8,9},{9,8},{10,11... | collective-permute-start | bytes 3145736 | tf_op jit(solution)/shard_map/ppermute | solution.py:315
  39.8 1.0 %copy-start.5 = (bf16[8,16,4096]{2,1,0:T(8,128)(2,1)}, bf16[8,16,4096]{2,1,0:T(8,128)(2,1)S(1)}, u32[]{:S(2)}) copy-start(bf16[8,16,4096]{2,1,0:T(8,128)(2,1)S(1)} %collective-permute-done.got_ref) | copy-start | bytes 3145732
  44.2 20.3 %copy-start = (f32[8,16,4096]{2,1,0:T(8,128)S(1)}, f32[8,16,4096]{2,1,0:T(8,128)}, u32[]{:S(2)}) copy-start(f32[8,16,4096]{2,1,0:T(8,128)} %pair.1.base_ref) | copy-start | bytes 6291460
  62.6 1.8 %collective-permute-start.1 = (bf16[32,4096]{1,0:T(8,128)(2,1)S(1)}, bf16[32,4096]{1,0:T(8,128)(2,1)S(1)}, u32[]{:S(2)}, u32[]{:S(2)}) collective-permute-start(bf16[32,4096]{1,0:T(8,128)(2,1)S(1)} %delta.1.own_ref), channel_id=1, source_target_pairs={{0,1},{1,0},{2,3},{3,2},{4,5},{5,4},{6,7},{7,6},{8,9},{9,8},{10,11... | collective-permute-start | bytes 786440 | tf_op jit(solution)/shard_map/ppermute | solution.py:342
  66.3 10.5 %collective-permute-start.2 = (bf16[4,16,2560]{2,1,0:T(8,128)(2,1)}, bf16[4,16,2560]{2,1,0:T(8,128)(2,1)}, u32[]{:S(2)}, u32[]{:S(2)}) collective-permute-start(bf16[4,16,2560]{2,1,0:T(8,128)(2,1)} %get-tuple-element.34), channel_id=1, source_target_pairs={{0,2},{1,3},{2,0},{3,1},{4,6},{5,7},{6,4},{7,5},{8,10},{9,11},{10,... | collective-permute-start | bytes 983048 | tf_op jit(solution)/shard_map/ppermute | solution.py:374
  70.0 0.8 copy-start.2
  70.7 10.3 %collective-permute-start.5 = (bf16[4,16,1536]{2,1,0:T(8,128)(2,1)}, bf16[4,16,1536]{2,1,0:T(8,128)(2,1)S(1)}, u32[]{:S(2)}, u32[]{:S(2)}) collective-permute-start(bf16[4,16,1536]{2,1,0:T(8,128)(2,1)} %get-tuple-element.40), channel_id=1, source_target_pairs={{0,4},{1,5},{2,6},{3,7},{4,0},{5,1},{6,2},{7,3},{8,12},{9,13},{10,... | collective-permute-start | bytes 589832 | tf_op jit(solution)/shard_map/ppermute | solution.py:374
  77.9 7.4 %collective-permute-start.3 = (bf16[2,16,2560]{2,1,0:T(8,128)(2,1)S(1)}, bf16[2,16,2560]{2,1,0:T(8,128)(2,1)S(1)}, u32[]{:S(2)}, u32[]{:S(2)}) collective-permute-start(bf16[2,16,2560]{2,1,0:T(8,128)(2,1)S(1)} %get-tuple-element.36), channel_id=1, source_target_pairs={{0,4},{1,5},{2,6},{3,7},{4,0},{5,1},{6,2},{7,3},{8,12},{9,13},{10,... | collective-permute-start | bytes 491528 | tf_op jit(solution)/shard_map/ppermute | solution.py:374
  81.1 1.0 %copy-start.3 = (f32[4,16,1536]{2,1,0:T(8,128)S(1)}, f32[4,16,1536]{2,1,0:T(8,128)}, u32[]{:S(2)}) copy-start(f32[4,16,1536]{2,1,0:T(8,128)} %copy-done.2) | copy-start | bytes 1179652
  82.1 8.6 %collective-permute-start.6 = (bf16[2,16,1536]{2,1,0:T(8,128)(2,1)S(1)}, bf16[2,16,1536]{2,1,0:T(8,128)(2,1)S(1)}, u32[]{:S(2)}, u32[]{:S(2)}) collective-permute-start(bf16[2,16,1536]{2,1,0:T(8,128)(2,1)S(1)} %get-tuple-element.42), channel_id=1, source_target_pairs={{0,8},{1,9},{2,10},{3,11},{4,12},{5,13},{6,14},{7,15},{8,0},{9,1},... | collective-permute-start | bytes 294920 | tf_op jit(solution)/shard_map/ppermute | solution.py:374
  85.3 9.5 %collective-permute-start.4 = (bf16[1,16,2560]{2,1,0:T(8,128)(2,1)S(1)}, bf16[1,16,2560]{2,1,0:T(8,128)(2,1)S(1)}, u32[]{:S(2)}, u32[]{:S(2)}) collective-permute-start(bf16[1,16,2560]{2,1,0:T(8,128)(2,1)S(1)} %get-tuple-element.38), channel_id=1, source_target_pairs={{0,8},{1,9},{2,10},{3,11},{4,12},{5,13},{6,14},{7,15},{8,0},{9,1},... | collective-permute-start | bytes 245768 | tf_op jit(solution)/shard_map/ppermute | solution.py:374
  90.7 4.2 %collective-permute-start.7 = (bf16[1,16,1536]{2,1,0:T(8,128)(2,1)S(1)}, bf16[1,16,1536]{2,1,0:T(8,128)(2,1)S(1)}, u32[]{:S(2)}, u32[]{:S(2)}) collective-permute-start(bf16[1,16,1536]{2,1,0:T(8,128)(2,1)S(1)} %get-tuple-element.44), channel_id=1, source_target_pairs={{0,2},{1,3},{2,0},{3,1},{4,6},{5,7},{6,4},{7,5},{8,10},{9,11},{10,... | collective-permute-start | bytes 147464 | tf_op jit(solution)/shard_map/ppermute | solution.py:374

commit v9 on v8

--- a/solution.py
+++ b/solution.py
@@ -1,4 +1,5 @@
 import functools
+import math
 
 import jax
 import jax.numpy as jnp
@@ -198,7 +199,7 @@
     lane = lane_iota(rows, slots)
     picks = [place_ref[...] - scal_ref[k] == lane for k in (2, 3)]
     picks = [jnp.where(pick, 1.0, 0.0).astype(BF16) for pick in picks]
-    step = cols // (cols // 512) if cols % 512 == 0 else cols
+    step = math.gcd(cols, 512)
     for c in range(0, cols, step):
         at = slice(first + c, first + c + step)
         part = jnp.dot(picks[0], own_ref[:, at], preferred_element_type=F32)
@@ -341,11 +342,11 @@
     )(block_ids, arrived, delta_values)
     others = lax.ppermute(deltas, "cols", pairs(1))
 
-    tile = width_d // 8
+    tile = width_d // 16
     above = [1 << k for k in range(1, peers.bit_length() - 1)]
     ends = []
     for side, order in enumerate((above, above[1:] + above[:1])):
-        first, tiles = ((0, 5), (5, 8 - 5))[side]
+        first, tiles = ((0, 11), (11, 16 - 11))[side]
         cols = tiles * tile
         open_bits = list(above)
         for count, step in enumerate(order):

time: 96 us -> 95 us (0.990)
  starting transfers between devices: 27.3 us -> 26.1 us
    ppermute x6, starting transfers between devices: 14.6 us -> 13.4 us  [body(): got = lax.ppermute(send, 'cols', pairs(step))]
  transfers between devices with their start and end apart: 10 -> 10, of which waited for: 8 -> 7; matrix products, arithmetic and copies ran while one was open for 0% -> 0% of each run, Pallas kernels for 12% -> 12%
where the time goes in v9:
time: 95 us; the launch traced here: 94.6 us
  waiting for transfers between devices  36.3 us (38%)
  Pallas kernels  27.7 us (29%)
  starting transfers between devices  26.1 us (27%)
  local copies, waits for them, and re-layouts  4.21 us (4%)
    all_to_all x1, waiting for transfers between devices, body(): x = lax.all_to_all(outgoing, 'cols', 0, 0)  14.4 us
    ppermute x6, starting transfers between devices, body(): got = lax.ppermute(send, 'cols', pairs(step))  13.4 us
    ppermute x6, waiting for transfers between devices, body(): got = lax.ppermute(send, 'cols', pairs(step))  9.66 us
    pallas_call x1, Pallas kernels, body(): pl.pallas_call(functools.partial(delta_kernel, plan, d_blocks, group), in...  9.27 us
    all_to_all x1, waiting for transfers between devices, body(): arrived = lax.all_to_all(slots, 'cols', 0, 0)  9.13 us
    all_to_all x1, starting transfers between devices, body(): x = lax.all_to_all(outgoing, 'cols', 0, 0)  7.4 us
    pallas_call x1, Pallas kernels, body(): pl.pallas_call(functools.partial(base_kernel, plan), in_specs=[smem, vmem...  5.43 us
    all_to_all x1, starting transfers between devices, body(): arrived = lax.all_to_all(slots, 'cols', 0, 0)  4.23 us
  transfers between devices with their start and end apart: 10, of which 7 were waited for; matrix products, arithmetic and copies ran while one was open for 0% of the time, Pallas kernels for 12%

profile of v9, /device:TPU:0, one launch (start us, length us, event | category | flops | bytes accessed | tf_op | source)
XLA Modules:
  0.0 94.6 jit_solution(9861355561831637796)
XLA Ops:
  0.0 1.9 %split_rows.1 = bf16[16,16,1024]{2,1,0:T(8,128)(2,1)} custom-call(bf16[16,14848]{1,0:T(8,128)(2,1)} %h_hbm.1, s32[1,16]{1,0:T(1,128)} %bitcast.9, s32[1,64]{1,0:T(1,128)} %bitcast.10), custom_call_target="tpu_custom_call" | custom-call | tf_op jit(solution)/shard_map/split_rows/pallas_call | solution.py:262
  1.9 7.4 %all-to-all-start = ((bf16[16,16,1024]{2,1,0:T(8,128)(2,1)}), bf16[16,16,1024]{2,1,0:T(8,128)(2,1)S(1)}, u32[]{:S(2)}, u32[]{:S(2)}) async-start(bf16[16,16,1024]{2,1,0:T(8,128)(2,1)} %split_rows.1), calls=%async_computation | async-start | bytes 1048576 | tf_op jit(solution)/shard_map/all_to_all | solution.py:275
  9.4 14.4 %all-to-all-done.x_ref = bf16[16,16,1024]{2,1,0:T(8,128)(2,1)S(1)} async-done(((bf16[16,16,1024]{2,1,0:T(8,128)(2,1)}), bf16[16,16,1024]{2,1,0:T(8,128)(2,1)S(1)}, u32[]{:S(2)}, u32[]{:S(2)}) %all-to-all-start) | async-done | bytes 524320 | tf_op jit(solution)/shard_map/all_to_all | solution.py:275
  23.8 2.3 %route.1 = (bf16[16,32,1024]{2,1,0:T(8,128)(2,1)}, s32[256,1]{1,0:T(8,128)S(1)}) custom-call(s32[4]{0:T(128)S(1)} %pad_add_fusion.shift_ref.scal_ref, bf16[16,16,1024]{2,1,0:T(8,128)(2,1)S(1)} %all-to-all-done.x_ref), custom_call_target="tpu_custom_call" | custom-call | tf_op jit(solution)/shard_map/route/pallas_call | solution.py:277
  26.1 4.2 %all-to-all-start.1 = ((bf16[16,32,1024]{2,1,0:T(8,128)(2,1)}), bf16[16,32,1024]{2,1,0:T(8,128)(2,1)S(1)}, u32[]{:S(2)}, u32[]{:S(2)}) async-start(bf16[16,32,1024]{2,1,0:T(8,128)(2,1)} %get-tuple-element.29), calls=%async_computation.1 | async-start | bytes 2097152 | tf_op jit(solution)/shard_map/all_to_all | solution.py:287
  30.3 5.4 %base.1 = (f32[8,16,4096]{2,1,0:T(8,128)S(1)}, bf16[8,16,4096]{2,1,0:T(8,128)(2,1)S(1)}) custom-call(s32[4]{0:T(128)S(1)} %pad_add_fusion.shift_ref.scal_ref, bf16[16,16,1024]{2,1,0:T(8,128)(2,1)S(1)} %all-to-all-done.x_ref, bf16[928,4096]{1,0:T(8,128)(2,1)} %w_hbm.1), custom_call_target="tpu_custom_call" | custom-call | flops 1946157056 | bytes 7602176 | tf_op jit(solution)/shard_map/base/pallas_call | solution.py:292
  35.8 1.3 %copy-done.1 = f32[8,16,4096]{2,1,0:T(8,128)} copy-done((f32[8,16,4096]{2,1,0:T(8,128)}, f32[8,16,4096]{2,1,0:T(8,128)S(1)}, u32[]{:S(2)}) %copy-start.1) | copy-done | bytes 2097176
  37.1 0.4 collective-permute-start
  37.5 2.3 %collective-permute-done.got_ref = bf16[8,16,4096]{2,1,0:T(8,128)(2,1)S(1)} collective-permute-done((bf16[8,16,4096]{2,1,0:T(8,128)(2,1)S(1)}, bf16[8,16,4096]{2,1,0:T(8,128)(2,1)S(1)}, u32[]{:S(2)}, u32[]{:S(2)}) %collective-permute-start) | collective-permute-done | bytes 1048608 | tf_op jit(solution)/shard_map/ppermute | solution.py:316
  39.8 1.0 %copy-done.5 = bf16[8,16,4096]{2,1,0:T(8,128)(2,1)} copy-done((bf16[8,16,4096]{2,1,0:T(8,128)(2,1)}, bf16[8,16,4096]{2,1,0:T(8,128)(2,1)S(1)}, u32[]{:S(2)}) %copy-start.5) | copy-done | bytes 1048600
  40.8 3.4 %pair.1.base_ref = f32[8,16,4096]{2,1,0:T(8,128)} custom-call(f32[8,16,4096]{2,1,0:T(8,128)} %copy-done.1, bf16[8,16,4096]{2,1,0:T(8,128)(2,1)} %copy-done.5), custom_call_target="tpu_custom_call" | custom-call | tf_op jit(solution)/shard_map/pair/pallas_call | solution.py:311
  44.2 9.1 %all-to-all-done.1.x_ref = bf16[16,32,1024]{2,1,0:T(8,128)(2,1)S(1)} async-done(((bf16[16,32,1024]{2,1,0:T(8,128)(2,1)}), bf16[16,32,1024]{2,1,0:T(8,128)(2,1)S(1)}, u32[]{:S(2)}, u32[]{:S(2)}) %all-to-all-start.1) | async-done | bytes 1048608 | tf_op jit(solution)/shard_map/all_to_all | solution.py:287
  53.3 9.3 %delta.1.own_ref = bf16[32,4096]{1,0:T(8,128)(2,1)S(1)} custom-call(s32[4,186]{1,0:T(4,128)S(1)} %copy-done.4, bf16[16,32,1024]{2,1,0:T(8,128)(2,1)S(1)} %all-to-all-done.1.x_ref, bf16[4,186,128,128]{3,2,1,0:T(8,128)(2,1)} %v_hbm.1), custom_call_target="tpu_custom_call" | custom-call | flops 195035136 | bytes 24379392 | tf_op jit(solution)/shard_map/delta/pallas_call | solution.py:324
  62.6 0.7 collective-permute-start.1
  63.2 0.1 reduce
  63.3 0.1 reshape.30
  63.6 0.8 collective-permute-done.1.got_ref
  64.4 1.9 %join.2 = (f32[4,16,2816]{2,1,0:T(8,128)S(1)}, bf16[4,16,2816]{2,1,0:T(8,128)(2,1)}) custom-call(s32[4]{0:T(128)S(1)} %pad_add_fusion.shift_ref.scal_ref, s32[1]{0:T(128)} %bitcast.6.bit_ref, f32[8,16,4096]{2,1,0:T(8,128)S(1)} %copy-done, s32[128,1]{1,0:T(8,128)S(1)} %reshape.32.place_ref, bf16[32,4096]{1,0:T(8,128)(2,1)S(1)} %delta.1.own_ref, ...), custom_call_target="tpu_custom_call" | custom-call | tf_op jit(solution)/shard_map/join/pallas_call | solution.py:359
  66.3 2.0 %collective-permute-start.2 = (bf16[4,16,2816]{2,1,0:T(8,128)(2,1)}, bf16[4,16,2816]{2,1,0:T(8,128)(2,1)}, u32[]{:S(2)}, u32[]{:S(2)}) collective-permute-start(bf16[4,16,2816]{2,1,0:T(8,128)(2,1)} %get-tuple-element.34), channel_id=1, source_target_pairs={{0,2},{1,3},{2,0},{3,1},{4,6},{5,7},{6,4},{7,5},{8,10},{9,11},{10,... | collective-permute-start | bytes 1081352 | tf_op jit(solution)/shard_map/ppermute | solution.py:375
  68.3 1.6 %join.3 = (f32[4,16,1280]{2,1,0:T(8,128)S(1)}, bf16[4,16,1280]{2,1,0:T(8,128)(2,1)}) custom-call(s32[4]{0:T(128)S(1)} %pad_add_fusion.shift_ref.scal_ref, s32[1]{0:T(128)} %bitcast.1.bit_ref, f32[8,16,4096]{2,1,0:T(8,128)S(1)} %copy-done, s32[128,1]{1,0:T(8,128)S(1)} %reshape.32.place_ref, bf16[32,4096]{1,0:T(8,128)(2,1)S(1)} %delta.1.own_ref, ...), custom_call_target="tpu_custom_call" | custom-call | tf_op jit(solution)/shard_map/join/pallas_call | solution.py:359
  70.0 0.7 copy-done.2
  70.7 3.0 %collective-permute-start.5 = (bf16[4,16,1280]{2,1,0:T(8,128)(2,1)}, bf16[4,16,1280]{2,1,0:T(8,128)(2,1)S(1)}, u32[]{:S(2)}, u32[]{:S(2)}) collective-permute-start(bf16[4,16,1280]{2,1,0:T(8,128)(2,1)} %get-tuple-element.40), channel_id=1, source_target_pairs={{0,4},{1,5},{2,6},{3,7},{4,0},{5,1},{6,2},{7,3},{8,12},{9,13},{10,... | collective-permute-start | bytes 491528 | tf_op jit(solution)/shard_map/ppermute | solution.py:375
  73.6 3.9 %collective-permute-done.2.got_ref = bf16[4,16,2816]{2,1,0:T(8,128)(2,1)} collective-permute-done((bf16[4,16,2816]{2,1,0:T(8,128)(2,1)}, bf16[4,16,2816]{2,1,0:T(8,128)(2,1)}, u32[]{:S(2)}, u32[]{:S(2)}) %collective-permute-start.2) | collective-permute-done | bytes 360480 | tf_op jit(solution)/shard_map/ppermute | solution.py:375
  77.6 1.1 %halve.4 = (f32[2,16,2816]{2,1,0:T(8,128)S(1)}, bf16[2,16,2816]{2,1,0:T(8,128)(2,1)S(1)}) custom-call(s32[1]{0:T(128)} %bitcast.1.bit_ref, f32[4,16,2816]{2,1,0:T(8,128)S(1)} %get-tuple-element.33.keep_ref, bf16[4,16,2816]{2,1,0:T(8,128)(2,1)} %collective-permute-done.2.got_ref), custom_call_target="tpu_custom_call" | custom-call | tf_op jit(solution)/shard_map/halve/pallas_call | solution.py:368
  78.6 3.2 %collective-permute-start.3 = (bf16[2,16,2816]{2,1,0:T(8,128)(2,1)S(1)}, bf16[2,16,2816]{2,1,0:T(8,128)(2,1)S(1)}, u32[]{:S(2)}, u32[]{:S(2)}) collective-permute-start(bf16[2,16,2816]{2,1,0:T(8,128)(2,1)S(1)} %get-tuple-element.36), channel_id=1, source_target_pairs={{0,4},{1,5},{2,6},{3,7},{4,0},{5,1},{6,2},{7,3},{8,12},{9,13},{10,... | collective-permute-start | bytes 540680 | tf_op jit(solution)/shard_map/ppermute | solution.py:375
  81.9 1.0 %copy-done.3 = f32[4,16,1280]{2,1,0:T(8,128)S(1)} copy-done((f32[4,16,1280]{2,1,0:T(8,128)S(1)}, f32[4,16,1280]{2,1,0:T(8,128)}, u32[]{:S(2)}) %copy-start.3) | copy-done | bytes 327704
  82.9 1.3 %collective-permute-start.6 = (bf16[2,16,1280]{2,1,0:T(8,128)(2,1)S(1)}, bf16[2,16,1280]{2,1,0:T(8,128)(2,1)S(1)}, u32[]{:S(2)}, u32[]{:S(2)}) collective-permute-start(bf16[2,16,1280]{2,1,0:T(8,128)(2,1)S(1)} %get-tuple-element.42), channel_id=1, source_target_pairs={{0,8},{1,9},{2,10},{3,11},{4,12},{5,13},{6,14},{7,15},{8,0},{9,1},... | collective-permute-start | bytes 245768 | tf_op jit(solution)/shard_map/ppermute | solution.py:375
  84.2 2.8 %collective-permute-done.3.got_ref = bf16[2,16,2816]{2,1,0:T(8,128)(2,1)S(1)} collective-permute-done((bf16[2,16,2816]{2,1,0:T(8,128)(2,1)S(1)}, bf16[2,16,2816]{2,1,0:T(8,128)(2,1)S(1)}, u32[]{:S(2)}, u32[]{:S(2)}) %collective-permute-start.3) | collective-permute-done | bytes 180256 | tf_op jit(solution)/shard_map/ppermute | solution.py:375
  87.0 2.8 %collective-permute-start.4 = (bf16[1,16,2816]{2,1,0:T(8,128)(2,1)S(1)}, bf16[1,16,2816]{2,1,0:T(8,128)(2,1)S(1)}, u32[]{:S(2)}, u32[]{:S(2)}) collective-permute-start(bf16[1,16,2816]{2,1,0:T(8,128)(2,1)S(1)} %get-tuple-element.38), channel_id=1, source_target_pairs={{0,8},{1,9},{2,10},{3,11},{4,12},{5,13},{6,14},{7,15},{8,0},{9,1},... | collective-permute-start | bytes 270344 | tf_op jit(solution)/shard_map/ppermute | solution.py:375
  89.8 1.1 %collective-permute-start.7 = (bf16[1,16,1280]{2,1,0:T(8,128)(2,1)S(1)}, bf16[1,16,1280]{2,1,0:T(8,128)(2,1)S(1)}, u32[]{:S(2)}, u32[]{:S(2)}) collective-permute-start(bf16[1,16,1280]{2,1,0:T(8,128)(2,1)S(1)} %get-tuple-element.44), channel_id=1, source_target_pairs={{0,2},{1,3},{2,0},{3,1},{4,6},{5,7},{6,4},{7,5},{8,10},{9,11},{10,... | collective-permute-start | bytes 122888 | tf_op jit(solution)/shard_map/ppermute | solution.py:375
  91.0 2.9 %collective-permute-done.7.refs_3_ = bf16[1,16,1280]{2,1,0:T(8,128)(2,1)S(1)} collective-permute-done((bf16[1,16,1280]{2,1,0:T(8,128)(2,1)S(1)}, bf16[1,16,1280]{2,1,0:T(8,128)(2,1)S(1)}, u32[]{:S(2)}, u32[]{:S(2)}) %collective-permute-start.7) | collective-permute-done | bytes 40992 | tf_op jit(solution)/shard_map/ppermute | solution.py:375
  93.9 0.7 finish.1
  (17 shorter events, 0.3 us)
Async XLA Ops:
  1.9 21.9 %all-to-all-start = ((bf16[16,16,1024]{2,1,0:T(8,128)(2,1)}), bf16[16,16,1024]{2,1,0:T(8,128)(2,1)S(1)}, u32[]{:S(2)}, u32[]{:S(2)}) async-start(bf16[16,16,1024]{2,1,0:T(8,128)(2,1)} %split_rows.1), calls=%async_computation | async-start | bytes 1048576 | tf_op jit(solution)/shard_map/all_to_all | solution.py:275
  26.1 27.2 %copy-start.4 = (s32[4,186]{1,0:T(4,128)S(1)}, s32[4,186]{1,0:T(4,128)}, u32[]{:S(2)}) copy-start(s32[4,186]{1,0:T(4,128)} %ids_ref.1) | copy-start | bytes 8932
  26.1 27.2 %all-to-all-start.1 = ((bf16[16,32,1024]{2,1,0:T(8,128)(2,1)}), bf16[16,32,1024]{2,1,0:T(8,128)(2,1)S(1)}, u32[]{:S(2)}, u32[]{:S(2)}) async-start(bf16[16,32,1024]{2,1,0:T(8,128)(2,1)} %get-tuple-element.29), calls=%async_computation.1 | async-start | bytes 2097152 | tf_op jit(solution)/shard_map/all_to_all | solution.py:287
  35.8 1.3 %copy-start.1 = (f32[8,16,4096]{2,1,0:T(8,128)}, f32[8,16,4096]{2,1,0:T(8,128)S(1)}, u32[]{:S(2)}) copy-start(f32[8,16,4096]{2,1,0:T(8,128)S(1)} %get-tuple-element.27.keep_ref) | copy-start | bytes 6291460
  37.1 2.7 %collective-permute-start = (bf16[8,16,4096]{2,1,0:T(8,128)(2,1)S(1)}, bf16[8,16,4096]{2,1,0:T(8,128)(2,1)S(1)}, u32[]{:S(2)}, u32[]{:S(2)}) collective-permute-start(bf16[8,16,4096]{2,1,0:T(8,128)(2,1)S(1)} %get-tuple-element.28), channel_id=1, source_target_pairs={{0,1},{1,0},{2,3},{3,2},{4,5},{5,4},{6,7},{7,6},{8,9},{9,8},{10,11... | collective-permute-start | bytes 3145736 | tf_op jit(solution)/shard_map/ppermute | solution.py:316
  39.8 1.0 %copy-start.5 = (bf16[8,16,4096]{2,1,0:T(8,128)(2,1)}, bf16[8,16,4096]{2,1,0:T(8,128)(2,1)S(1)}, u32[]{:S(2)}) copy-start(bf16[8,16,4096]{2,1,0:T(8,128)(2,1)S(1)} %collective-permute-done.got_ref) | copy-start | bytes 3145732
  44.2 20.3 %copy-start = (f32[8,16,4096]{2,1,0:T(8,128)S(1)}, f32[8,16,4096]{2,1,0:T(8,128)}, u32[]{:S(2)}) copy-start(f32[8,16,4096]{2,1,0:T(8,128)} %pair.1.base_ref) | copy-start | bytes 6291460
  62.6 1.8 %collective-permute-start.1 = (bf16[32,4096]{1,0:T(8,128)(2,1)S(1)}, bf16[32,4096]{1,0:T(8,128)(2,1)S(1)}, u32[]{:S(2)}, u32[]{:S(2)}) collective-permute-start(bf16[32,4096]{1,0:T(8,128)(2,1)S(1)} %delta.1.own_ref), channel_id=1, source_target_pairs={{0,1},{1,0},{2,3},{3,2},{4,5},{5,4},{6,7},{7,6},{8,9},{9,8},{10,11... | collective-permute-start | bytes 786440 | tf_op jit(solution)/shard_map/ppermute | solution.py:343
  66.3 11.2 %collective-permute-start.2 = (bf16[4,16,2816]{2,1,0:T(8,128)(2,1)}, bf16[4,16,2816]{2,1,0:T(8,128)(2,1)}, u32[]{:S(2)}, u32[]{:S(2)}) collective-permute-start(bf16[4,16,2816]{2,1,0:T(8,128)(2,1)} %get-tuple-element.34), channel_id=1, source_target_pairs={{0,2},{1,3},{2,0},{3,1},{4,6},{5,7},{6,4},{7,5},{8,10},{9,11},{10,... | collective-permute-start | bytes 1081352 | tf_op jit(solution)/shard_map/ppermute | solution.py:375
  70.0 0.7 copy-start.2
  70.7 11.2 %collective-permute-start.5 = (bf16[4,16,1280]{2,1,0:T(8,128)(2,1)}, bf16[4,16,1280]{2,1,0:T(8,128)(2,1)S(1)}, u32[]{:S(2)}, u32[]{:S(2)}) collective-permute-start(bf16[4,16,1280]{2,1,0:T(8,128)(2,1)} %get-tuple-element.40), channel_id=1, source_target_pairs={{0,4},{1,5},{2,6},{3,7},{4,0},{5,1},{6,2},{7,3},{8,12},{9,13},{10,... | collective-permute-start | bytes 491528 | tf_op jit(solution)/shard_map/ppermute | solution.py:375
  78.6 8.3 %collective-permute-start.3 = (bf16[2,16,2816]{2,1,0:T(8,128)(2,1)S(1)}, bf16[2,16,2816]{2,1,0:T(8,128)(2,1)S(1)}, u32[]{:S(2)}, u32[]{:S(2)}) collective-permute-start(bf16[2,16,2816]{2,1,0:T(8,128)(2,1)S(1)} %get-tuple-element.36), channel_id=1, source_target_pairs={{0,4},{1,5},{2,6},{3,7},{4,0},{5,1},{6,2},{7,3},{8,12},{9,13},{10,... | collective-permute-start | bytes 540680 | tf_op jit(solution)/shard_map/ppermute | solution.py:375
  81.8 1.0 %copy-start.3 = (f32[4,16,1280]{2,1,0:T(8,128)S(1)}, f32[4,16,1280]{2,1,0:T(8,128)}, u32[]{:S(2)}) copy-start(f32[4,16,1280]{2,1,0:T(8,128)} %copy-done.2) | copy-start | bytes 983044
  82.9 7.0 %collective-permute-start.6 = (bf16[2,16,1280]{2,1,0:T(8,128)(2,1)S(1)}, bf16[2,16,1280]{2,1,0:T(8,128)(2,1)S(1)}, u32[]{:S(2)}, u32[]{:S(2)}) collective-permute-start(bf16[2,16,1280]{2,1,0:T(8,128)(2,1)S(1)} %get-tuple-element.42), channel_id=1, source_target_pairs={{0,8},{1,9},{2,10},{3,11},{4,12},{5,13},{6,14},{7,15},{8,0},{9,1},... | collective-permute-start | bytes 245768 | tf_op jit(solution)/shard_map/ppermute | solution.py:375
  87.0 6.9 %collective-permute-start.4 = (bf16[1,16,2816]{2,1,0:T(8,128)(2,1)S(1)}, bf16[1,16,2816]{2,1,0:T(8,128)(2,1)S(1)}, u32[]{:S(2)}, u32[]{:S(2)}) collective-permute-start(bf16[1,16,2816]{2,1,0:T(8,128)(2,1)S(1)} %get-tuple-element.38), channel_id=1, source_target_pairs={{0,8},{1,9},{2,10},{3,11},{4,12},{5,13},{6,14},{7,15},{8,0},{9,1},... | collective-permute-start | bytes 270344 | tf_op jit(solution)/shard_map/ppermute | solution.py:375
  89.8 4.1 %collective-permute-start.7 = (bf16[1,16,1280]{2,1,0:T(8,128)(2,1)S(1)}, bf16[1,16,1280]{2,1,0:T(8,128)(2,1)S(1)}, u32[]{:S(2)}, u32[]{:S(2)}) collective-permute-start(bf16[1,16,1280]{2,1,0:T(8,128)(2,1)S(1)} %get-tuple-element.44), channel_id=1, source_target_pairs={{0,2},{1,3},{2,0},{3,1},{4,6},{5,7},{6,4},{7,5},{8,10},{9,11},{10,... | collective-permute-start | bytes 122888 | tf_op jit(solution)/shard_map/ppermute | solution.py:375

commit v10 on v9

--- a/solution.py
+++ b/solution.py
@@ -32,7 +32,9 @@
     return lax.broadcasted_iota(jnp.int32, (rows, lanes), 1)
 
 
-def split_kernel(plan, h_hbm, id_hbm, slot_hbm, o_ref, h_ref, id_ref, slot_ref, sems):
+def split_kernel(
+    plan, h_hbm, id_hbm, slot_hbm, o_hbm, h_ref, id_ref, slot_ref, o_ref, sems, out_sems
+):
     share, window, _, starts = plan
     rows, width = h_ref.shape
     variants = slot_ref.shape[1]
@@ -55,6 +57,8 @@
     slot = jnp.sum(jnp.where(named, slot_ref[...].astype(F32), 0.0), axis=1, keepdims=True)
     copies[2].wait()
     late = True
+    owners = len(starts) // out_sems.shape[0]
+    done = []
     for s, b in enumerate(starts):
         if late and b * LANES + window > cut:
             copies[3].wait()
@@ -62,6 +66,14 @@
         spare = (s * share - b * LANES + share) % window
         piece = h_ref[:, b * LANES : b * LANES + window].astype(F32)
         o_ref[s] = jnp.where(lane == spare, slot, piece).astype(BF16)
+        if (s + 1) % owners == 0:
+            at = pl.ds(s + 1 - owners, owners)
+            done.append(
+                pltpu.make_async_copy(o_ref.at[at], o_hbm.at[at], out_sems.at[s // owners])
+            )
+            done[-1].start()
+    for copy in done:
+        copy.wait()
 
 
 def own_shift(plan):
@@ -70,7 +82,7 @@
     return start - jnp.minimum(start // LANES, last) * LANES
 
 
-def route_kernel(plan, capacity, shift_ref, x_ref, o_ref, place_ref):
+def route_kernel(plan, capacity, shift_ref, x_ref, o_hbm, place_ref, o_ref, sems):
     share, window, _, _ = plan
     peers, row_dev, _ = x_ref.shape
     rows = peers * row_dev
@@ -91,10 +103,21 @@
     place = slot * capacity + rank
     place_ref[...] = place.astype(jnp.int32)
     across = jnp.sum(jnp.where(row_i == row_j, place, 0.0), axis=0, keepdims=True)
-    pick = across.astype(jnp.int32) == lax.broadcasted_iota(jnp.int32, (slots, rows), 0)
-    pick = jnp.where(pick, 1.0, 0.0).astype(BF16)
-    filled = jnp.dot(pick, data, preferred_element_type=F32).astype(BF16)
-    o_ref[...] = filled.reshape(o_ref.shape)
+    across = across.astype(jnp.int32)
+    parts = sems.shape[0]
+    owners = peers // parts
+    copies = []
+    for p in range(parts):
+        some = slots // parts
+        named = lax.broadcasted_iota(jnp.int32, (some, rows), 0) + p * some
+        pick = jnp.where(across == named, 1.0, 0.0).astype(BF16)
+        filled = jnp.dot(pick, data, preferred_element_type=F32).astype(BF16)
+        at = pl.ds(p * owners, owners)
+        o_ref[at] = filled.reshape((owners,) + o_ref.shape[1:])
+        copies.append(pltpu.make_async_copy(o_ref.at[at], o_hbm.at[at], sems.at[p]))
+        copies[-1].start()
+    for copy in copies:
+        copy.wait()
 
 
 def base_kernel(plan, scal_ref, x_ref, w_hbm, keep_ref, send_ref, mine_ref, w_ref, sems):
@@ -262,12 +285,15 @@
     outgoing = pl.pallas_call(
         functools.partial(split_kernel, plan),
         in_specs=[anywhere] * 3,
+        out_specs=anywhere,
         out_shape=jax.ShapeDtypeStruct((peers, row_dev, window), BF16),
         scratch_shapes=[
             pltpu.VMEM((row_dev, width_f), BF16),
             pltpu.VMEM((1, row_dev), jnp.int32),
             pltpu.VMEM((1, variants), jnp.int32),
+            pltpu.VMEM((peers, row_dev, window), BF16),
             pltpu.SemaphoreType.DMA((4,)),
+            pltpu.SemaphoreType.DMA((split_factor(peers, 4),)),
         ],
         compiler_params=params(60),
         name="split_rows",
@@ -281,6 +307,11 @@
             jax.ShapeDtypeStruct((all_rows, 1), jnp.int32),
         ),
         in_specs=[smem, vmem],
+        out_specs=(anywhere, vmem),
+        scratch_shapes=[
+            pltpu.VMEM((peers, local_slots, window), BF16),
+            pltpu.SemaphoreType.DMA((split_factor(peers, 4),)),
+        ],
         compiler_params=params(),
         name="route",
     )(scal, x)

time: 95 us -> 94.8 us (level)
  no operation moved by 1% of the time
where the time goes in v10:
time: 94.8 us; the launch traced here: 94.3 us
  waiting for transfers between devices  36.3 us (38%)
  Pallas kernels  27.5 us (29%)
  starting transfers between devices  26 us (27%)
  local copies, waits for them, and re-layouts  4.21 us (4%)
    all_to_all x1, waiting for transfers between devices, body(): x = lax.all_to_all(outgoing, 'cols', 0, 0)  14.4 us
    ppermute x6, starting transfers between devices, body(): got = lax.ppermute(send, 'cols', pairs(step))  13.4 us
    ppermute x6, waiting for transfers between devices, body(): got = lax.ppermute(send, 'cols', pairs(step))  9.64 us
    pallas_call x1, Pallas kernels, body(): pl.pallas_call(functools.partial(delta_kernel, plan, d_blocks, group), in...  9.27 us
    all_to_all x1, waiting for transfers between devices, body(): arrived = lax.all_to_all(slots, 'cols', 0, 0)  9.13 us
    all_to_all x1, starting transfers between devices, body(): x = lax.all_to_all(outgoing, 'cols', 0, 0)  7.4 us
    pallas_call x1, Pallas kernels, body(): pl.pallas_call(functools.partial(base_kernel, plan), in_specs=[smem, vmem...  5.42 us
    all_to_all x1, starting transfers between devices, body(): arrived = lax.all_to_all(slots, 'cols', 0, 0)  4.11 us
  transfers between devices with their start and end apart: 10, of which 7 were waited for; matrix products, arithmetic and copies ran while one was open for 0% of the time, Pallas kernels for 12%

profile of v10, /device:TPU:0, one launch (start us, length us, event | category | flops | bytes accessed | tf_op | source)
XLA Modules:
  0.0 94.3 jit_solution(17243722656570520256)
XLA Ops:
  0.0 1.9 %split_rows.1 = bf16[16,16,1024]{2,1,0:T(8,128)(2,1)} custom-call(bf16[16,14848]{1,0:T(8,128)(2,1)} %h_hbm.1, s32[1,16]{1,0:T(1,128)} %bitcast.9, s32[1,64]{1,0:T(1,128)} %bitcast.10), custom_call_target="tpu_custom_call" | custom-call | tf_op jit(solution)/shard_map/split_rows/pallas_call | solution.py:285
  1.9 7.4 %all-to-all-start = ((bf16[16,16,1024]{2,1,0:T(8,128)(2,1)}), bf16[16,16,1024]{2,1,0:T(8,128)(2,1)S(1)}, u32[]{:S(2)}, u32[]{:S(2)}) async-start(bf16[16,16,1024]{2,1,0:T(8,128)(2,1)} %split_rows.1), calls=%async_computation | async-start | bytes 1048576 | tf_op jit(solution)/shard_map/all_to_all | solution.py:301
  9.4 14.4 %all-to-all-done.x_ref = bf16[16,16,1024]{2,1,0:T(8,128)(2,1)S(1)} async-done(((bf16[16,16,1024]{2,1,0:T(8,128)(2,1)}), bf16[16,16,1024]{2,1,0:T(8,128)(2,1)S(1)}, u32[]{:S(2)}, u32[]{:S(2)}) %all-to-all-start) | async-done | bytes 524320 | tf_op jit(solution)/shard_map/all_to_all | solution.py:301
  23.7 2.2 %route.1 = (bf16[16,32,1024]{2,1,0:T(8,128)(2,1)}, s32[256,1]{1,0:T(8,128)S(1)}) custom-call(s32[4]{0:T(128)S(1)} %pad_add_fusion.shift_ref.scal_ref, bf16[16,16,1024]{2,1,0:T(8,128)(2,1)S(1)} %all-to-all-done.x_ref), custom_call_target="tpu_custom_call" | custom-call | tf_op jit(solution)/shard_map/route/pallas_call | solution.py:303
  26.0 4.1 %all-to-all-start.1 = ((bf16[16,32,1024]{2,1,0:T(8,128)(2,1)}), bf16[16,32,1024]{2,1,0:T(8,128)(2,1)S(1)}, u32[]{:S(2)}, u32[]{:S(2)}) async-start(bf16[16,32,1024]{2,1,0:T(8,128)(2,1)} %get-tuple-element.29), calls=%async_computation.1 | async-start | bytes 2097152 | tf_op jit(solution)/shard_map/all_to_all | solution.py:318
  30.1 5.4 %base.1 = (f32[8,16,4096]{2,1,0:T(8,128)S(1)}, bf16[8,16,4096]{2,1,0:T(8,128)(2,1)S(1)}) custom-call(s32[4]{0:T(128)S(1)} %pad_add_fusion.shift_ref.scal_ref, bf16[16,16,1024]{2,1,0:T(8,128)(2,1)S(1)} %all-to-all-done.x_ref, bf16[928,4096]{1,0:T(8,128)(2,1)} %w_hbm.1), custom_call_target="tpu_custom_call" | custom-call | flops 1946157056 | bytes 7602176 | tf_op jit(solution)/shard_map/base/pallas_call | solution.py:323
  35.5 1.3 %copy-done.1 = f32[8,16,4096]{2,1,0:T(8,128)} copy-done((f32[8,16,4096]{2,1,0:T(8,128)}, f32[8,16,4096]{2,1,0:T(8,128)S(1)}, u32[]{:S(2)}) %copy-start.1) | copy-done | bytes 2097176
  36.8 0.4 collective-permute-start
  37.2 2.3 %collective-permute-done.got_ref = bf16[8,16,4096]{2,1,0:T(8,128)(2,1)S(1)} collective-permute-done((bf16[8,16,4096]{2,1,0:T(8,128)(2,1)S(1)}, bf16[8,16,4096]{2,1,0:T(8,128)(2,1)S(1)}, u32[]{:S(2)}, u32[]{:S(2)}) %collective-permute-start) | collective-permute-done | bytes 1048608 | tf_op jit(solution)/shard_map/ppermute | solution.py:347
  39.5 1.0 %copy-done.5 = bf16[8,16,4096]{2,1,0:T(8,128)(2,1)} copy-done((bf16[8,16,4096]{2,1,0:T(8,128)(2,1)}, bf16[8,16,4096]{2,1,0:T(8,128)(2,1)S(1)}, u32[]{:S(2)}) %copy-start.5) | copy-done | bytes 1048600
  40.5 3.4 %pair.1.base_ref = f32[8,16,4096]{2,1,0:T(8,128)} custom-call(f32[8,16,4096]{2,1,0:T(8,128)} %copy-done.1, bf16[8,16,4096]{2,1,0:T(8,128)(2,1)} %copy-done.5), custom_call_target="tpu_custom_call" | custom-call | tf_op jit(solution)/shard_map/pair/pallas_call | solution.py:342
  43.9 9.1 %all-to-all-done.1.x_ref = bf16[16,32,1024]{2,1,0:T(8,128)(2,1)S(1)} async-done(((bf16[16,32,1024]{2,1,0:T(8,128)(2,1)}), bf16[16,32,1024]{2,1,0:T(8,128)(2,1)S(1)}, u32[]{:S(2)}, u32[]{:S(2)}) %all-to-all-start.1) | async-done | bytes 1048608 | tf_op jit(solution)/shard_map/all_to_all | solution.py:318
  53.0 9.3 %delta.1.own_ref = bf16[32,4096]{1,0:T(8,128)(2,1)S(1)} custom-call(s32[4,186]{1,0:T(4,128)S(1)} %copy-done.4, bf16[16,32,1024]{2,1,0:T(8,128)(2,1)S(1)} %all-to-all-done.1.x_ref, bf16[4,186,128,128]{3,2,1,0:T(8,128)(2,1)} %v_hbm.1), custom_call_target="tpu_custom_call" | custom-call | flops 195035136 | bytes 24379392 | tf_op jit(solution)/shard_map/delta/pallas_call | solution.py:355
  62.3 0.7 collective-permute-start.1
  63.0 0.1 reduce
  63.1 0.1 reshape.30
  63.3 0.8 collective-permute-done.1.got_ref
  64.1 1.9 %join.2 = (f32[4,16,2816]{2,1,0:T(8,128)S(1)}, bf16[4,16,2816]{2,1,0:T(8,128)(2,1)}) custom-call(s32[4]{0:T(128)S(1)} %pad_add_fusion.shift_ref.scal_ref, s32[1]{0:T(128)} %bitcast.6.bit_ref, f32[8,16,4096]{2,1,0:T(8,128)S(1)} %copy-done, s32[128,1]{1,0:T(8,128)S(1)} %reshape.32.place_ref, bf16[32,4096]{1,0:T(8,128)(2,1)S(1)} %delta.1.own_ref, ...), custom_call_target="tpu_custom_call" | custom-call | tf_op jit(solution)/shard_map/join/pallas_call | solution.py:390
  66.1 2.0 %collective-permute-start.2 = (bf16[4,16,2816]{2,1,0:T(8,128)(2,1)}, bf16[4,16,2816]{2,1,0:T(8,128)(2,1)}, u32[]{:S(2)}, u32[]{:S(2)}) collective-permute-start(bf16[4,16,2816]{2,1,0:T(8,128)(2,1)} %get-tuple-element.34), channel_id=1, source_target_pairs={{0,2},{1,3},{2,0},{3,1},{4,6},{5,7},{6,4},{7,5},{8,10},{9,11},{10,... | collective-permute-start | bytes 1081352 | tf_op jit(solution)/shard_map/ppermute | solution.py:406
  68.1 1.6 %join.3 = (f32[4,16,1280]{2,1,0:T(8,128)S(1)}, bf16[4,16,1280]{2,1,0:T(8,128)(2,1)}) custom-call(s32[4]{0:T(128)S(1)} %pad_add_fusion.shift_ref.scal_ref, s32[1]{0:T(128)} %bitcast.1.bit_ref, f32[8,16,4096]{2,1,0:T(8,128)S(1)} %copy-done, s32[128,1]{1,0:T(8,128)S(1)} %reshape.32.place_ref, bf16[32,4096]{1,0:T(8,128)(2,1)S(1)} %delta.1.own_ref, ...), custom_call_target="tpu_custom_call" | custom-call | tf_op jit(solution)/shard_map/join/pallas_call | solution.py:390
  69.7 0.7 copy-done.2
  70.4 3.0 %collective-permute-start.5 = (bf16[4,16,1280]{2,1,0:T(8,128)(2,1)}, bf16[4,16,1280]{2,1,0:T(8,128)(2,1)S(1)}, u32[]{:S(2)}, u32[]{:S(2)}) collective-permute-start(bf16[4,16,1280]{2,1,0:T(8,128)(2,1)} %get-tuple-element.40), channel_id=1, source_target_pairs={{0,4},{1,5},{2,6},{3,7},{4,0},{5,1},{6,2},{7,3},{8,12},{9,13},{10,... | collective-permute-start | bytes 491528 | tf_op jit(solution)/shard_map/ppermute | solution.py:406
  73.4 3.9 %collective-permute-done.2.got_ref = bf16[4,16,2816]{2,1,0:T(8,128)(2,1)} collective-permute-done((bf16[4,16,2816]{2,1,0:T(8,128)(2,1)}, bf16[4,16,2816]{2,1,0:T(8,128)(2,1)}, u32[]{:S(2)}, u32[]{:S(2)}) %collective-permute-start.2) | collective-permute-done | bytes 360480 | tf_op jit(solution)/shard_map/ppermute | solution.py:406
  77.3 1.1 %halve.4 = (f32[2,16,2816]{2,1,0:T(8,128)S(1)}, bf16[2,16,2816]{2,1,0:T(8,128)(2,1)S(1)}) custom-call(s32[1]{0:T(128)} %bitcast.1.bit_ref, f32[4,16,2816]{2,1,0:T(8,128)S(1)} %get-tuple-element.33.keep_ref, bf16[4,16,2816]{2,1,0:T(8,128)(2,1)} %collective-permute-done.2.got_ref), custom_call_target="tpu_custom_call" | custom-call | tf_op jit(solution)/shard_map/halve/pallas_call | solution.py:399
  78.4 3.2 %collective-permute-start.3 = (bf16[2,16,2816]{2,1,0:T(8,128)(2,1)S(1)}, bf16[2,16,2816]{2,1,0:T(8,128)(2,1)S(1)}, u32[]{:S(2)}, u32[]{:S(2)}) collective-permute-start(bf16[2,16,2816]{2,1,0:T(8,128)(2,1)S(1)} %get-tuple-element.36), channel_id=1, source_target_pairs={{0,4},{1,5},{2,6},{3,7},{4,0},{5,1},{6,2},{7,3},{8,12},{9,13},{10,... | collective-permute-start | bytes 540680 | tf_op jit(solution)/shard_map/ppermute | solution.py:406
  81.6 1.0 %copy-done.3 = f32[4,16,1280]{2,1,0:T(8,128)S(1)} copy-done((f32[4,16,1280]{2,1,0:T(8,128)S(1)}, f32[4,16,1280]{2,1,0:T(8,128)}, u32[]{:S(2)}) %copy-start.3) | copy-done | bytes 327704
  82.6 1.3 %collective-permute-start.6 = (bf16[2,16,1280]{2,1,0:T(8,128)(2,1)S(1)}, bf16[2,16,1280]{2,1,0:T(8,128)(2,1)S(1)}, u32[]{:S(2)}, u32[]{:S(2)}) collective-permute-start(bf16[2,16,1280]{2,1,0:T(8,128)(2,1)S(1)} %get-tuple-element.42), channel_id=1, source_target_pairs={{0,8},{1,9},{2,10},{3,11},{4,12},{5,13},{6,14},{7,15},{8,0},{9,1},... | collective-permute-start | bytes 245768 | tf_op jit(solution)/shard_map/ppermute | solution.py:406
  83.9 2.8 %collective-permute-done.3.got_ref = bf16[2,16,2816]{2,1,0:T(8,128)(2,1)S(1)} collective-permute-done((bf16[2,16,2816]{2,1,0:T(8,128)(2,1)S(1)}, bf16[2,16,2816]{2,1,0:T(8,128)(2,1)S(1)}, u32[]{:S(2)}, u32[]{:S(2)}) %collective-permute-start.3) | collective-permute-done | bytes 180256 | tf_op jit(solution)/shard_map/ppermute | solution.py:406
  86.8 2.8 %collective-permute-start.4 = (bf16[1,16,2816]{2,1,0:T(8,128)(2,1)S(1)}, bf16[1,16,2816]{2,1,0:T(8,128)(2,1)S(1)}, u32[]{:S(2)}, u32[]{:S(2)}) collective-permute-start(bf16[1,16,2816]{2,1,0:T(8,128)(2,1)S(1)} %get-tuple-element.38), channel_id=1, source_target_pairs={{0,8},{1,9},{2,10},{3,11},{4,12},{5,13},{6,14},{7,15},{8,0},{9,1},... | collective-permute-start | bytes 270344 | tf_op jit(solution)/shard_map/ppermute | solution.py:406
  89.6 1.1 %collective-permute-start.7 = (bf16[1,16,1280]{2,1,0:T(8,128)(2,1)S(1)}, bf16[1,16,1280]{2,1,0:T(8,128)(2,1)S(1)}, u32[]{:S(2)}, u32[]{:S(2)}) collective-permute-start(bf16[1,16,1280]{2,1,0:T(8,128)(2,1)S(1)} %get-tuple-element.44), channel_id=1, source_target_pairs={{0,2},{1,3},{2,0},{3,1},{4,6},{5,7},{6,4},{7,5},{8,10},{9,11},{10,... | collective-permute-start | bytes 122888 | tf_op jit(solution)/shard_map/ppermute | solution.py:406
  90.7 2.9 %collective-permute-done.7.refs_3_ = bf16[1,16,1280]{2,1,0:T(8,128)(2,1)S(1)} collective-permute-done((bf16[1,16,1280]{2,1,0:T(8,128)(2,1)S(1)}, bf16[1,16,1280]{2,1,0:T(8,128)(2,1)S(1)}, u32[]{:S(2)}, u32[]{:S(2)}) %collective-permute-start.7) | collective-permute-done | bytes 40992 | tf_op jit(solution)/shard_map/ppermute | solution.py:406
  93.6 0.7 finish.1
  (17 shorter events, 0.3 us)
Async XLA Ops:
  1.9 21.9 %all-to-all-start = ((bf16[16,16,1024]{2,1,0:T(8,128)(2,1)}), bf16[16,16,1024]{2,1,0:T(8,128)(2,1)S(1)}, u32[]{:S(2)}, u32[]{:S(2)}) async-start(bf16[16,16,1024]{2,1,0:T(8,128)(2,1)} %split_rows.1), calls=%async_computation | async-start | bytes 1048576 | tf_op jit(solution)/shard_map/all_to_all | solution.py:301
  25.9 27.1 %copy-start.4 = (s32[4,186]{1,0:T(4,128)S(1)}, s32[4,186]{1,0:T(4,128)}, u32[]{:S(2)}) copy-start(s32[4,186]{1,0:T(4,128)} %ids_ref.1) | copy-start | bytes 8932
  26.0 27.1 %all-to-all-start.1 = ((bf16[16,32,1024]{2,1,0:T(8,128)(2,1)}), bf16[16,32,1024]{2,1,0:T(8,128)(2,1)S(1)}, u32[]{:S(2)}, u32[]{:S(2)}) async-start(bf16[16,32,1024]{2,1,0:T(8,128)(2,1)} %get-tuple-element.29), calls=%async_computation.1 | async-start | bytes 2097152 | tf_op jit(solution)/shard_map/all_to_all | solution.py:318
  35.5 1.3 %copy-start.1 = (f32[8,16,4096]{2,1,0:T(8,128)}, f32[8,16,4096]{2,1,0:T(8,128)S(1)}, u32[]{:S(2)}) copy-start(f32[8,16,4096]{2,1,0:T(8,128)S(1)} %get-tuple-element.27.keep_ref) | copy-start | bytes 6291460
  36.8 2.7 %collective-permute-start = (bf16[8,16,4096]{2,1,0:T(8,128)(2,1)S(1)}, bf16[8,16,4096]{2,1,0:T(8,128)(2,1)S(1)}, u32[]{:S(2)}, u32[]{:S(2)}) collective-permute-start(bf16[8,16,4096]{2,1,0:T(8,128)(2,1)S(1)} %get-tuple-element.28), channel_id=1, source_target_pairs={{0,1},{1,0},{2,3},{3,2},{4,5},{5,4},{6,7},{7,6},{8,9},{9,8},{10,11... | collective-permute-start | bytes 3145736 | tf_op jit(solution)/shard_map/ppermute | solution.py:347
  39.5 1.0 %copy-start.5 = (bf16[8,16,4096]{2,1,0:T(8,128)(2,1)}, bf16[8,16,4096]{2,1,0:T(8,128)(2,1)S(1)}, u32[]{:S(2)}) copy-start(bf16[8,16,4096]{2,1,0:T(8,128)(2,1)S(1)} %collective-permute-done.got_ref) | copy-start | bytes 3145732
  43.9 20.3 %copy-start = (f32[8,16,4096]{2,1,0:T(8,128)S(1)}, f32[8,16,4096]{2,1,0:T(8,128)}, u32[]{:S(2)}) copy-start(f32[8,16,4096]{2,1,0:T(8,128)} %pair.1.base_ref) | copy-start | bytes 6291460
  62.3 1.8 %collective-permute-start.1 = (bf16[32,4096]{1,0:T(8,128)(2,1)S(1)}, bf16[32,4096]{1,0:T(8,128)(2,1)S(1)}, u32[]{:S(2)}, u32[]{:S(2)}) collective-permute-start(bf16[32,4096]{1,0:T(8,128)(2,1)S(1)} %delta.1.own_ref), channel_id=1, source_target_pairs={{0,1},{1,0},{2,3},{3,2},{4,5},{5,4},{6,7},{7,6},{8,9},{9,8},{10,11... | collective-permute-start | bytes 786440 | tf_op jit(solution)/shard_map/ppermute | solution.py:374
  66.1 11.2 %collective-permute-start.2 = (bf16[4,16,2816]{2,1,0:T(8,128)(2,1)}, bf16[4,16,2816]{2,1,0:T(8,128)(2,1)}, u32[]{:S(2)}, u32[]{:S(2)}) collective-permute-start(bf16[4,16,2816]{2,1,0:T(8,128)(2,1)} %get-tuple-element.34), channel_id=1, source_target_pairs={{0,2},{1,3},{2,0},{3,1},{4,6},{5,7},{6,4},{7,5},{8,10},{9,11},{10,... | collective-permute-start | bytes 1081352 | tf_op jit(solution)/shard_map/ppermute | solution.py:406
  69.7 0.7 copy-start.2
  70.4 11.2 %collective-permute-start.5 = (bf16[4,16,1280]{2,1,0:T(8,128)(2,1)}, bf16[4,16,1280]{2,1,0:T(8,128)(2,1)S(1)}, u32[]{:S(2)}, u32[]{:S(2)}) collective-permute-start(bf16[4,16,1280]{2,1,0:T(8,128)(2,1)} %get-tuple-element.40), channel_id=1, source_target_pairs={{0,4},{1,5},{2,6},{3,7},{4,0},{5,1},{6,2},{7,3},{8,12},{9,13},{10,... | collective-permute-start | bytes 491528 | tf_op jit(solution)/shard_map/ppermute | solution.py:406
  78.4 8.4 %collective-permute-start.3 = (bf16[2,16,2816]{2,1,0:T(8,128)(2,1)S(1)}, bf16[2,16,2816]{2,1,0:T(8,128)(2,1)S(1)}, u32[]{:S(2)}, u32[]{:S(2)}) collective-permute-start(bf16[2,16,2816]{2,1,0:T(8,128)(2,1)S(1)} %get-tuple-element.36), channel_id=1, source_target_pairs={{0,4},{1,5},{2,6},{3,7},{4,0},{5,1},{6,2},{7,3},{8,12},{9,13},{10,... | collective-permute-start | bytes 540680 | tf_op jit(solution)/shard_map/ppermute | solution.py:406
  81.6 1.0 %copy-start.3 = (f32[4,16,1280]{2,1,0:T(8,128)S(1)}, f32[4,16,1280]{2,1,0:T(8,128)}, u32[]{:S(2)}) copy-start(f32[4,16,1280]{2,1,0:T(8,128)} %copy-done.2) | copy-start | bytes 983044
  82.6 6.9 %collective-permute-start.6 = (bf16[2,16,1280]{2,1,0:T(8,128)(2,1)S(1)}, bf16[2,16,1280]{2,1,0:T(8,128)(2,1)S(1)}, u32[]{:S(2)}, u32[]{:S(2)}) collective-permute-start(bf16[2,16,1280]{2,1,0:T(8,128)(2,1)S(1)} %get-tuple-element.42), channel_id=1, source_target_pairs={{0,8},{1,9},{2,10},{3,11},{4,12},{5,13},{6,14},{7,15},{8,0},{9,1},... | collective-permute-start | bytes 245768 | tf_op jit(solution)/shard_map/ppermute | solution.py:406
  86.8 6.9 %collective-permute-start.4 = (bf16[1,16,2816]{2,1,0:T(8,128)(2,1)S(1)}, bf16[1,16,2816]{2,1,0:T(8,128)(2,1)S(1)}, u32[]{:S(2)}, u32[]{:S(2)}) collective-permute-start(bf16[1,16,2816]{2,1,0:T(8,128)(2,1)S(1)} %get-tuple-element.38), channel_id=1, source_target_pairs={{0,8},{1,9},{2,10},{3,11},{4,12},{5,13},{6,14},{7,15},{8,0},{9,1},... | collective-permute-start | bytes 270344 | tf_op jit(solution)/shard_map/ppermute | solution.py:406
  89.6 4.1 %collective-permute-start.7 = (bf16[1,16,1280]{2,1,0:T(8,128)(2,1)S(1)}, bf16[1,16,1280]{2,1,0:T(8,128)(2,1)S(1)}, u32[]{:S(2)}, u32[]{:S(2)}) collective-permute-start(bf16[1,16,1280]{2,1,0:T(8,128)(2,1)S(1)} %get-tuple-element.44), channel_id=1, source_target_pairs={{0,2},{1,3},{2,0},{3,1},{4,6},{5,7},{6,4},{7,5},{8,10},{9,11},{10,... | collective-permute-start | bytes 122888 | tf_op jit(solution)/shard_map/ppermute | solution.py:406

commit v11 on v10

--- a/solution.py
+++ b/solution.py
@@ -373,11 +373,11 @@
     )(block_ids, arrived, delta_values)
     others = lax.ppermute(deltas, "cols", pairs(1))
 
-    tile = width_d // 16
+    tile = width_d // 32
     above = [1 << k for k in range(1, peers.bit_length() - 1)]
     ends = []
     for side, order in enumerate((above, above[1:] + above[:1])):
-        first, tiles = ((0, 11), (11, 16 - 11))[side]
+        first, tiles = ((0, 21), (21, 32 - 21))[side]
         cols = tiles * tile
         open_bits = list(above)
         for count, step in enumerate(order):

time: 94.8 us -> 94.8 us (level)
  starting transfers between devices: 26 us -> 27.5 us
  waiting for transfers between devices: 36.3 us -> 34.8 us
    ppermute x6, starting transfers between devices: 13.4 us -> 14.9 us  [body(): got = lax.ppermute(send, 'cols', pairs(step))]
    ppermute x6, waiting for transfers between devices: 9.64 us -> 8.18 us  [body(): got = lax.ppermute(send, 'cols', pairs(step))]
where the time goes in v11:
time: 94.8 us; the launch traced here: 94.4 us
  waiting for transfers between devices  34.8 us (37%)
  Pallas kernels  27.6 us (29%)
  starting transfers between devices  27.5 us (29%)
  local copies, waits for them, and re-layouts  4.23 us (4%)
    ppermute x6, starting transfers between devices, body(): got = lax.ppermute(send, 'cols', pairs(step))  14.9 us
    all_to_all x1, waiting for transfers between devices, body(): x = lax.all_to_all(outgoing, 'cols', 0, 0)  14.4 us
    pallas_call x1, Pallas kernels, body(): pl.pallas_call(functools.partial(delta_kernel, plan, d_blocks, group), in...  9.27 us
    all_to_all x1, waiting for transfers between devices, body(): arrived = lax.all_to_all(slots, 'cols', 0, 0)  9.13 us
    ppermute x6, waiting for transfers between devices, body(): got = lax.ppermute(send, 'cols', pairs(step))  8.18 us
    all_to_all x1, starting transfers between devices, body(): x = lax.all_to_all(outgoing, 'cols', 0, 0)  7.4 us
    pallas_call x1, Pallas kernels, body(): pl.pallas_call(functools.partial(base_kernel, plan), in_specs=[smem, vmem...  5.42 us
    all_to_all x1, starting transfers between devices, body(): arrived = lax.all_to_all(slots, 'cols', 0, 0)  4.11 us
  transfers between devices with their start and end apart: 10, of which 7 were waited for; matrix products, arithmetic and copies ran while one was open for 0% of the time, Pallas kernels for 12%

profile of v11, /device:TPU:0, one launch (start us, length us, event | category | flops | bytes accessed | tf_op | source)
XLA Modules:
  0.0 94.4 jit_solution(5144173826184469807)
XLA Ops:
  0.0 1.9 %split_rows.1 = bf16[16,16,1024]{2,1,0:T(8,128)(2,1)} custom-call(bf16[16,14848]{1,0:T(8,128)(2,1)} %h_hbm.1, s32[1,16]{1,0:T(1,128)} %bitcast.9, s32[1,64]{1,0:T(1,128)} %bitcast.10), custom_call_target="tpu_custom_call" | custom-call | tf_op jit(solution)/shard_map/split_rows/pallas_call | solution.py:285
  1.9 7.4 %all-to-all-start = ((bf16[16,16,1024]{2,1,0:T(8,128)(2,1)}), bf16[16,16,1024]{2,1,0:T(8,128)(2,1)S(1)}, u32[]{:S(2)}, u32[]{:S(2)}) async-start(bf16[16,16,1024]{2,1,0:T(8,128)(2,1)} %split_rows.1), calls=%async_computation | async-start | bytes 1048576 | tf_op jit(solution)/shard_map/all_to_all | solution.py:301
  9.4 14.4 %all-to-all-done.x_ref = bf16[16,16,1024]{2,1,0:T(8,128)(2,1)S(1)} async-done(((bf16[16,16,1024]{2,1,0:T(8,128)(2,1)}), bf16[16,16,1024]{2,1,0:T(8,128)(2,1)S(1)}, u32[]{:S(2)}, u32[]{:S(2)}) %all-to-all-start) | async-done | bytes 524320 | tf_op jit(solution)/shard_map/all_to_all | solution.py:301
  23.7 2.2 %route.1 = (bf16[16,32,1024]{2,1,0:T(8,128)(2,1)}, s32[256,1]{1,0:T(8,128)S(1)}) custom-call(s32[4]{0:T(128)S(1)} %pad_add_fusion.shift_ref.scal_ref, bf16[16,16,1024]{2,1,0:T(8,128)(2,1)S(1)} %all-to-all-done.x_ref), custom_call_target="tpu_custom_call" | custom-call | tf_op jit(solution)/shard_map/route/pallas_call | solution.py:303
  26.0 4.1 %all-to-all-start.1 = ((bf16[16,32,1024]{2,1,0:T(8,128)(2,1)}), bf16[16,32,1024]{2,1,0:T(8,128)(2,1)S(1)}, u32[]{:S(2)}, u32[]{:S(2)}) async-start(bf16[16,32,1024]{2,1,0:T(8,128)(2,1)} %get-tuple-element.29), calls=%async_computation.1 | async-start | bytes 2097152 | tf_op jit(solution)/shard_map/all_to_all | solution.py:318
  30.1 5.4 %base.1 = (f32[8,16,4096]{2,1,0:T(8,128)S(1)}, bf16[8,16,4096]{2,1,0:T(8,128)(2,1)S(1)}) custom-call(s32[4]{0:T(128)S(1)} %pad_add_fusion.shift_ref.scal_ref, bf16[16,16,1024]{2,1,0:T(8,128)(2,1)S(1)} %all-to-all-done.x_ref, bf16[928,4096]{1,0:T(8,128)(2,1)} %w_hbm.1), custom_call_target="tpu_custom_call" | custom-call | flops 1946157056 | bytes 7602176 | tf_op jit(solution)/shard_map/base/pallas_call | solution.py:323
  35.5 1.3 %copy-done.1 = f32[8,16,4096]{2,1,0:T(8,128)} copy-done((f32[8,16,4096]{2,1,0:T(8,128)}, f32[8,16,4096]{2,1,0:T(8,128)S(1)}, u32[]{:S(2)}) %copy-start.1) | copy-done | bytes 2097176
  36.8 0.4 collective-permute-start
  37.2 2.3 %collective-permute-done.got_ref = bf16[8,16,4096]{2,1,0:T(8,128)(2,1)S(1)} collective-permute-done((bf16[8,16,4096]{2,1,0:T(8,128)(2,1)S(1)}, bf16[8,16,4096]{2,1,0:T(8,128)(2,1)S(1)}, u32[]{:S(2)}, u32[]{:S(2)}) %collective-permute-start) | collective-permute-done | bytes 1048608 | tf_op jit(solution)/shard_map/ppermute | solution.py:347
  39.5 1.0 %copy-done.5 = bf16[8,16,4096]{2,1,0:T(8,128)(2,1)} copy-done((bf16[8,16,4096]{2,1,0:T(8,128)(2,1)}, bf16[8,16,4096]{2,1,0:T(8,128)(2,1)S(1)}, u32[]{:S(2)}) %copy-start.5) | copy-done | bytes 1048600
  40.5 3.4 %pair.1.base_ref = f32[8,16,4096]{2,1,0:T(8,128)} custom-call(f32[8,16,4096]{2,1,0:T(8,128)} %copy-done.1, bf16[8,16,4096]{2,1,0:T(8,128)(2,1)} %copy-done.5), custom_call_target="tpu_custom_call" | custom-call | tf_op jit(solution)/shard_map/pair/pallas_call | solution.py:342
  43.9 9.1 %all-to-all-done.1.x_ref = bf16[16,32,1024]{2,1,0:T(8,128)(2,1)S(1)} async-done(((bf16[16,32,1024]{2,1,0:T(8,128)(2,1)}), bf16[16,32,1024]{2,1,0:T(8,128)(2,1)S(1)}, u32[]{:S(2)}, u32[]{:S(2)}) %all-to-all-start.1) | async-done | bytes 1048608 | tf_op jit(solution)/shard_map/all_to_all | solution.py:318
  53.0 9.3 %delta.1.own_ref = bf16[32,4096]{1,0:T(8,128)(2,1)S(1)} custom-call(s32[4,186]{1,0:T(4,128)S(1)} %copy-done.4, bf16[16,32,1024]{2,1,0:T(8,128)(2,1)S(1)} %all-to-all-done.1.x_ref, bf16[4,186,128,128]{3,2,1,0:T(8,128)(2,1)} %v_hbm.1), custom_call_target="tpu_custom_call" | custom-call | flops 195035136 | bytes 24379392 | tf_op jit(solution)/shard_map/delta/pallas_call | solution.py:355
  62.3 0.7 collective-permute-start.1
  63.0 0.1 reduce
  63.1 0.1 reshape.30
  63.3 0.8 collective-permute-done.1.got_ref
  64.1 1.9 %join.2 = (f32[4,16,2688]{2,1,0:T(8,128)S(1)}, bf16[4,16,2688]{2,1,0:T(8,128)(2,1)}) custom-call(s32[4]{0:T(128)S(1)} %pad_add_fusion.shift_ref.scal_ref, s32[1]{0:T(128)} %bitcast.6.bit_ref, f32[8,16,4096]{2,1,0:T(8,128)S(1)} %copy-done, s32[128,1]{1,0:T(8,128)S(1)} %reshape.32.place_ref, bf16[32,4096]{1,0:T(8,128)(2,1)S(1)} %delta.1.own_ref, ...), custom_call_target="tpu_custom_call" | custom-call | tf_op jit(solution)/shard_map/join/pallas_call | solution.py:390
  66.1 2.0 %collective-permute-start.2 = (bf16[4,16,2688]{2,1,0:T(8,128)(2,1)}, bf16[4,16,2688]{2,1,0:T(8,128)(2,1)}, u32[]{:S(2)}, u32[]{:S(2)}) collective-permute-start(bf16[4,16,2688]{2,1,0:T(8,128)(2,1)} %get-tuple-element.34), channel_id=1, source_target_pairs={{0,2},{1,3},{2,0},{3,1},{4,6},{5,7},{6,4},{7,5},{8,10},{9,11},{10,... | collective-permute-start | bytes 1032200 | tf_op jit(solution)/shard_map/ppermute | solution.py:406
  68.1 1.7 %join.3 = (f32[4,16,1408]{2,1,0:T(8,128)S(1)}, bf16[4,16,1408]{2,1,0:T(8,128)(2,1)}) custom-call(s32[4]{0:T(128)S(1)} %pad_add_fusion.shift_ref.scal_ref, s32[1]{0:T(128)} %bitcast.1.bit_ref, f32[8,16,4096]{2,1,0:T(8,128)S(1)} %copy-done, s32[128,1]{1,0:T(8,128)S(1)} %reshape.32.place_ref, bf16[32,4096]{1,0:T(8,128)(2,1)S(1)} %delta.1.own_ref, ...), custom_call_target="tpu_custom_call" | custom-call | tf_op jit(solution)/shard_map/join/pallas_call | solution.py:390
  69.7 0.7 copy-done.2
  70.5 3.0 %collective-permute-start.5 = (bf16[4,16,1408]{2,1,0:T(8,128)(2,1)}, bf16[4,16,1408]{2,1,0:T(8,128)(2,1)S(1)}, u32[]{:S(2)}, u32[]{:S(2)}) collective-permute-start(bf16[4,16,1408]{2,1,0:T(8,128)(2,1)} %get-tuple-element.40), channel_id=1, source_target_pairs={{0,4},{1,5},{2,6},{3,7},{4,0},{5,1},{6,2},{7,3},{8,12},{9,13},{10,... | collective-permute-start | bytes 540680 | tf_op jit(solution)/shard_map/ppermute | solution.py:406
  73.4 3.5 %collective-permute-done.2.got_ref = bf16[4,16,2688]{2,1,0:T(8,128)(2,1)} collective-permute-done((bf16[4,16,2688]{2,1,0:T(8,128)(2,1)}, bf16[4,16,2688]{2,1,0:T(8,128)(2,1)}, u32[]{:S(2)}, u32[]{:S(2)}) %collective-permute-start.2) | collective-permute-done | bytes 344096 | tf_op jit(solution)/shard_map/ppermute | solution.py:406
  77.0 1.0 %halve.4 = (f32[2,16,2688]{2,1,0:T(8,128)S(1)}, bf16[2,16,2688]{2,1,0:T(8,128)(2,1)S(1)}) custom-call(s32[1]{0:T(128)} %bitcast.1.bit_ref, f32[4,16,2688]{2,1,0:T(8,128)S(1)} %get-tuple-element.33.keep_ref, bf16[4,16,2688]{2,1,0:T(8,128)(2,1)} %collective-permute-done.2.got_ref), custom_call_target="tpu_custom_call" | custom-call | tf_op jit(solution)/shard_map/halve/pallas_call | solution.py:399
  78.0 3.2 %collective-permute-start.3 = (bf16[2,16,2688]{2,1,0:T(8,128)(2,1)S(1)}, bf16[2,16,2688]{2,1,0:T(8,128)(2,1)S(1)}, u32[]{:S(2)}, u32[]{:S(2)}) collective-permute-start(bf16[2,16,2688]{2,1,0:T(8,128)(2,1)S(1)} %get-tuple-element.36), channel_id=1, source_target_pairs={{0,4},{1,5},{2,6},{3,7},{4,0},{5,1},{6,2},{7,3},{8,12},{9,13},{10,... | collective-permute-start | bytes 516104 | tf_op jit(solution)/shard_map/ppermute | solution.py:406
  81.2 1.0 %copy-done.3 = f32[4,16,1408]{2,1,0:T(8,128)S(1)} copy-done((f32[4,16,1408]{2,1,0:T(8,128)S(1)}, f32[4,16,1408]{2,1,0:T(8,128)}, u32[]{:S(2)}) %copy-start.3) | copy-done | bytes 360472
  82.2 1.3 %collective-permute-start.6 = (bf16[2,16,1408]{2,1,0:T(8,128)(2,1)S(1)}, bf16[2,16,1408]{2,1,0:T(8,128)(2,1)S(1)}, u32[]{:S(2)}, u32[]{:S(2)}) collective-permute-start(bf16[2,16,1408]{2,1,0:T(8,128)(2,1)S(1)} %get-tuple-element.42), channel_id=1, source_target_pairs={{0,8},{1,9},{2,10},{3,11},{4,12},{5,13},{6,14},{7,15},{8,0},{9,1},... | collective-permute-start | bytes 270344 | tf_op jit(solution)/shard_map/ppermute | solution.py:406
  83.6 2.6 %collective-permute-done.3.got_ref = bf16[2,16,2688]{2,1,0:T(8,128)(2,1)S(1)} collective-permute-done((bf16[2,16,2688]{2,1,0:T(8,128)(2,1)S(1)}, bf16[2,16,2688]{2,1,0:T(8,128)(2,1)S(1)}, u32[]{:S(2)}, u32[]{:S(2)}) %collective-permute-start.3) | collective-permute-done | bytes 172064 | tf_op jit(solution)/shard_map/ppermute | solution.py:406
  86.2 2.9 %collective-permute-start.4 = (bf16[1,16,2688]{2,1,0:T(8,128)(2,1)S(1)}, bf16[1,16,2688]{2,1,0:T(8,128)(2,1)S(1)}, u32[]{:S(2)}, u32[]{:S(2)}) collective-permute-start(bf16[1,16,2688]{2,1,0:T(8,128)(2,1)S(1)} %get-tuple-element.38), channel_id=1, source_target_pairs={{0,8},{1,9},{2,10},{3,11},{4,12},{5,13},{6,14},{7,15},{8,0},{9,1},... | collective-permute-start | bytes 258056 | tf_op jit(solution)/shard_map/ppermute | solution.py:406
  89.1 2.6 %collective-permute-start.7 = (bf16[1,16,1408]{2,1,0:T(8,128)(2,1)S(1)}, bf16[1,16,1408]{2,1,0:T(8,128)(2,1)S(1)}, u32[]{:S(2)}, u32[]{:S(2)}) collective-permute-start(bf16[1,16,1408]{2,1,0:T(8,128)(2,1)S(1)} %get-tuple-element.44), channel_id=1, source_target_pairs={{0,2},{1,3},{2,0},{3,1},{4,6},{5,7},{6,4},{7,5},{8,10},{9,11},{10,... | collective-permute-start | bytes 135176 | tf_op jit(solution)/shard_map/ppermute | solution.py:406
  91.7 2.0 %collective-permute-done.7.refs_3_ = bf16[1,16,1408]{2,1,0:T(8,128)(2,1)S(1)} collective-permute-done((bf16[1,16,1408]{2,1,0:T(8,128)(2,1)S(1)}, bf16[1,16,1408]{2,1,0:T(8,128)(2,1)S(1)}, u32[]{:S(2)}, u32[]{:S(2)}) %collective-permute-start.7) | collective-permute-done | bytes 45088 | tf_op jit(solution)/shard_map/ppermute | solution.py:406
  93.7 0.7 finish.1
  (17 shorter events, 0.3 us)
Async XLA Ops:
  1.9 21.9 %all-to-all-start = ((bf16[16,16,1024]{2,1,0:T(8,128)(2,1)}), bf16[16,16,1024]{2,1,0:T(8,128)(2,1)S(1)}, u32[]{:S(2)}, u32[]{:S(2)}) async-start(bf16[16,16,1024]{2,1,0:T(8,128)(2,1)} %split_rows.1), calls=%async_computation | async-start | bytes 1048576 | tf_op jit(solution)/shard_map/all_to_all | solution.py:301
  25.9 27.1 %copy-start.4 = (s32[4,186]{1,0:T(4,128)S(1)}, s32[4,186]{1,0:T(4,128)}, u32[]{:S(2)}) copy-start(s32[4,186]{1,0:T(4,128)} %ids_ref.1) | copy-start | bytes 8932
  26.0 27.1 %all-to-all-start.1 = ((bf16[16,32,1024]{2,1,0:T(8,128)(2,1)}), bf16[16,32,1024]{2,1,0:T(8,128)(2,1)S(1)}, u32[]{:S(2)}, u32[]{:S(2)}) async-start(bf16[16,32,1024]{2,1,0:T(8,128)(2,1)} %get-tuple-element.29), calls=%async_computation.1 | async-start | bytes 2097152 | tf_op jit(solution)/shard_map/all_to_all | solution.py:318
  35.5 1.3 %copy-start.1 = (f32[8,16,4096]{2,1,0:T(8,128)}, f32[8,16,4096]{2,1,0:T(8,128)S(1)}, u32[]{:S(2)}) copy-start(f32[8,16,4096]{2,1,0:T(8,128)S(1)} %get-tuple-element.27.keep_ref) | copy-start | bytes 6291460
  36.8 2.7 %collective-permute-start = (bf16[8,16,4096]{2,1,0:T(8,128)(2,1)S(1)}, bf16[8,16,4096]{2,1,0:T(8,128)(2,1)S(1)}, u32[]{:S(2)}, u32[]{:S(2)}) collective-permute-start(bf16[8,16,4096]{2,1,0:T(8,128)(2,1)S(1)} %get-tuple-element.28), channel_id=1, source_target_pairs={{0,1},{1,0},{2,3},{3,2},{4,5},{5,4},{6,7},{7,6},{8,9},{9,8},{10,11... | collective-permute-start | bytes 3145736 | tf_op jit(solution)/shard_map/ppermute | solution.py:347
  39.5 1.0 %copy-start.5 = (bf16[8,16,4096]{2,1,0:T(8,128)(2,1)}, bf16[8,16,4096]{2,1,0:T(8,128)(2,1)S(1)}, u32[]{:S(2)}) copy-start(bf16[8,16,4096]{2,1,0:T(8,128)(2,1)S(1)} %collective-permute-done.got_ref) | copy-start | bytes 3145732
  43.9 20.3 %copy-start = (f32[8,16,4096]{2,1,0:T(8,128)S(1)}, f32[8,16,4096]{2,1,0:T(8,128)}, u32[]{:S(2)}) copy-start(f32[8,16,4096]{2,1,0:T(8,128)} %pair.1.base_ref) | copy-start | bytes 6291460
  62.3 1.8 %collective-permute-start.1 = (bf16[32,4096]{1,0:T(8,128)(2,1)S(1)}, bf16[32,4096]{1,0:T(8,128)(2,1)S(1)}, u32[]{:S(2)}, u32[]{:S(2)}) collective-permute-start(bf16[32,4096]{1,0:T(8,128)(2,1)S(1)} %delta.1.own_ref), channel_id=1, source_target_pairs={{0,1},{1,0},{2,3},{3,2},{4,5},{5,4},{6,7},{7,6},{8,9},{9,8},{10,11... | collective-permute-start | bytes 786440 | tf_op jit(solution)/shard_map/ppermute | solution.py:374
  66.1 10.9 %collective-permute-start.2 = (bf16[4,16,2688]{2,1,0:T(8,128)(2,1)}, bf16[4,16,2688]{2,1,0:T(8,128)(2,1)}, u32[]{:S(2)}, u32[]{:S(2)}) collective-permute-start(bf16[4,16,2688]{2,1,0:T(8,128)(2,1)} %get-tuple-element.34), channel_id=1, source_target_pairs={{0,2},{1,3},{2,0},{3,1},{4,6},{5,7},{6,4},{7,5},{8,10},{9,11},{10,... | collective-permute-start | bytes 1032200 | tf_op jit(solution)/shard_map/ppermute | solution.py:406
  69.7 0.7 copy-start.2
  70.5 10.8 %collective-permute-start.5 = (bf16[4,16,1408]{2,1,0:T(8,128)(2,1)}, bf16[4,16,1408]{2,1,0:T(8,128)(2,1)S(1)}, u32[]{:S(2)}, u32[]{:S(2)}) collective-permute-start(bf16[4,16,1408]{2,1,0:T(8,128)(2,1)} %get-tuple-element.40), channel_id=1, source_target_pairs={{0,4},{1,5},{2,6},{3,7},{4,0},{5,1},{6,2},{7,3},{8,12},{9,13},{10,... | collective-permute-start | bytes 540680 | tf_op jit(solution)/shard_map/ppermute | solution.py:406
  78.0 8.2 %collective-permute-start.3 = (bf16[2,16,2688]{2,1,0:T(8,128)(2,1)S(1)}, bf16[2,16,2688]{2,1,0:T(8,128)(2,1)S(1)}, u32[]{:S(2)}, u32[]{:S(2)}) collective-permute-start(bf16[2,16,2688]{2,1,0:T(8,128)(2,1)S(1)} %get-tuple-element.36), channel_id=1, source_target_pairs={{0,4},{1,5},{2,6},{3,7},{4,0},{5,1},{6,2},{7,3},{8,12},{9,13},{10,... | collective-permute-start | bytes 516104 | tf_op jit(solution)/shard_map/ppermute | solution.py:406
  81.2 1.0 %copy-start.3 = (f32[4,16,1408]{2,1,0:T(8,128)S(1)}, f32[4,16,1408]{2,1,0:T(8,128)}, u32[]{:S(2)}) copy-start(f32[4,16,1408]{2,1,0:T(8,128)} %copy-done.2) | copy-start | bytes 1081348
  82.2 6.8 %collective-permute-start.6 = (bf16[2,16,1408]{2,1,0:T(8,128)(2,1)S(1)}, bf16[2,16,1408]{2,1,0:T(8,128)(2,1)S(1)}, u32[]{:S(2)}, u32[]{:S(2)}) collective-permute-start(bf16[2,16,1408]{2,1,0:T(8,128)(2,1)S(1)} %get-tuple-element.42), channel_id=1, source_target_pairs={{0,8},{1,9},{2,10},{3,11},{4,12},{5,13},{6,14},{7,15},{8,0},{9,1},... | collective-permute-start | bytes 270344 | tf_op jit(solution)/shard_map/ppermute | solution.py:406
  86.2 7.5 %collective-permute-start.4 = (bf16[1,16,2688]{2,1,0:T(8,128)(2,1)S(1)}, bf16[1,16,2688]{2,1,0:T(8,128)(2,1)S(1)}, u32[]{:S(2)}, u32[]{:S(2)}) collective-permute-start(bf16[1,16,2688]{2,1,0:T(8,128)(2,1)S(1)} %get-tuple-element.38), channel_id=1, source_target_pairs={{0,8},{1,9},{2,10},{3,11},{4,12},{5,13},{6,14},{7,15},{8,0},{9,1},... | collective-permute-start | bytes 258056 | tf_op jit(solution)/shard_map/ppermute | solution.py:406
  89.1 4.6 %collective-permute-start.7 = (bf16[1,16,1408]{2,1,0:T(8,128)(2,1)S(1)}, bf16[1,16,1408]{2,1,0:T(8,128)(2,1)S(1)}, u32[]{:S(2)}, u32[]{:S(2)}) collective-permute-start(bf16[1,16,1408]{2,1,0:T(8,128)(2,1)S(1)} %get-tuple-element.44), channel_id=1, source_target_pairs={{0,2},{1,3},{2,0},{3,1},{4,6},{5,7},{6,4},{7,5},{8,10},{9,11},{10,... | collective-permute-start | bytes 135176 | tf_op jit(solution)/shard_map/ppermute | solution.py:406
